TPU v7x, 256 devices: a whole 4x4x8 slice. The times are simulated.
256 devices in a mesh: chan: 32 (over z_lo, x, core), win: 8 (over y, z_hi).
Axes of the slice: x: 4, y: 4, z: 8 (z_hi: 2, z_lo: 4; z = z_hi * 4 + z_lo), core: 2. Of those that a mesh axis runs over, the one named last changes fastest.
Arguments:
- samples: bfloat16 [1024, 131072], P('chan', 'win'), may hold values from -6 to 6
- fir_taps: float32 [128], replicated, may hold values from -0.75 to 0.75
- tap_counts: int32 [8], P('win'), may hold values from 64 to 128, as said below
- band_start: int32 [1], replicated, may hold values from 1 to 7681
- grid_blocks: int32 [32], replicated, may hold values from 0 to 31, each once
Outputs:
- cross_spectra: bfloat16 [1024, 1024, 1024], P('chan', 'win')
Inputs may be any that keep to these rules, and one draw needn't show every extreme that they name: `tap_counts`: at least one window uses all 128 taps. `grid_blocks`: each channel block is named once.
All inputs are finite; a program needn't handle non-finite values.
Results may differ from a plain program's by a relative error of at most 0.011.
Values may be sent and summed in bfloat16 or wider, within the bound.
No kernel may reach another device: no remote copies, remote signals or barrier semaphores. Data moves between devices by JAX's collectives and lax.ppermute only.
A program may use at most 64 MiB of HBM per device.

v0:
```python
import math

import jax
import jax.numpy as jnp
from jax import lax
from jax.sharding import PartitionSpec as P

LEN = 16384
FACTOR = 128
BAND = 512
KMAX = 128


def shifted(block, axis, distance):
    devices = range(lax.axis_size(axis))
    route = [(i - distance, i) for i in devices if i - distance in devices]
    return lax.ppermute(block, axis, route)


def fir_matrix(kept):
    lagged = (
        jnp.arange(FACTOR, dtype=jnp.int32)[None, :]
        + FACTOR
        - jnp.arange(2 * FACTOR, dtype=jnp.int32)[:, None]
    )
    taps_index = jnp.arange(KMAX, dtype=jnp.int32)
    picked = jnp.where(lagged[..., None] == taps_index, kept[None, None, :], 0.0)
    return jnp.sum(picked, axis=-1).astype(jnp.bfloat16)


def first_table():
    index = jnp.arange(FACTOR, dtype=jnp.int32)
    turns = jnp.mod(index[:, None] * index[None, :], FACTOR).astype(jnp.float32)
    angles = turns * (2.0 * math.pi / FACTOR)
    return jnp.stack([jnp.cos(angles), -jnp.sin(angles)]).astype(jnp.bfloat16)


def second_table(start):
    residue = jnp.arange(FACTOR, dtype=jnp.int32)[:, None]
    quarter = jnp.arange(BAND // FACTOR, dtype=jnp.int32)[None, :]
    freq = start + jnp.mod(residue - start, FACTOR) + FACTOR * quarter
    inner = jnp.arange(FACTOR, dtype=jnp.int32)
    turns = jnp.mod(freq[:, :, None] * inner[None, None, :], LEN).astype(jnp.float32)
    theta = turns * (2.0 * math.pi / LEN)
    cosine = jnp.cos(theta) / FACTOR
    sine = jnp.sin(theta) / FACTOR
    table = jnp.stack([jnp.stack([cosine, -sine]), jnp.stack([sine, cosine])])
    table = jnp.transpose(table, (2, 0, 4, 1, 3))
    return table.reshape(FACTOR, 2 * FACTOR, 2 * (BAND // FACTOR)).astype(jnp.bfloat16)


def whiten(product):
    width = BAND // FACTOR
    real_part = product[..., :width]
    imag_part = product[..., width:]
    scale = 1.0 / jnp.sqrt(real_part * real_part + imag_part * imag_part + 1.0)
    white = (product * jnp.concatenate([scale, scale], axis=-1)).astype(jnp.bfloat16)
    count = product.shape[1]
    white = white.reshape(FACTOR, count, 2, width)
    return jnp.transpose(white, (1, 2, 0, 3)).reshape(count, 2 * BAND)


def cross_block(left, right):
    left_re = left[..., :BAND]
    left_im = left[..., BAND:]
    right_re = right[..., :BAND]
    right_im = right[..., BAND:]
    real_part = jnp.einsum("wap,wbp->abp", left_re, right_re, preferred_element_type=jnp.float32)
    real_part = real_part + jnp.einsum(
        "wap,wbp->abp", left_im, right_im, preferred_element_type=jnp.float32
    )
    imag_part = jnp.einsum("wap,wbp->abp", left_im, right_re, preferred_element_type=jnp.float32)
    imag_part = imag_part - jnp.einsum(
        "wap,wbp->abp", left_re, right_im, preferred_element_type=jnp.float32
    )
    return jnp.concatenate([real_part, imag_part], axis=-1).astype(jnp.bfloat16)


def shards(samples, fir_taps, tap_counts, band_start, grid_blocks):
    count = samples.shape[0]
    segments = samples.reshape(count, LEN // FACTOR, FACTOR)
    arrived = shifted(segments[:, -1, :], "win", 1)
    previous = jnp.concatenate([arrived[:, None, :], segments[:, :-1, :]], axis=1)
    stacked = jnp.concatenate([previous, segments], axis=2)
    taps_index = jnp.arange(KMAX, dtype=jnp.int32)
    kept = fir_taps * (taps_index < tap_counts[0]).astype(jnp.float32)
    matrix = fir_matrix(kept)
    filtered = jnp.einsum(
        "caj,jb->cab", stacked, matrix, preferred_element_type=jnp.float32
    ).astype(jnp.bfloat16)
    section = jnp.einsum(
        "pra,cab->rcpb", first_table(), filtered, preferred_element_type=jnp.float32
    ).astype(jnp.bfloat16)
    section = section.reshape(FACTOR, count, 2 * FACTOR)
    product = lax.dot_general(
        section,
        second_table(band_start[0]),
        (((2,), (1,)), ((0,), (0,))),
        preferred_element_type=jnp.float32,
    )
    spectra = whiten(product)
    blocks_total = lax.axis_size("chan")
    columns = lax.axis_size("win")
    groups = blocks_total // columns
    every = lax.all_gather(spectra, "chan", axis=0, tiled=True)
    ordered = jnp.take(every.reshape(blocks_total, count, 2 * BAND), grid_blocks, axis=0)
    mine = lax.dynamic_index_in_dim(ordered, lax.axis_index("chan"), 0, keepdims=True)
    row_panel = lax.all_gather(mine, "win", axis=0, tiled=True)
    column_panel = lax.all_to_all(
        ordered.reshape(columns, groups * count, 2 * BAND),
        "win",
        split_axis=0,
        concat_axis=0,
        tiled=True,
    )
    return cross_block(row_panel, column_panel)


def solution(mesh):
    placed = (P("chan", "win"), P(), P("win"), P(), P())
    return jax.shard_map(
        shards, mesh=mesh, in_specs=placed, out_specs=P("chan", "win", None), check_vma=False
    )
```

profile of v0, /device:TPU:32, one launch (start us, length us, event | category | flops | bytes accessed | tf_op | source)
XLA Modules:
  0.0 250.1 jit_solution(11774982137246924904)
XLA Ops:
  6.5 1.5 copy.85
  8.1 8.2 %collective-permute-start = (bf16[32,128]{1,0:T(8,128)(2,1)S(1)}, bf16[32,128]{1,0:T(8,128)(2,1)S(1)}, u32[]{:S(2)}, u32[]{:S(2)}) collective-permute-start(bf16[32,128]{1,0:T(8,128)(2,1)S(1)} %bitcast.62), channel_id=1, source_target_pairs={{0,1},{1,2},{2,3},{3,4},{4,5},{5,6},{6,7},{8,9},{9,10},{10,11},{11... | collective-permute-start | bytes 24584 | tf_op jit(solution)/shard_map/ppermute | solution.py:17
  17.7 1.3 negate_convert_fusion
  19.0 0.7 compare_select_fusion.3
  19.6 10.3 %select_reduce_fusion = bf16[256,128]{1,0:T(8,128)(2,1)S(1)} fusion(f32[128]{0:T(128)S(1)} %compare_select_fusion.3, s32[256,128]{1,0:T(8,128)S(1)} %iota_subtract_fusion), kind=kLoop, calls=%fused_computation.1 | loop fusion | flops 12550144 | bytes 197120 | tf_op jit(solution)/shard_map/reduce_sum | solution.py:28
  31.2 2.8 %convolution_convert_fusion = bf16[32,128,2,128]{3,1,2,0:T(8,128)(2,1)} fusion(bf16[32,128,128]{2,1,0:T(8,128)(2,1)S(1)} %bitcast.57, bf16[32,127,128]{2,1,0:T(8,128)(2,1)S(1)} %bitcast.58, bf16[32,1,128]{2,1,0:T(2,128)(2,1)S(1)} %copy.62, bf16[1,128,128]{2,1,0:T(8,128)(2,1)S(1)} %get-tuple-element.14, bf16[1,128,128]{2,1,0:T(8,128)(2,1)S(1)} %get-tuple-element.15, ...), kind=kOutput, calls=%fused_computation.15 | convolution fusion | flops 544866304 | bytes 4325376 | tf_op jit(solution)/shard_map/pra,cab->rcpb/dot_general | solution.py:91
  34.0 3.4 %copy.65 = bf16[128,32,256]{2,1,0:T(8,128)(2,1)S(1)} copy(bf16[128,32,256]{0,2,1:T(8,128)(2,1)} %bitcast.55) | data formatting | bytes 4194304 | tf_op jit(solution)/shard_map/reshape | solution.py:94
  38.5 0.8 copy.70
  39.6 57.9 %all-gather.2.cloned.1.call-done = bf16[1024,1024]{1,0:T(8,128)(2,1)} async-done(((bf16[32,1024]{1,0:T(8,128)(2,1)}), bf16[1024,1024]{1,0:T(8,128)(2,1)}) %all-gather.2.cloned.1.call-update) | async-done | bytes 2097168 | tf_op jit(solution)/shard_map/all_gather | solution.py:105
  97.5 2.3 gather_fusion
  99.8 1.6 bitcast_select_fusion
  101.3 3.9 %copy.71 = bf16[8,128,1024]{1,2,0:T(8,128)(2,1)} copy(bf16[8,128,1024]{2,1,0:T(8,128)(2,1)} %bitcast_select_fusion) | data formatting | bytes 4194304 | tf_op jit(solution)/shard_map/jit(_take)/select_n | solution.py:106
  105.2 7.7 %all-to-all-start = ((bf16[8,128,1024]{1,2,0:T(8,128)(2,1)}), bf16[8,128,1024]{1,2,0:T(8,128)(2,1)}, u32[]{:S(2)}, u32[]{:S(2)}) async-start(bf16[8,128,1024]{1,2,0:T(8,128)(2,1)} %copy.71), calls=%async_computation | async-start | bytes 4194304 | tf_op jit(solution)/shard_map/all_to_all | solution.py:109
  113.5 0.7 dynamic-slice_select_fusion
  114.2 94.0 %all_gather.7 = bf16[8,32,1024]{2,1,0:T(8,128)(2,1)S(1)} all-gather(bf16[1,32,1024]{2,1,0:T(8,128)(2,1)S(1)} %dynamic-slice_select_fusion), channel_id=1, replica_groups=mesh['chan'=32,'win'=8] {'win'}, dimensions={0}, use_global_device_ids=true | all-gather | bytes 589824 | tf_op jit(solution)/shard_map/all_gather | solution.py:108
  208.2 0.8 copy.82
  209.0 0.8 copy.84
  209.8 1.7 fusion.49
  211.5 1.3 fusion.18
  212.8 1.3 fusion.20
  214.2 4.8 %fusion.1 = bf16[32,128,512]{1,0,2:T(8,128)(2,1)} fusion(f32[512,128,32]{1,2,0:T(8,128)S(1)} %fusion.18, bf16[8,32,512]{1,0,2:T(8,128)(2,1)S(1)} %copy.82, bf16[8,128,512]{1,2,0:T(8,128)(2,1)S(1)} %get-tuple-element.5), kind=kOutput, calls=%fused_computation.7 | convolution fusion | flops 37748736 | bytes 13893632 | tf_op jit(solution)/shard_map/wap,wbp->abp/dot_general | solution.py:73
  218.9 4.8 %fusion = bf16[32,128,512]{1,0,2:T(8,128)(2,1)} fusion(f32[512,128,32]{1,2,0:T(8,128)S(1)} %fusion.20, bf16[8,32,512]{1,0,2:T(8,128)(2,1)S(1)} %copy.84, bf16[8,128,512]{1,2,0:T(8,128)(2,1)S(1)} %get-tuple-element.5), kind=kOutput, calls=%fused_computation.6 | convolution fusion | flops 37748736 | bytes 13893632 | tf_op jit(solution)/shard_map/wap,wbp->abp/dot_general | solution.py:69
  223.7 7.4 %pad_maximum_fusion = bf16[32,128,1024]{1,0,2:T(8,128)(2,1)} fusion(bf16[32,128,512]{1,0,2:T(8,128)(2,1)} %fusion.1, bf16[32,128,512]{1,0,2:T(8,128)(2,1)} %fusion), kind=kLoop, calls=%fused_computation.3 | loop fusion | flops 4194304 | bytes 16777216 | tf_op jit(solution)/shard_map/concatenate | solution.py:76
  231.1 12.1 %copy.76 = bf16[32,128,1024]{2,1,0:T(8,128)(2,1)} copy(bf16[32,128,1024]{1,0,2:T(8,128)(2,1)} %pad_maximum_fusion) | data formatting | bytes 16777216 | tf_op jit(solution)/shard_map/concatenate | solution.py:76
  (32 shorter events, 3.4 us)
Async XLA Ops:
  6.5 90.9 %all-gather.2.cloned.1.call-start = ((), (), s32[]{:S(2)}) async-start(), calls=%async_computation.1 | async-start | bytes 2162688 | tf_op jit(solution)/shard_map/all_gather | solution.py:105
  8.1 23.1 %collective-permute-start = (bf16[32,128]{1,0:T(8,128)(2,1)S(1)}, bf16[32,128]{1,0:T(8,128)(2,1)S(1)}, u32[]{:S(2)}, u32[]{:S(2)}) collective-permute-start(bf16[32,128]{1,0:T(8,128)(2,1)S(1)} %bitcast.62), channel_id=1, source_target_pairs={{0,1},{1,2},{2,3},{3,4},{4,5},{5,6},{6,7},{8,9},{9,10},{10,11},{11... | collective-permute-start | bytes 24584 | tf_op jit(solution)/shard_map/ppermute | solution.py:17
  34.0 5.3 %copy-start = (s32[32]{0:T(128)S(1)}, s32[32]{0:T(128)}, u32[]{:S(2)}) copy-start(s32[32]{0:T(128)} %param.9) | copy-start | bytes 388
  105.2 104.6 %all-to-all-start = ((bf16[8,128,1024]{1,2,0:T(8,128)(2,1)}), bf16[8,128,1024]{1,2,0:T(8,128)(2,1)}, u32[]{:S(2)}, u32[]{:S(2)}) async-start(bf16[8,128,1024]{1,2,0:T(8,128)(2,1)} %copy.71), calls=%async_computation | async-start | bytes 4194304 | tf_op jit(solution)/shard_map/all_to_all | solution.py:109
Sparse Core Ops, SparseCore 0:
  39.4 58.0 all-gather.1
where the time goes:
time: 251 us; the launch traced here: 250 us
  blocking collectives  94 us (37%)
  waiting for transfers between devices  57.9 us (23%)
  local copies, waits for them, and re-layouts  29.3 us (12%)
  other arithmetic  22.4 us (9%)
  starting transfers between devices  15.9 us (6%)
  matrix products  15.6 us (6%)
  between operations  14.9 us (6%)
    all_gather x1, blocking collectives, shards(): row_panel = lax.all_gather(mine, 'win', axis=0, tiled=True)  94 us
    all_gather x1, waiting for transfers between devices, shards(): every = lax.all_gather(spectra, 'chan', axis=0, tiled=True)  57.9 us
    concatenate x1, local copies, waits for them, and re-layouts, cross_block(): return jnp.concatenate([real_part, imag_part], axis=-1).astype(jnp.bfloat16)  12.1 us
    reduce_sum x1, other arithmetic, fir_matrix(): return jnp.sum(picked, axis=-1).astype(jnp.bfloat16)  10.3 us
    ppermute x1, starting transfers between devices, shifted(): return lax.ppermute(block, axis, route)  8.19 us
    all_to_all x1, starting transfers between devices, shards(): lax.all_to_all(ordered.reshape(columns, groups * count, 2 * BAND), 'win',...  7.7 us
    concatenate x1, other arithmetic, cross_block(): return jnp.concatenate([real_part, imag_part], axis=-1).astype(jnp.bfloat16)  7.41 us
  transfers between devices with their start and end apart: 3, of which 1 were waited for; matrix products, arithmetic and copies ran while one was open for 7% of the time, Pallas kernels for 0%

commit v1 on v0

v1 whole, which is shorter than its diff:
```python
import functools
import math

import jax
import jax.numpy as jnp
import numpy as np
from jax import lax
from jax.experimental import pallas as pl
from jax.experimental.pallas import tpu as pltpu
from jax.sharding import PartitionSpec as P

LEN = 16384
FACTOR = 128
BAND = 512
KMAX = 128
COUNT = 32
QUARTERS = BAND // FACTOR
TURNS = QUARTERS + 1
WINDOWS = 8
LIMIT = 48 * 1024 * 1024

VMEM = pl.BlockSpec(memory_space=pltpu.VMEM)
SMEM = pl.BlockSpec(memory_space=pltpu.SMEM)
BF16 = jnp.bfloat16
F32 = jnp.float32


def tables():
    index = np.arange(FACTOR)
    turns = np.mod(index[:, None] * index[None, :], FACTOR)
    angles = turns * (2.0 * math.pi / FACTOR)
    cosine, sine = np.cos(angles), np.sin(angles)
    first = np.concatenate([cosine, -sine]).astype(BF16)
    theta = index[:, None] * index[None, :] * (2.0 * math.pi / LEN)
    twist = np.stack([np.cos(theta), -np.sin(theta)]).astype(np.float32)
    outer = np.stack([cosine, sine])[:, :72].astype(np.float32)
    place = np.arange(BAND)
    source = (place % QUARTERS) * FACTOR + place // QUARTERS
    interleave = np.zeros((BAND, BAND), np.float32)
    interleave[source, place] = 1.0
    return first, twist, outer, interleave.astype(BF16)


def dot(a, b):
    return jnp.dot(a, b, preferred_element_type=F32)


def dot_t(a, b):
    return lax.dot_general(a, b, (((1,), (1,)), ((), ())), preferred_element_type=F32)


def front_kernel(taps_used, start, taps, x, first, twist, outer, product, edge, head):
    lane = lax.broadcasted_iota(jnp.int32, (1, 2 * FACTOR), 1)
    kept = jnp.where(lane < taps_used[0], taps[...], 0.0)
    spread = jnp.broadcast_to(kept, (2 * FACTOR, 2 * FACTOR))
    matrix = pltpu.roll(spread, FACTOR, 1, stride=1, stride_axis=0)[:, :FACTOR].astype(BF16)
    head[...] = matrix[:FACTOR]
    both = jnp.concatenate([matrix[FACTOR:], matrix[:FACTOR]], axis=1)
    low = lax.shift_right_logical(start[0], 7)
    cosine = outer[0, pl.ds(low, 8), :]
    sine = outer[1, pl.ds(low, 8), :]
    scale = 1.0 / FACTOR
    second = jnp.concatenate(
        [jnp.concatenate([cosine, sine], axis=1), jnp.concatenate([-sine, cosine], axis=1)], axis=0
    )
    second = (second * scale).astype(BF16)
    twist_re = twist[0]
    twist_im = twist[1]
    for turn in range(TURNS):
        c = cosine[turn : turn + 1] * scale
        s = sine[turn : turn + 1] * scale
        edge[turn] = (twist_re * c + twist_im * s).astype(BF16)
        edge[TURNS + turn] = (twist_im * c - twist_re * s).astype(BF16)
    row = lax.broadcasted_iota(jnp.int32, (FACTOR, FACTOR), 0)

    def one(i, carry):
        parts = []
        for j in range(2):
            y = dot(x[2 * i + j], both)
            late = jnp.where(row == 0, 0.0, pltpu.roll(y[:, FACTOR:], 1, 0))
            parts.append((y[:, :FACTOR] + late).astype(BF16))
        section = dot(first[...], jnp.concatenate(parts, axis=1))
        halves = []
        for j in range(2):
            re = section[:FACTOR, j * FACTOR : (j + 1) * FACTOR]
            im = section[FACTOR:, j * FACTOR : (j + 1) * FACTOR]
            halves.append(
                jnp.concatenate([re * twist_re - im * twist_im, re * twist_im + im * twist_re], axis=1).astype(BF16)
            )
        got = dot_t(second, jnp.concatenate(halves, axis=0))
        for j in range(2):
            product[:, pl.ds(2 * i + j, 1), :] = got[:, None, j * FACTOR : (j + 1) * FACTOR]
        return carry

    lax.fori_loop(0, COUNT // 2, one, 0, unroll=2)


def whiten_kernel(start, product, edge, head, tail, interleave, out):
    extra = dot(tail[...], head[...]).astype(BF16)
    parts = []
    for o in range(2):
        for turn in range(TURNS):
            parts.append(product[8 * o + turn] + dot_t(extra, edge[TURNS * o + turn]))
    residue = lax.broadcasted_iota(jnp.int32, (COUNT, FACTOR), 1)
    early = residue >= (start[0] & (FACTOR - 1))
    white = [[], []]
    for q in range(QUARTERS):
        re = jnp.where(early, parts[q], parts[q + 1])
        im = jnp.where(early, parts[TURNS + q], parts[TURNS + q + 1])
        scale = lax.rsqrt(re * re + im * im + 1.0)
        white[0].append((re * scale).astype(BF16))
        white[1].append((im * scale).astype(BF16))
    flat = jnp.concatenate([jnp.concatenate(white[0], axis=1), jnp.concatenate(white[1], axis=1)], axis=0)
    placed = dot(flat, interleave[...])
    for z in range(4):
        for x in range(4):
            lanes = slice(x * FACTOR, (x + 1) * FACTOR)
            for core in range(2):
                at = (z * 2 + core) * 4
                piece = jnp.concatenate(
                    [placed[at : at + 4, lanes], placed[COUNT + at : COUNT + at + 4, lanes]], axis=0
                )
                out[z * 8 + x * 2 + core] = piece.astype(BF16)


def order_kernel(blocks, every, out):
    for i in range(COUNT):
        out[i] = every[blocks[i]]


M_STEP = 8


def cross_kernel(place, *refs):
    mine, theirs, rows = refs[:3]
    out, held, col, row = refs[-4:]
    step = pl.program_id(0)
    part = pl.program_id(1)
    chunk, z, core = place[0], place[1], place[2]

    @pl.when((step == 0) & (part == 0))
    def _():
        upper = lax.broadcasted_iota(jnp.int32, (8, FACTOR), 0) < 4
        first = core == 0

        def cols(w, carry):
            for other in range(4):
                d = z ^ other
                for b in range(4):
                    a = mine[d, w, b].astype(F32)
                    t = theirs[d, w, b].astype(F32)
                    c0 = jnp.where(first, a, t)
                    c1 = jnp.where(first, t, a)
                    col[w, 0, b * 4 + other] = jnp.where(upper, c0, pltpu.roll(c1, 4, 0))
                    col[w, 1, b * 4 + other] = jnp.where(upper, pltpu.roll(c0, 4, 0), c1)
            return carry

        lax.fori_loop(0, WINDOWS, cols, 0)

    @pl.when((part == 0))
    def _():
        upper = lax.broadcasted_iota(jnp.int32, (8, FACTOR), 0) < 4

        def rows_of(w, carry):
            at = step * 8 + chunk * 2
            c0 = rows[w, at].astype(F32)
            c1 = rows[w, at + 1].astype(F32)
            row[w, 0] = jnp.where(upper, c0, pltpu.roll(c1, 4, 0))
            row[w, 1] = jnp.where(upper, pltpu.roll(c0, 4, 0), c1)
            return carry

        lax.fori_loop(0, WINDOWS, rows_of, 0)

        def pair(t, carry):
            vr = [[col[w, 0, 2 * t + h] for w in range(WINDOWS)] for h in range(2)]
            vi = [[col[w, 1, 2 * t + h] for w in range(WINDOWS)] for h in range(2)]
            for m in range(M_STEP):
                re = [None, None]
                im = [None, None]
                for w in range(WINDOWS):
                    ur = row[w, 0, pl.ds(m, 1), :]
                    ui = row[w, 1, pl.ds(m, 1), :]
                    for h in range(2):
                        a = ur * vr[h][w] + ui * vi[h][w]
                        b = ui * vr[h][w] - ur * vi[h][w]
                        re[h] = a if w == 0 else re[h] + a
                        im[h] = b if w == 0 else im[h] + b
                out[m, pl.ds(pl.multiple_of(16 * t, 16), 16), :] = jnp.concatenate(re, axis=0).astype(BF16)
                held[m, pl.ds(pl.multiple_of(16 * t, 16), 16), :] = jnp.concatenate(im, axis=0).astype(BF16)
            return carry

        lax.fori_loop(0, 8, pair, 0)

    @pl.when(part == 1)
    def _():
        out[...] = held[...]


def cross(place, mine, theirs, rows, before):
    ins = [VMEM, VMEM, VMEM]
    args = [mine, theirs, rows]
    aliases = {}
    if before is not None:
        ins.append(pl.BlockSpec(memory_space=pl.ANY))
        args.append(before)
        aliases = {4: 0}
    return pl.pallas_call(
        cross_kernel,
        grid_spec=pltpu.PrefetchScalarGridSpec(
            num_scalar_prefetch=1,
            grid=(COUNT // M_STEP, 2),
            in_specs=ins,
            out_specs=pl.BlockSpec((M_STEP, 128, FACTOR), lambda s, o, place: (s, 0, place[0] + 4 * o)),
            scratch_shapes=[
                pltpu.VMEM((M_STEP, 128, FACTOR), BF16),
                pltpu.VMEM((WINDOWS, 2, 16, 8, FACTOR), F32),
                pltpu.VMEM((WINDOWS, 2, 8, FACTOR), F32),
            ],
        ),
        out_shape=jax.ShapeDtypeStruct((COUNT, 128, 2 * BAND), BF16),
        input_output_aliases=aliases,
        compiler_params=pltpu.CompilerParams(vmem_limit_bytes=LIMIT),
    )(place, *args)


def chan_swap(dz, dx, dc):
    spots = [(z, x, c) for z in range(4) for x in range(4) for c in range(2)]
    at = lambda z, x, c: z * 8 + x * 2 + c
    return [(at(z, x, c), at(z ^ dz, x ^ dx, c ^ dc)) for z, x, c in spots]


def shards(samples, fir_taps, tap_counts, band_start, grid_blocks):
    first, twist, outer, interleave = tables()
    tail = lax.ppermute(samples[:, -FACTOR:], "win", [(i, i + 1) for i in range(WINDOWS - 1)])
    product, edge, head = pl.pallas_call(
        front_kernel,
        in_specs=[SMEM, SMEM, VMEM, VMEM, VMEM, VMEM, VMEM],
        out_specs=[VMEM, VMEM, VMEM],
        out_shape=[
            jax.ShapeDtypeStruct((16, COUNT, FACTOR), F32),
            jax.ShapeDtypeStruct((2 * TURNS, FACTOR, FACTOR), BF16),
            jax.ShapeDtypeStruct((FACTOR, FACTOR), BF16),
        ],
        compiler_params=pltpu.CompilerParams(vmem_limit_bytes=LIMIT),
    )(
        tap_counts,
        band_start,
        jnp.pad(fir_taps, (0, FACTOR)).reshape(1, 2 * FACTOR),
        samples.reshape(COUNT, FACTOR, FACTOR),
        first,
        twist,
        outer,
    )
    pieces = pl.pallas_call(
        whiten_kernel,
        in_specs=[SMEM, VMEM, VMEM, VMEM, VMEM, VMEM],
        out_specs=VMEM,
        out_shape=jax.ShapeDtypeStruct((COUNT, 8, FACTOR), BF16),
        compiler_params=pltpu.CompilerParams(vmem_limit_bytes=LIMIT),
    )(band_start, product, edge, head, tail, interleave)
    every = lax.all_to_all(pieces, "chan", 0, 0, tiled=True)
    ordered = pl.pallas_call(
        order_kernel,
        in_specs=[SMEM, VMEM],
        out_specs=VMEM,
        out_shape=jax.ShapeDtypeStruct((COUNT, 8, FACTOR), BF16),
    )(grid_blocks, every)
    mine_rows = lax.all_to_all(ordered, "chan", 0, 0, tiled=True)
    sent = jnp.concatenate(
        [ordered.reshape(WINDOWS, 4, 8, FACTOR), jnp.broadcast_to(mine_rows[None], (WINDOWS, COUNT, 8, FACTOR))], axis=1
    )
    got = lax.all_to_all(sent, "win", 0, 0, tiled=True)
    cols, rows = got[:, :4], got[:, 4:]
    mine = [jnp.stack([cols] + [lax.ppermute(cols, "chan", chan_swap(d, 0, 0)) for d in (1, 2, 3)])]
    mine += [lax.ppermute(mine[0], "chan", chan_swap(0, d, 0)) for d in (1, 2, 3)]
    here = lax.axis_index("chan")
    z, x, core = here // 8, (here // 2) % 4, here % 2
    out = None
    for d in range(4):
        theirs = lax.ppermute(mine[d], "chan", chan_swap(0, 0, 1))
        place = jnp.stack([x ^ d, z, core]).astype(jnp.int32)
        out = cross(place, mine[d], theirs, rows, out)
    return out


def solution(mesh):
    placed = (P("chan", "win"), P(), P("win"), P(), P())
    return jax.shard_map(
        shards, mesh=mesh, in_specs=placed, out_specs=P("chan", "win", None), check_vma=False
    )
```

time: 251 us -> 140 us (0.56)
  Pallas kernels: 0 us -> 43.8 us
  blocking collectives: 94 us -> 52.5 us
  waiting for transfers between devices: 57.9 us -> 16.8 us
  local copies, waits for them, and re-layouts: 29.3 us -> 6.61 us
  other arithmetic: 22.4 us -> 1.16 us
  matrix products: 15.6 us -> 0 us
  between operations: 14.9 us -> 1.41 us
    all_gather x1 -> x0, blocking collectives: 94 us -> none  [shards(): row_panel = lax.all_gather(mine, 'win', axis=0, tiled=True)]
    all_gather x1 -> x0, waiting for transfers between devices: 57.9 us -> none  [shards(): every = lax.all_gather(spectra, 'chan', axis=0, tiled=True)]
    all_to_all x0 -> x3, blocking collectives: none -> 52.5 us  [the longest x1 27.3 us: shards(): got = lax.all_to_all(sent, 'win', 0, 0, tiled=True)]
    pallas_call x0 -> x7, Pallas kernels: none -> 43.8 us  [the longest x4 34.1 us: cross(): pl.pallas_call(cross_kernel, grid_spec=pltpu.PrefetchScalarGridSpec(num_s...]
    ppermute x1 -> x11, waiting for transfers between devices: 0.01 us -> 16.8 us  [the longest x3 11.5 us: shards(): lax.ppermute(mine[0], 'chan', chan_swap(0, d, 0))]
    dot_general x6 -> x0, matrix products: 15.6 us -> none  [the longest x1 4.78 us: cross_block(): jnp.einsum('wap,wbp->abp', left_re, right_im, preferred_element_type=jnp....]
    concatenate x1 -> x0, local copies, waits for them, and re-layouts: 12.1 us -> none  [cross_block(): return jnp.concatenate([real_part, imag_part], axis=-1).astype(jnp.bfloat16)]
    reduce_sum x1 -> x0, other arithmetic: 10.3 us -> none  [fir_matrix(): return jnp.sum(picked, axis=-1).astype(jnp.bfloat16)]
  transfers between devices with their start and end apart: 3 -> 11, of which waited for: 1 -> 6; matrix products, arithmetic and copies ran while one was open for 7% -> 2% of each run, Pallas kernels for 0% -> 24%
where the time goes in v1:
time: 140 us; the launch traced here: 139 us
  blocking collectives  52.5 us (38%)
  Pallas kernels  43.8 us (31%)
  waiting for transfers between devices  16.8 us (12%)
  starting transfers between devices  16.5 us (12%)
  local copies, waits for them, and re-layouts  6.61 us (5%)
  between operations  1.41 us (1%)
    pallas_call x4, Pallas kernels, cross(): pl.pallas_call(cross_kernel, grid_spec=pltpu.PrefetchScalarGridSpec(num_s...  34.1 us
    all_to_all x1, blocking collectives, shards(): got = lax.all_to_all(sent, 'win', 0, 0, tiled=True)  27.3 us
    all_to_all x1, blocking collectives, shards(): every = lax.all_to_all(pieces, 'chan', 0, 0, tiled=True)  13.4 us
    all_to_all x1, blocking collectives, shards(): mine_rows = lax.all_to_all(ordered, 'chan', 0, 0, tiled=True)  11.7 us
    ppermute x3, waiting for transfers between devices, shards(): lax.ppermute(mine[0], 'chan', chan_swap(0, d, 0))  11.5 us
    ppermute x1, starting transfers between devices, shards(): lax.ppermute(samples[:, -FACTOR:], 'win', [(i, i + 1) for i in range(WIND...  8.18 us
    pallas_call x1, Pallas kernels, shards(): pl.pallas_call(front_kernel, in_specs=[SMEM, SMEM, VMEM, VMEM, VMEM, VMEM...  7.65 us
    ppermute x3, waiting for transfers between devices, shards(): lax.ppermute(cols, 'chan', chan_swap(d, 0, 0))  5.31 us
  transfers between devices with their start and end apart: 11, of which 6 were waited for; matrix products, arithmetic and copies ran while one was open for 2% of the time, Pallas kernels for 24%

profile of v1, /device:TPU:32, one launch (start us, length us, event | category | flops | bytes accessed | tf_op | source)
XLA Modules:
  0.0 138.9 jit_solution(13274760258615677717)
XLA Ops:
  0.7 8.2 %collective-permute-start = (bf16[32,128]{1,0:T(8,128)(2,1)S(1)}, bf16[32,128]{1,0:T(8,128)(2,1)S(1)}, u32[]{:S(2)}, u32[]{:S(2)}) collective-permute-start(bf16[32,128]{1,0:T(8,128)(2,1)S(1)} %slice.9), channel_id=1, source_target_pairs={{0,1},{1,2},{2,3},{3,4},{4,5},{5,6},{6,7},{8,9},{9,10},{10,11},{11... | collective-permute-start | bytes 24584 | tf_op jit(solution)/shard_map/ppermute | solution.py:234
  9.5 1.5 %copy.13 = bf16[4,8,128,128]{3,2,1,0:T(8,128)(2,1)S(1)} copy(bf16[4,8,128,128]{3,1,2,0:T(8,128)(2,1)} %bitcast.17) | data formatting | bytes 2097152
  12.3 0.9 copy-done.1
  13.2 0.9 copy-done.2
  15.0 7.7 %shard_map.91 = (f32[16,32,128]{2,1,0:T(8,128)S(1)}, bf16[10,128,128]{2,1,0:T(8,128)(2,1)S(1)}, bf16[128,128]{1,0:T(8,128)(2,1)S(1)}) custom-call(s32[1]{0:T(128)S(6)} %copy.17.taps_used, s32[1]{0:T(128)S(6)} %copy.18.start, f32[1,256]{1,0:T(1,128)S(1)} %bitcast.16, bf16[32,128,128]{2,1,0:T(8,128)(2,1)S(1)} %bitcast.15, bf16[256,128]{1,0:T(8,128)(2,1)S(1)} %copy-done.3, ...), custom_call_target="tpu_custom_call" | custom-call | tf_op jit(solution)/shard_map/pallas_call | solution.py:235
  22.6 1.0 copy-done
  24.2 13.4 %all_to_all.15.every = bf16[32,8,128]{2,1,0:T(8,128)(2,1)} all-to-all(bf16[32,8,128]{2,1,0:T(8,128)(2,1)S(1)} %shard_map.92), channel_id=1, replica_groups=mesh['chan'=32,'win'=8] {'chan'}, dimensions={0} | all-to-all | bytes 131072 | tf_op jit(solution)/shard_map/all_to_all | solution.py:261
  37.7 1.5 %shard_map.93 = bf16[32,8,128]{2,1,0:T(8,128)(2,1)} custom-call(s32[32]{0:T(128)} %blocks.1, bf16[32,8,128]{2,1,0:T(8,128)(2,1)} %all_to_all.15.every), custom_call_target="tpu_custom_call" | custom-call | tf_op jit(solution)/shard_map/pallas_call | solution.py:262
  39.2 11.7 %all_to_all.16 = bf16[32,8,128]{2,1,0:T(8,128)(2,1)S(1)} all-to-all(bf16[32,8,128]{2,1,0:T(8,128)(2,1)} %shard_map.93), channel_id=1, replica_groups=mesh['chan'=32,'win'=8] {'chan'}, dimensions={0} | all-to-all | bytes 131072 | tf_op jit(solution)/shard_map/all_to_all | solution.py:268
  51.0 0.9 pad_maximum_fusion
  51.9 27.3 %all_to_all.17 = bf16[8,36,8,128]{3,2,1,0:T(8,128)(2,1)S(1)} all-to-all(bf16[8,36,8,128]{3,2,1,0:T(8,128)(2,1)S(1)} %pad_maximum_fusion), channel_id=1, replica_groups=mesh['chan'=32,'win'=8] {'win'}, dimensions={0} | all-to-all | bytes 1179648 | tf_op jit(solution)/shard_map/all_to_all | solution.py:272
  79.3 2.1 %collective-permute-start.2 = (bf16[8,4,8,128]{3,2,1,0:T(8,128)(2,1)S(1)}, bf16[8,4,8,128]{3,2,1,0:T(8,128)(2,1)S(1)}, u32[]{:S(2)}, u32[]{:S(2)}) collective-permute-start(bf16[8,4,8,128]{3,2,1,0:T(8,128)(2,1)S(1)} %get-tuple-element.12), channel_id=1, source_target_pairs={{0,128},{8,136},{16,144},{24,152},{32,160},{40,168},{48,176},{56,1... | collective-permute-start | bytes 196616 | tf_op jit(solution)/shard_map/ppermute | solution.py:274
  81.4 1.4 %collective-permute-start.3 = (bf16[8,4,8,128]{3,2,1,0:T(8,128)(2,1)S(1)}, bf16[8,4,8,128]{3,2,1,0:T(8,128)(2,1)S(1)}, u32[]{:S(2)}, u32[]{:S(2)}) collective-permute-start(bf16[8,4,8,128]{3,2,1,0:T(8,128)(2,1)S(1)} %get-tuple-element.12), channel_id=1, source_target_pairs={{0,192},{8,200},{16,208},{24,216},{32,224},{40,232},{48,240},{56,2... | collective-permute-start | bytes 196616 | tf_op jit(solution)/shard_map/ppermute | solution.py:274
  83.6 1.9 %collective-permute-done.2 = bf16[8,4,8,128]{3,2,1,0:T(8,128)(2,1)S(1)} collective-permute-done((bf16[8,4,8,128]{3,2,1,0:T(8,128)(2,1)S(1)}, bf16[8,4,8,128]{3,2,1,0:T(8,128)(2,1)S(1)}, u32[]{:S(2)}, u32[]{:S(2)}) %collective-permute-start.2) | collective-permute-done | bytes 65568 | tf_op jit(solution)/shard_map/ppermute | solution.py:274
  85.4 2.6 %collective-permute-done.3 = bf16[8,4,8,128]{3,2,1,0:T(8,128)(2,1)S(1)} collective-permute-done((bf16[8,4,8,128]{3,2,1,0:T(8,128)(2,1)S(1)}, bf16[8,4,8,128]{3,2,1,0:T(8,128)(2,1)S(1)}, u32[]{:S(2)}, u32[]{:S(2)}) %collective-permute-start.3) | collective-permute-done | bytes 65568 | tf_op jit(solution)/shard_map/ppermute | solution.py:274
  88.8 2.1 %collective-permute-start.6 = (bf16[4,8,4,8,128]{4,3,2,1,0:T(8,128)(2,1)S(1)}, bf16[4,8,4,8,128]{4,3,2,1,0:T(8,128)(2,1)S(1)}, u32[]{:S(2)}, u32[]{:S(2)}) collective-permute-start(bf16[4,8,4,8,128]{4,3,2,1,0:T(8,128)(2,1)S(1)} %pad_maximum_fusion.1.refs_0_), channel_id=1, source_target_pairs={{0,32},{8,40},{16,48},{24,56},{32,0},{40,8},{48,16},{56,24},{64,96... | collective-permute-start | bytes 786440 | tf_op jit(solution)/shard_map/ppermute | solution.py:275
  90.9 2.0 %collective-permute-start.4 = (bf16[4,8,4,8,128]{4,3,2,1,0:T(8,128)(2,1)S(1)}, bf16[4,8,4,8,128]{4,3,2,1,0:T(8,128)(2,1)S(1)}, u32[]{:S(2)}, u32[]{:S(2)}) collective-permute-start(bf16[4,8,4,8,128]{4,3,2,1,0:T(8,128)(2,1)S(1)} %pad_maximum_fusion.1.refs_0_), channel_id=1, source_target_pairs={{0,48},{8,56},{16,32},{24,40},{32,16},{40,24},{48,0},{56,8},{64,11... | collective-permute-start | bytes 786440 | tf_op jit(solution)/shard_map/ppermute | solution.py:275
  92.9 4.5 %collective-permute-done.8.refs_0_ = bf16[4,8,4,8,128]{4,3,2,1,0:T(8,128)(2,1)S(1)} collective-permute-done((bf16[4,8,4,8,128]{4,3,2,1,0:T(8,128)(2,1)S(1)}, bf16[4,8,4,8,128]{4,3,2,1,0:T(8,128)(2,1)S(1)}, u32[]{:S(2)}, u32[]{:S(2)}) %collective-permute-start.8) | collective-permute-done | bytes 262176 | tf_op jit(solution)/shard_map/ppermute | solution.py:275
  97.4 4.4 %collective-permute-done.6.refs_0_ = bf16[4,8,4,8,128]{4,3,2,1,0:T(8,128)(2,1)S(1)} collective-permute-done((bf16[4,8,4,8,128]{4,3,2,1,0:T(8,128)(2,1)S(1)}, bf16[4,8,4,8,128]{4,3,2,1,0:T(8,128)(2,1)S(1)}, u32[]{:S(2)}, u32[]{:S(2)}) %collective-permute-start.6) | collective-permute-done | bytes 262176 | tf_op jit(solution)/shard_map/ppermute | solution.py:275
  101.9 2.6 %collective-permute-done.4.refs_0_ = bf16[4,8,4,8,128]{4,3,2,1,0:T(8,128)(2,1)S(1)} collective-permute-done((bf16[4,8,4,8,128]{4,3,2,1,0:T(8,128)(2,1)S(1)}, bf16[4,8,4,8,128]{4,3,2,1,0:T(8,128)(2,1)S(1)}, u32[]{:S(2)}, u32[]{:S(2)}) %collective-permute-start.4) | collective-permute-done | bytes 262176 | tf_op jit(solution)/shard_map/ppermute | solution.py:275
  104.7 8.5 %shard_map.94.refs_3_ = bf16[32,128,1024]{2,1,0:T(8,128)(2,1)} custom-call(s32[3]{0:T(128)S(1)} %add_add_fusion.3.place, bf16[4,8,4,8,128]{4,3,2,1,0:T(8,128)(2,1)S(1)} %pad_maximum_fusion.1.refs_0_, bf16[4,8,4,8,128]{4,3,2,1,0:T(8,128)(2,1)S(1)} %collective-permute-done.10.refs_1_, bf16[8,32,8,128]{3,2,1,0:T(8,128)(2,1)S(1)} %slice.13.refs_2_), custom_call_target="tpu_custom_call" | custom-call | tf_op jit(solution)/shard_map/pallas_call | solution.py:207
  113.2 8.5 %shard_map.95.refs_3_ = bf16[32,128,1024]{2,1,0:T(8,128)(2,1)} custom-call(s32[3]{0:T(128)S(1)} %add_add_fusion.2.place, bf16[4,8,4,8,128]{4,3,2,1,0:T(8,128)(2,1)S(1)} %collective-permute-done.8.refs_0_, bf16[4,8,4,8,128]{4,3,2,1,0:T(8,128)(2,1)S(1)} %collective-permute-done.9.refs_1_, ...), custom_call_target="tpu_custom_call", output_to_operand_aliasing={{}: (4, {})} | custom-call | tf_op jit(solution)/shard_map/pallas_call | solution.py:207
  121.8 8.5 %shard_map.96.refs_3_ = bf16[32,128,1024]{2,1,0:T(8,128)(2,1)} custom-call(s32[3]{0:T(128)S(1)} %get-tuple-element.14.place, bf16[4,8,4,8,128]{4,3,2,1,0:T(8,128)(2,1)S(1)} %collective-permute-done.6.refs_0_, bf16[4,8,4,8,128]{4,3,2,1,0:T(8,128)(2,1)S(1)} %collective-permute-done.7.refs_1_, ...), custom_call_target="tpu_custom_call", output_to_operand_aliasing={{}: (4, {})} | custom-call | tf_op jit(solution)/shard_map/pallas_call | solution.py:207
  130.3 8.5 %shard_map.97 = bf16[32,128,1024]{2,1,0:T(8,128)(2,1)} custom-call(s32[3]{0:T(128)S(1)} %get-tuple-element.13.place, bf16[4,8,4,8,128]{4,3,2,1,0:T(8,128)(2,1)S(1)} %collective-permute-done.4.refs_0_, bf16[4,8,4,8,128]{4,3,2,1,0:T(8,128)(2,1)S(1)} %collective-permute-done.5.refs_1_, ...), custom_call_target="tpu_custom_call", output_to_operand_aliasing={{}: (4, {})} | custom-call | tf_op jit(solution)/shard_map/pallas_call | solution.py:207
  (27 shorter events, 4.7 us)
Async XLA Ops:
  0.7 21.9 %collective-permute-start = (bf16[32,128]{1,0:T(8,128)(2,1)S(1)}, bf16[32,128]{1,0:T(8,128)(2,1)S(1)}, u32[]{:S(2)}, u32[]{:S(2)}) collective-permute-start(bf16[32,128]{1,0:T(8,128)(2,1)S(1)} %slice.9), channel_id=1, source_target_pairs={{0,1},{1,2},{2,3},{3,4},{4,5},{5,6},{6,7},{8,9},{9,10},{10,11},{11... | collective-permute-start | bytes 24584 | tf_op jit(solution)/shard_map/ppermute | solution.py:234
  12.3 0.9 copy-start.1
  13.2 0.9 copy-start.2
  14.1 0.8 copy-start.3
  22.6 1.0 copy-start
  79.2 4.4 %collective-permute-start.1 = (bf16[8,4,8,128]{3,2,1,0:T(8,128)(2,1)S(1)}, bf16[8,4,8,128]{3,2,1,0:T(8,128)(2,1)S(1)}, u32[]{:S(2)}, u32[]{:S(2)}) collective-permute-start(bf16[8,4,8,128]{3,2,1,0:T(8,128)(2,1)S(1)} %get-tuple-element.12), channel_id=1, source_target_pairs={{0,64},{8,72},{16,80},{24,88},{32,96},{40,104},{48,112},{56,120},{... | collective-permute-start | bytes 196616 | tf_op jit(solution)/shard_map/ppermute | solution.py:274
  79.3 6.2 %collective-permute-start.2 = (bf16[8,4,8,128]{3,2,1,0:T(8,128)(2,1)S(1)}, bf16[8,4,8,128]{3,2,1,0:T(8,128)(2,1)S(1)}, u32[]{:S(2)}, u32[]{:S(2)}) collective-permute-start(bf16[8,4,8,128]{3,2,1,0:T(8,128)(2,1)S(1)} %get-tuple-element.12), channel_id=1, source_target_pairs={{0,128},{8,136},{16,144},{24,152},{32,160},{40,168},{48,176},{56,1... | collective-permute-start | bytes 196616 | tf_op jit(solution)/shard_map/ppermute | solution.py:274
  81.4 6.7 %collective-permute-start.3 = (bf16[8,4,8,128]{3,2,1,0:T(8,128)(2,1)S(1)}, bf16[8,4,8,128]{3,2,1,0:T(8,128)(2,1)S(1)}, u32[]{:S(2)}, u32[]{:S(2)}) collective-permute-start(bf16[8,4,8,128]{3,2,1,0:T(8,128)(2,1)S(1)} %get-tuple-element.12), channel_id=1, source_target_pairs={{0,192},{8,200},{16,208},{24,216},{32,224},{40,232},{48,240},{56,2... | collective-permute-start | bytes 196616 | tf_op jit(solution)/shard_map/ppermute | solution.py:274
  88.1 9.3 %collective-permute-start.8 = (bf16[4,8,4,8,128]{4,3,2,1,0:T(8,128)(2,1)S(1)}, bf16[4,8,4,8,128]{4,3,2,1,0:T(8,128)(2,1)S(1)}, u32[]{:S(2)}, u32[]{:S(2)}) collective-permute-start(bf16[4,8,4,8,128]{4,3,2,1,0:T(8,128)(2,1)S(1)} %pad_maximum_fusion.1.refs_0_), channel_id=1, source_target_pairs={{0,16},{8,24},{16,0},{24,8},{32,48},{40,56},{48,32},{56,40},{64,80... | collective-permute-start | bytes 786440 | tf_op jit(solution)/shard_map/ppermute | solution.py:275
  88.8 13.1 %collective-permute-start.6 = (bf16[4,8,4,8,128]{4,3,2,1,0:T(8,128)(2,1)S(1)}, bf16[4,8,4,8,128]{4,3,2,1,0:T(8,128)(2,1)S(1)}, u32[]{:S(2)}, u32[]{:S(2)}) collective-permute-start(bf16[4,8,4,8,128]{4,3,2,1,0:T(8,128)(2,1)S(1)} %pad_maximum_fusion.1.refs_0_), channel_id=1, source_target_pairs={{0,32},{8,40},{16,48},{24,56},{32,0},{40,8},{48,16},{56,24},{64,96... | collective-permute-start | bytes 786440 | tf_op jit(solution)/shard_map/ppermute | solution.py:275
  90.9 13.5 %collective-permute-start.4 = (bf16[4,8,4,8,128]{4,3,2,1,0:T(8,128)(2,1)S(1)}, bf16[4,8,4,8,128]{4,3,2,1,0:T(8,128)(2,1)S(1)}, u32[]{:S(2)}, u32[]{:S(2)}) collective-permute-start(bf16[4,8,4,8,128]{4,3,2,1,0:T(8,128)(2,1)S(1)} %pad_maximum_fusion.1.refs_0_), channel_id=1, source_target_pairs={{0,48},{8,56},{16,32},{24,40},{32,16},{40,24},{48,0},{56,8},{64,11... | collective-permute-start | bytes 786440 | tf_op jit(solution)/shard_map/ppermute | solution.py:275
  92.9 11.8 %collective-permute-start.10 = (bf16[4,8,4,8,128]{4,3,2,1,0:T(8,128)(2,1)S(1)}, bf16[4,8,4,8,128]{4,3,2,1,0:T(8,128)(2,1)S(1)}, u32[]{:S(2)}, u32[]{:S(2)}) collective-permute-start(bf16[4,8,4,8,128]{4,3,2,1,0:T(8,128)(2,1)S(1)} %pad_maximum_fusion.1.refs_0_), channel_id=1, source_target_pairs={{0,8},{8,0},{16,24},{24,16},{32,40},{40,32},{48,56},{56,48},{64,72... | collective-permute-start | bytes 786440 | tf_op jit(solution)/shard_map/ppermute | solution.py:280
  97.4 15.8 %collective-permute-start.9 = (bf16[4,8,4,8,128]{4,3,2,1,0:T(8,128)(2,1)S(1)}, bf16[4,8,4,8,128]{4,3,2,1,0:T(8,128)(2,1)S(1)}, u32[]{:S(2)}, u32[]{:S(2)}) collective-permute-start(bf16[4,8,4,8,128]{4,3,2,1,0:T(8,128)(2,1)S(1)} %collective-permute-done.8.refs_0_), channel_id=1, source_target_pairs={{0,8},{8,0},{16,24},{24,16},{32,40},{40,32},{48,56},{56,48},{64,72... | collective-permute-start | bytes 786440 | tf_op jit(solution)/shard_map/ppermute | solution.py:280
  101.8 19.9 %collective-permute-start.7 = (bf16[4,8,4,8,128]{4,3,2,1,0:T(8,128)(2,1)S(1)}, bf16[4,8,4,8,128]{4,3,2,1,0:T(8,128)(2,1)S(1)}, u32[]{:S(2)}, u32[]{:S(2)}) collective-permute-start(bf16[4,8,4,8,128]{4,3,2,1,0:T(8,128)(2,1)S(1)} %collective-permute-done.6.refs_0_), channel_id=1, source_target_pairs={{0,8},{8,0},{16,24},{24,16},{32,40},{40,32},{48,56},{56,48},{64,72... | collective-permute-start | bytes 786440 | tf_op jit(solution)/shard_map/ppermute | solution.py:280
  104.4 25.9 %collective-permute-start.5 = (bf16[4,8,4,8,128]{4,3,2,1,0:T(8,128)(2,1)S(1)}, bf16[4,8,4,8,128]{4,3,2,1,0:T(8,128)(2,1)S(1)}, u32[]{:S(2)}, u32[]{:S(2)}) collective-permute-start(bf16[4,8,4,8,128]{4,3,2,1,0:T(8,128)(2,1)S(1)} %collective-permute-done.4.refs_0_), channel_id=1, source_target_pairs={{0,8},{8,0},{16,24},{24,16},{32,40},{40,32},{48,56},{56,48},{64,72... | collective-permute-start | bytes 786440 | tf_op jit(solution)/shard_map/ppermute | solution.py:280

commit v2 on v1

v2 whole, which is shorter than its diff:
```python
import functools
import math

import jax
import jax.numpy as jnp
import numpy as np
from jax import lax
from jax.experimental import pallas as pl
from jax.experimental.pallas import tpu as pltpu
from jax.sharding import PartitionSpec as P

LEN = 16384
FACTOR = 128
BAND = 512
KMAX = 128
COUNT = 32
QUARTERS = BAND // FACTOR
TURNS = QUARTERS + 1
WINDOWS = 8
BATCH = 8
LIMIT = 48 * 1024 * 1024

VMEM = pl.BlockSpec(memory_space=pltpu.VMEM)
SMEM = pl.BlockSpec(memory_space=pltpu.SMEM)
HBM = pl.BlockSpec(memory_space=pltpu.HBM)
BF16 = jnp.bfloat16
F32 = jnp.float32


def tables():
    index = np.arange(FACTOR)
    turns = np.mod(index[:, None] * index[None, :], FACTOR)
    angles = turns * (2.0 * math.pi / FACTOR)
    cosine, sine = np.cos(angles), np.sin(angles)
    first = np.concatenate([cosine, -sine]).astype(BF16)
    theta = index[:, None] * index[None, :] * (2.0 * math.pi / LEN)
    twist = np.stack([np.cos(theta), -np.sin(theta)]).astype(np.float32)
    outer = np.stack([cosine, sine])[:, :72].astype(np.float32)
    place = np.arange(BAND)
    source = (place % QUARTERS) * FACTOR + place // QUARTERS
    interleave = np.zeros((BAND, BAND), np.float32)
    interleave[source, place] = 1.0
    return first, twist, outer, interleave.astype(BF16)


def dot(a, b):
    return jnp.dot(a, b, preferred_element_type=F32)


def dot_t(a, b):
    return lax.dot_general(a, b, (((1,), (1,)), ((), ())), preferred_element_type=F32)


def front_kernel(
    used_in, start_in, taps_in, x, first_in, twist_in, outer_in,
    product, edge, head, taps_used, start, taps, first, twist, outer, sems,
):
    copies = [
        pltpu.make_async_copy(source, target, sems.at[i])
        for i, (source, target) in enumerate(
            (
                (used_in, taps_used),
                (start_in, start),
                (taps_in, taps),
                (outer_in, outer),
                (twist_in, twist),
                (first_in, first),
            )
        )
    ]
    for copy in copies:
        copy.start()
    for copy in copies[:3]:
        copy.wait()
    lane = lax.broadcasted_iota(jnp.int32, (1, FACTOR), 1)
    kept = jnp.where(lane < taps_used[0], taps[...], 0.0)
    kept = jnp.concatenate([kept, jnp.zeros_like(kept)], axis=1)
    spread = jnp.broadcast_to(kept, (2 * FACTOR, 2 * FACTOR))
    matrix = pltpu.roll(spread, FACTOR, 1, stride=1, stride_axis=0)[:, :FACTOR].astype(BF16)
    head[...] = matrix[:FACTOR]
    both = jnp.concatenate([matrix[FACTOR:], matrix[:FACTOR]], axis=1)
    low = lax.shift_right_logical(start[0], 7)
    for copy in copies[3:]:
        copy.wait()
    cosine = outer[0, pl.ds(low, 8), :]
    sine = outer[1, pl.ds(low, 8), :]
    scale = 1.0 / FACTOR
    second = jnp.concatenate(
        [jnp.concatenate([cosine, sine], axis=1), jnp.concatenate([-sine, cosine], axis=1)], axis=0
    )
    second = (second * scale).astype(BF16)
    twist_re = twist[0]
    twist_im = twist[1]
    for turn in range(TURNS):
        c = cosine[turn : turn + 1] * scale
        s = sine[turn : turn + 1] * scale
        edge[turn] = (twist_re * c + twist_im * s).astype(BF16)
        edge[TURNS + turn] = (twist_im * c - twist_re * s).astype(BF16)
    row = lax.broadcasted_iota(jnp.int32, (FACTOR, FACTOR), 0)

    def some(i, carry):
        y = dot(x[pl.ds(BATCH * i, BATCH)].reshape(BATCH * FACTOR, FACTOR), both)
        parts = []
        for j in range(BATCH):
            now = y[j * FACTOR : (j + 1) * FACTOR]
            late = jnp.where(row == 0, 0.0, pltpu.roll(now[:, FACTOR:], 1, 0))
            parts.append((now[:, :FACTOR] + late).astype(BF16))
        section = dot(first[...], jnp.concatenate(parts, axis=1))
        halves = []
        for j in range(BATCH):
            re = section[:FACTOR, j * FACTOR : (j + 1) * FACTOR]
            im = section[FACTOR:, j * FACTOR : (j + 1) * FACTOR]
            halves.append(
                jnp.concatenate([re * twist_re - im * twist_im, re * twist_im + im * twist_re], axis=1).astype(BF16)
            )
        got = dot_t(second, jnp.concatenate(halves, axis=0))
        for j in range(BATCH):
            product[:, pl.ds(BATCH * i + j, 1), :] = got[:, None, j * FACTOR : (j + 1) * FACTOR]
        return carry

    lax.fori_loop(0, COUNT // BATCH, some, 0)


def whiten_kernel(start_in, blocks_in, product, edge, head, tail, interleave_in, out, blocks, interleave, start, sems):
    copies = [
        pltpu.make_async_copy(source, target, sems.at[i])
        for i, (source, target) in enumerate(((start_in, start), (blocks_in, blocks), (interleave_in, interleave)))
    ]
    for copy in copies:
        copy.start()
    extra = dot(tail[...], head[...]).astype(BF16)
    parts = []
    for o in range(2):
        for turn in range(TURNS):
            parts.append(product[8 * o + turn] + dot_t(extra, edge[TURNS * o + turn]))
    for copy in copies:
        copy.wait()
    residue = lax.broadcasted_iota(jnp.int32, (COUNT, FACTOR), 1)
    early = residue >= (start[0] & (FACTOR - 1))
    white = [[], []]
    for q in range(QUARTERS):
        re = jnp.where(early, parts[q], parts[q + 1])
        im = jnp.where(early, parts[TURNS + q], parts[TURNS + q + 1])
        scale = lax.rsqrt(re * re + im * im + 1.0)
        white[0].append((re * scale).astype(BF16))
        white[1].append((im * scale).astype(BF16))
    flat = jnp.concatenate([jnp.concatenate(white[0], axis=1), jnp.concatenate(white[1], axis=1)], axis=0)
    placed = dot(flat, interleave[...])
    for z in range(4):
        for x in range(4):
            lanes = slice(x * FACTOR, (x + 1) * FACTOR)
            for core in range(2):
                at = (z * 2 + core) * 4
                piece = jnp.concatenate(
                    [placed[at : at + 4, lanes], placed[COUNT + at : COUNT + at + 4, lanes]], axis=0
                )
                out[z * 8 + x * 2 + core] = piece.astype(BF16)


def order_kernel(blocks, every, out):
    for i in range(COUNT):
        out[i] = every[blocks[i]]


M_STEP = 8
GROUPS = 8
WIDTH = FACTOR // GROUPS


def spiral(parts, bits):
    for s in range(3):
        parts = [jnp.where(bits[s], parts[(a + (1 << s)) % GROUPS], parts[a]) for a in range(GROUPS)]
    return parts


def cross_kernel(parts, place, *refs):
    count = len(parts)
    mine, theirs, rows = refs[:count], refs[count : 2 * count], refs[2 * count]
    out, left, coef, mixed, stage, done = refs[-6:]
    x, z, core = place[0], place[1], place[2]
    upper = lax.broadcasted_iota(jnp.int32, (8, FACTOR), 0) < 4
    spot = lax.broadcasted_iota(jnp.int32, (8, FACTOR), 1) // WIDTH
    bits = [(spot & (1 << s)) != 0 for s in range(3)]
    inner = lax.broadcasted_iota(jnp.int32, (WIDTH, FACTOR), 0)
    lane = lax.broadcasted_iota(jnp.int32, (WIDTH, FACTOR), 1)
    diagonal = inner == (lane & (WIDTH - 1))

    def join(c0, c1):
        return jnp.where(upper, c0, pltpu.roll(c1, 4, 0)), jnp.where(upper, pltpu.roll(c0, 4, 0), c1)

    def cols(part, b, carry):
        for pair in range(2):
            tiles = []
            for half in range(2):
                d = z ^ (2 * pair + half)
                whole = [[], []]
                for w in range(WINDOWS):
                    a = mine[part][d, w, b].astype(F32)
                    t = theirs[part][d, w, b].astype(F32)
                    re, im = join(jnp.where(core == 0, a, t), jnp.where(core == 0, t, a))
                    whole[0].append(pltpu.roll(re, WIDTH * w, 1) if w else re)
                    whole[1].append(pltpu.roll(im, WIDTH * w, 1) if w else im)
                tiles.append([spiral(whole[i], bits) for i in range(2)])
            at = pl.multiple_of(b * 32 + pair * 16, 16)
            for g in range(GROUPS):
                for i in range(2):
                    packed = jnp.concatenate([tiles[h][i][-g % GROUPS] for h in range(2)], axis=0)
                    left[part, g, pl.ds(at, 16), i * FACTOR : (i + 1) * FACTOR] = packed.astype(BF16)
        return carry

    for part in range(count):
        lax.fori_loop(0, 4, functools.partial(cols, part), 0)

    def chunk_of(part):
        turn = jnp.int32(parts[0])
        for i in range(1, count):
            turn = jnp.where(part == i, parts[i], turn)
        return x ^ turn

    def multiply(step, slot):
        part = lax.shift_right_logical(step, 2)
        at = (step & 3) * 8 + chunk_of(part) * 2
        for w in range(WINDOWS):
            re, im = join(rows[w, at].astype(F32), rows[w, at + 1].astype(F32))
            for i, u in enumerate((re, im)):
                u = pltpu.roll(u, 0, 1, stride=WIDTH, stride_axis=0)
                for s in range(3):
                    u = jnp.where(bits[s], pltpu.roll(u, 8 - (1 << s), 0), u)
                coef[slot, w, i] = u
                if i == 0:
                    coef[slot, w, 2] = -u
        for g in range(GROUPS):
            blocks = [
                [
                    jnp.where(diagonal, coef[slot, w, i, pl.ds(-g % GROUPS, 1), :], 0.0).astype(BF16)
                    for i in range(3)
                ]
                for w in range(WINDOWS)
            ]
            order = [blocks[(c - g) % GROUPS] for c in range(GROUPS)]
            top = jnp.concatenate([jnp.concatenate([k[0], k[1]], axis=1) for k in order], axis=0)
            low = jnp.concatenate([jnp.concatenate([k[1], k[2]], axis=1) for k in order], axis=0)
            mixed[slot, g] = dot(left[part, g], jnp.concatenate([top, low], axis=0))

    def copies(step, slot):
        chunk = chunk_of(lax.shift_right_logical(step, 2))
        for o in range(2):
            lanes = pl.ds(pl.multiple_of((chunk + 4 * o) * FACTOR, FACTOR), FACTOR)
            yield pltpu.make_async_copy(
                stage.at[slot, o], out.at[pl.ds((step & 3) * M_STEP, M_STEP), :, lanes], done.at[slot, o]
            )

    def spread(slot):
        for t in range(8):
            for o in range(2):
                halves = []
                for h in range(2):
                    lanes = slice(o * FACTOR, (o + 1) * FACTOR)
                    parts = [mixed[slot, g, 16 * t + 8 * h : 16 * t + 8 * h + 8, lanes] for g in range(GROUPS)]
                    halves.append(spiral(parts, bits))
                for m in range(M_STEP):
                    pair = [pltpu.roll(x[-m % GROUPS], FACTOR - WIDTH * m, 1) if m else x[0] for x in halves]
                    stage[slot, o, m, 16 * t : 16 * t + 16, :] = jnp.concatenate(pair, axis=0).astype(BF16)

    steps = count * (COUNT // M_STEP)
    multiply(jnp.int32(0), 0)

    def both(i, carry):
        for slot in range(2):
            step = 2 * i + slot

            @pl.when(i > 0)
            def _():
                for copy in copies(step - 2, slot):
                    copy.wait()

            multiply(jnp.minimum(step + 1, steps - 1), 1 - slot)
            spread(slot)
            for copy in copies(step, slot):
                copy.start()
        return carry

    lax.fori_loop(0, steps // 2, both, 0)
    for slot in range(2):
        for copy in copies(jnp.int32(steps - 2 + slot), slot):
            copy.wait()


def cross(parts, place, mine, theirs, rows, before):
    args = [place, *mine, *theirs, rows]
    specs = [SMEM] + [VMEM] * (len(args) - 1)
    aliases = {}
    if before is not None:
        aliases = {len(args): 0}
        args.append(before)
        specs.append(pl.BlockSpec(memory_space=pl.ANY))
    return pl.pallas_call(
        functools.partial(cross_kernel, parts),
        in_specs=specs,
        out_specs=pl.BlockSpec(memory_space=pl.ANY),
        scratch_shapes=[
            pltpu.VMEM((len(parts), GROUPS, FACTOR, 2 * FACTOR), BF16),
            pltpu.VMEM((2, WINDOWS, 3, 8, FACTOR), F32),
            pltpu.VMEM((2, GROUPS, FACTOR, 2 * FACTOR), F32),
            pltpu.VMEM((2, 2, M_STEP, FACTOR, FACTOR), BF16),
            pltpu.SemaphoreType.DMA((2, 2)),
        ],
        out_shape=jax.ShapeDtypeStruct((COUNT, 128, 2 * BAND), BF16),
        input_output_aliases=aliases,
        compiler_params=pltpu.CompilerParams(vmem_limit_bytes=LIMIT),
    )(*args)


def chan_swap(dz, dx, dc):
    spots = [(z, x, c) for z in range(4) for x in range(4) for c in range(2)]
    at = lambda z, x, c: z * 8 + x * 2 + c
    return [(at(z, x, c), at(z ^ dz, x ^ dx, c ^ dc)) for z, x, c in spots]


def shards(samples, fir_taps, tap_counts, band_start, grid_blocks):
    first, twist, outer, interleave = tables()
    tail = lax.ppermute(samples[:, -FACTOR:], "win", [(i, i + 1) for i in range(WINDOWS - 1)])
    product, edge, head = pl.pallas_call(
        front_kernel,
        in_specs=[HBM, HBM, HBM, VMEM, HBM, HBM, HBM],
        out_specs=[VMEM, VMEM, VMEM],
        out_shape=[
            jax.ShapeDtypeStruct((16, COUNT, FACTOR), F32),
            jax.ShapeDtypeStruct((2 * TURNS, FACTOR, FACTOR), BF16),
            jax.ShapeDtypeStruct((FACTOR, FACTOR), BF16),
        ],
        scratch_shapes=[
            pltpu.SMEM((1,), jnp.int32),
            pltpu.SMEM((1,), jnp.int32),
            pltpu.VMEM((1, FACTOR), F32),
            pltpu.VMEM(first.shape, BF16),
            pltpu.VMEM(twist.shape, F32),
            pltpu.VMEM(outer.shape, F32),
            pltpu.SemaphoreType.DMA((6,)),
        ],
        compiler_params=pltpu.CompilerParams(vmem_limit_bytes=LIMIT),
    )(
        tap_counts,
        band_start,
        fir_taps.reshape(1, FACTOR),
        samples.reshape(COUNT, FACTOR, FACTOR),
        first,
        twist,
        outer,
    )
    pieces, blocks = pl.pallas_call(
        whiten_kernel,
        in_specs=[HBM, HBM, VMEM, VMEM, VMEM, VMEM, HBM],
        scratch_shapes=[
            pltpu.VMEM((BAND, BAND), BF16),
            pltpu.SMEM((1,), jnp.int32),
            pltpu.SemaphoreType.DMA((3,)),
        ],
        out_specs=[VMEM, SMEM],
        out_shape=[
            jax.ShapeDtypeStruct((COUNT, 8, FACTOR), BF16),
            jax.ShapeDtypeStruct((COUNT,), jnp.int32),
        ],
        compiler_params=pltpu.CompilerParams(vmem_limit_bytes=LIMIT),
    )(band_start, grid_blocks, product, edge, head, tail, interleave)
    every = lax.all_to_all(pieces, "chan", 0, 0, tiled=True)
    ordered = pl.pallas_call(
        order_kernel,
        in_specs=[SMEM, VMEM],
        out_specs=VMEM,
        out_shape=jax.ShapeDtypeStruct((COUNT, 8, FACTOR), BF16),
    )(blocks, every)
    cols = lax.all_to_all(ordered.reshape(WINDOWS, 4, 8, FACTOR), "win", 0, 0, tiled=True)
    ordered, cols = lax.optimization_barrier((ordered, cols))
    near = [lax.ppermute(cols, "chan", chan_swap(d, 0, 0)) for d in (1, 2, 3)]
    rows = lax.all_to_all(ordered, "chan", 0, 0, tiled=True)
    rows, near = lax.optimization_barrier((rows, near))
    mine = [jnp.stack([cols] + near)]
    mine += [lax.ppermute(mine[0], "chan", chan_swap(0, d, 0)) for d in (1, 2, 3)]
    theirs = [lax.ppermute(this, "chan", chan_swap(0, 0, 1)) for this in mine]
    rows = lax.all_to_all(
        jnp.broadcast_to(rows[None], (WINDOWS, COUNT, 8, FACTOR)), "win", 0, 0, tiled=True
    )
    here = lax.axis_index("chan")
    place = jnp.stack([(here // 2) % 4, here // 8, here % 2]).astype(jnp.int32)
    return cross((0, 1, 2, 3), place, mine, theirs, rows, None)


def solution(mesh):
    placed = (P("chan", "win"), P(), P("win"), P(), P())
    return jax.shard_map(
        shards, mesh=mesh, in_specs=placed, out_specs=P("chan", "win", None), check_vma=False
    )
```

time: 140 us -> 105 us (0.75)
  Pallas kernels: 43.8 us -> 19.4 us
  blocking collectives: 52.5 us -> 29.8 us
  starting transfers between devices: 16.5 us -> 25.4 us
  waiting for transfers between devices: 16.8 us -> 19.5 us
    pallas_call x6 -> x3, Pallas kernels: 42.3 us -> 17.9 us  [the longest x1 12.9 us: cross(): pl.pallas_call(functools.partial(cross_kernel, parts), in_specs=specs, ou...]
    all_to_all x2 -> x1, blocking collectives: 39 us -> 16.3 us  [shards(): lax.all_to_all(ordered.reshape(WINDOWS, 4, 8, FACTOR), 'win', 0, 0, tiled...]
    all_to_all x0 -> x2, starting transfers between devices: none -> 8.47 us  [the longest x1 4.97 us: shards(): rows = lax.all_to_all(ordered, 'chan', 0, 0, tiled=True)]
    all_to_all x0 -> x2, waiting for transfers between devices: none -> 2.53 us  [the longest x1 2.53 us: shards(): lax.all_to_all(jnp.broadcast_to(rows[None], (WINDOWS, COUNT, 8, FACTOR)),...]
    unnamed x9 -> x15, local copies, waits for them, and re-layouts: 5.13 us -> 6.44 us
  transfers between devices with their start and end apart: 11 -> 13, of which waited for: 6 -> 8; matrix products, arithmetic and copies ran while one was open for 2% -> 2% of each run, Pallas kernels for 24% -> 4%
where the time goes in v2:
time: 105 us; the launch traced here: 104 us
  blocking collectives  29.8 us (28%)
  starting transfers between devices  25.4 us (24%)
  waiting for transfers between devices  19.5 us (19%)
  Pallas kernels  19.4 us (18%)
  local copies, waits for them, and re-layouts  8 us (8%)
  between operations  1.4 us (1%)
    all_to_all x1, blocking collectives, shards(): lax.all_to_all(ordered.reshape(WINDOWS, 4, 8, FACTOR), 'win', 0, 0, tiled...  16.3 us
    all_to_all x1, blocking collectives, shards(): every = lax.all_to_all(pieces, 'chan', 0, 0, tiled=True)  13.4 us
    pallas_call x1, Pallas kernels, cross(): pl.pallas_call(functools.partial(cross_kernel, parts), in_specs=specs, ou...  12.9 us
    ppermute x3, waiting for transfers between devices, shards(): lax.ppermute(mine[0], 'chan', chan_swap(0, d, 0))  10.4 us
    ppermute x1, starting transfers between devices, shards(): lax.ppermute(samples[:, -FACTOR:], 'win', [(i, i + 1) for i in range(WIND...  8.18 us
    unnamed x15, local copies, waits for them, and re-layouts  6.44 us
    all_to_all x1, starting transfers between devices, shards(): rows = lax.all_to_all(ordered, 'chan', 0, 0, tiled=True)  4.97 us
    ppermute x3, waiting for transfers between devices, shards(): near = [lax.ppermute(cols, 'chan', chan_swap(d, 0, 0)) for d in (1, 2, 3)]  4.97 us
  transfers between devices with their start and end apart: 13, of which 8 were waited for; matrix products, arithmetic and copies ran while one was open for 2% of the time, Pallas kernels for 4%

profile of v2, /device:TPU:32, one launch (start us, length us, event | category | flops | bytes accessed | tf_op | source)
XLA Modules:
  0.0 103.5 jit_solution(16004303162728153700)
XLA Ops:
  0.7 8.2 %collective-permute-start = (bf16[32,128]{1,0:T(8,128)(2,1)S(1)}, bf16[32,128]{1,0:T(8,128)(2,1)S(1)}, u32[]{:S(2)}, u32[]{:S(2)}) collective-permute-start(bf16[32,128]{1,0:T(8,128)(2,1)S(1)} %slice.3), channel_id=1, source_target_pairs={{0,1},{1,2},{2,3},{3,4},{4,5},{5,6},{6,7},{8,9},{9,10},{10,11},{11... | collective-permute-start | bytes 24584 | tf_op jit(solution)/shard_map/ppermute | solution.py:322
  10.2 1.5 %copy.10 = bf16[4,8,128,128]{3,2,1,0:T(8,128)(2,1)S(1)} copy(bf16[4,8,128,128]{3,1,2,0:T(8,128)(2,1)} %bitcast.13) | data formatting | bytes 2097152
  11.7 0.9 copy-done.1
  12.6 0.9 copy-done.2
  13.5 0.8 copy-done.3
  14.9 3.9 %shard_map.91 = (f32[16,32,128]{2,1,0:T(8,128)S(1)}, bf16[10,128,128]{2,1,0:T(8,128)(2,1)S(1)}, bf16[128,128]{1,0:T(8,128)(2,1)S(1)}) custom-call(s32[1]{0:T(128)S(6)} %copy.11.used_in, s32[1]{0:T(128)S(6)} %copy.12.start_in, f32[1,128]{1,0:T(1,128)S(1)} %bitcast.12, bf16[32,128,128]{2,1,0:T(8,128)(2,1)S(1)} %bitcast.11, bf16[256,128]{1,0:T(8,128)(2,1)S(1)} %copy-done.3, ...), custom_call_target="tpu_custom_call" | custom-call | tf_op jit(solution)/shard_map/pallas_call | solution.py:323
  18.9 1.0 copy-done
  20.6 1.2 %shard_map.92 = (bf16[32,8,128]{2,1,0:T(8,128)(2,1)S(1)}, s32[32]{0:T(128)S(1)}) custom-call(s32[1]{0:T(128)S(6)} %copy.12.start_in, s32[32]{0:T(128)S(1)} %copy-done.5, f32[16,32,128]{2,1,0:T(8,128)S(1)} %get-tuple-element.16.product, bf16[10,128,128]{2,1,0:T(8,128)(2,1)S(1)} %get-tuple-element.17.edge, bf16[128,128]{1,0:T(8,128)(2,1)S(1)} %get-tuple-element.18.head, ...), custom_call_target="tpu_custom_call" | custom-call | tf_op jit(solution)/shard_map/pallas_call | solution.py:351
  21.8 13.4 %all_to_all.20.every = bf16[32,8,128]{2,1,0:T(8,128)(2,1)} all-to-all(bf16[32,8,128]{2,1,0:T(8,128)(2,1)S(1)} %get-tuple-element.20), channel_id=1, replica_groups=mesh['chan'=32,'win'=8] {'chan'}, dimensions={0} | all-to-all | bytes 131072 | tf_op jit(solution)/shard_map/all_to_all | solution.py:366
  35.2 1.5 %shard_map.93 = bf16[32,8,128]{2,1,0:T(8,128)(2,1)} custom-call(s32[32]{0:T(128)} %copy-done.6, bf16[32,8,128]{2,1,0:T(8,128)(2,1)} %all_to_all.20.every), custom_call_target="tpu_custom_call" | custom-call | tf_op jit(solution)/shard_map/pallas_call | solution.py:367
  36.7 16.3 %all_to_all.21 = bf16[8,4,8,128]{3,2,1,0:T(8,128)(2,1)S(1)} all-to-all(bf16[8,4,8,128]{3,2,1,0:T(8,128)(2,1)} %bitcast.14), channel_id=1, replica_groups=mesh['chan'=32,'win'=8] {'win'}, dimensions={0} | all-to-all | bytes 131072 | tf_op jit(solution)/shard_map/all_to_all | solution.py:373
  53.0 5.0 %all-to-all-start.2 = ((bf16[32,8,128]{2,1,0:T(8,128)(2,1)}), bf16[32,8,128]{2,1,0:T(8,128)(2,1)S(1)}, u32[]{:S(2)}, u32[]{:S(2)}) async-start(bf16[32,8,128]{2,1,0:T(8,128)(2,1)} %shard_map.93), calls=%async_computation.2 | async-start | bytes 131072 | tf_op jit(solution)/shard_map/all_to_all | solution.py:376
  58.0 1.6 %collective-permute-start.3 = (bf16[8,4,8,128]{3,2,1,0:T(8,128)(2,1)S(1)}, bf16[8,4,8,128]{3,2,1,0:T(8,128)(2,1)S(1)}, u32[]{:S(2)}, u32[]{:S(2)}) collective-permute-start(bf16[8,4,8,128]{3,2,1,0:T(8,128)(2,1)S(1)} %all_to_all.21), channel_id=1, source_target_pairs={{0,192},{8,200},{16,208},{24,216},{32,224},{40,232},{48,240},{56,2... | collective-permute-start | bytes 196616 | tf_op jit(solution)/shard_map/ppermute | solution.py:375
  59.6 1.1 %collective-permute-start.2 = (bf16[8,4,8,128]{3,2,1,0:T(8,128)(2,1)S(1)}, bf16[8,4,8,128]{3,2,1,0:T(8,128)(2,1)S(1)}, u32[]{:S(2)}, u32[]{:S(2)}) collective-permute-start(bf16[8,4,8,128]{3,2,1,0:T(8,128)(2,1)S(1)} %all_to_all.21), channel_id=1, source_target_pairs={{0,128},{8,136},{16,144},{24,152},{32,160},{40,168},{48,176},{56,1... | collective-permute-start | bytes 196616 | tf_op jit(solution)/shard_map/ppermute | solution.py:375
  60.8 1.3 %collective-permute-start.1 = (bf16[8,4,8,128]{3,2,1,0:T(8,128)(2,1)S(1)}, bf16[8,4,8,128]{3,2,1,0:T(8,128)(2,1)S(1)}, u32[]{:S(2)}, u32[]{:S(2)}) collective-permute-start(bf16[8,4,8,128]{3,2,1,0:T(8,128)(2,1)S(1)} %all_to_all.21), channel_id=1, source_target_pairs={{0,64},{8,72},{16,80},{24,88},{32,96},{40,104},{48,112},{56,120},{... | collective-permute-start | bytes 196616 | tf_op jit(solution)/shard_map/ppermute | solution.py:375
  62.0 4.7 %collective-permute-done.3 = bf16[8,4,8,128]{3,2,1,0:T(8,128)(2,1)S(1)} collective-permute-done((bf16[8,4,8,128]{3,2,1,0:T(8,128)(2,1)S(1)}, bf16[8,4,8,128]{3,2,1,0:T(8,128)(2,1)S(1)}, u32[]{:S(2)}, u32[]{:S(2)}) %collective-permute-start.3) | collective-permute-done | bytes 65568 | tf_op jit(solution)/shard_map/ppermute | solution.py:375
  67.0 0.9 broadcast_in_dim.2
  67.9 3.5 %all-to-all-start.3 = ((bf16[8,32,8,128]{3,2,1,0:T(8,128)(2,1)}), bf16[8,32,8,128]{3,2,1,0:T(8,128)(2,1)S(1)}, u32[]{:S(2)}, u32[]{:S(2)}) async-start(bf16[8,32,8,128]{3,2,1,0:T(8,128)(2,1)} %broadcast_in_dim.2), calls=%async_computation.3 | async-start | bytes 1048576 | tf_op jit(solution)/shard_map/all_to_all | solution.py:381
  71.4 2.8 %collective-permute-start.6 = (bf16[4,8,4,8,128]{4,3,2,1,0:T(8,128)(2,1)S(1)}, bf16[4,8,4,8,128]{4,3,2,1,0:T(8,128)(2,1)S(1)}, u32[]{:S(2)}, u32[]{:S(2)}) collective-permute-start(bf16[4,8,4,8,128]{4,3,2,1,0:T(8,128)(2,1)S(1)} %pad_maximum_fusion.refs_0_), channel_id=1, source_target_pairs={{0,48},{8,56},{16,32},{24,40},{32,16},{40,24},{48,0},{56,8},{64,11... | collective-permute-start | bytes 786440 | tf_op jit(solution)/shard_map/ppermute | solution.py:379
  74.2 0.8 collective-permute-start.5
  75.6 10.3 %collective-permute-done.6.refs_3_ = bf16[4,8,4,8,128]{4,3,2,1,0:T(8,128)(2,1)S(1)} collective-permute-done((bf16[4,8,4,8,128]{4,3,2,1,0:T(8,128)(2,1)S(1)}, bf16[4,8,4,8,128]{4,3,2,1,0:T(8,128)(2,1)S(1)}, u32[]{:S(2)}, u32[]{:S(2)}) %collective-permute-start.6) | collective-permute-done | bytes 262176 | tf_op jit(solution)/shard_map/ppermute | solution.py:379
  86.6 0.8 collective-permute-done.10.refs_7_
  88.2 2.5 %all-to-all-done.3.refs_8_ = bf16[8,32,8,128]{3,2,1,0:T(8,128)(2,1)S(1)} async-done(((bf16[8,32,8,128]{3,2,1,0:T(8,128)(2,1)}), bf16[8,32,8,128]{3,2,1,0:T(8,128)(2,1)S(1)}, u32[]{:S(2)}, u32[]{:S(2)}) %all-to-all-start.3) | async-done | bytes 524320 | tf_op jit(solution)/shard_map/all_to_all | solution.py:381
  90.7 12.9 %shard_map.94 = bf16[32,128,1024]{2,1,0:T(8,128)(2,1)} custom-call(s32[3]{0:T(128)S(1)} %pad_add_fusion.place, bf16[4,8,4,8,128]{4,3,2,1,0:T(8,128)(2,1)S(1)} %pad_maximum_fusion.refs_0_, bf16[4,8,4,8,128]{4,3,2,1,0:T(8,128)(2,1)S(1)} %collective-permute-done.4.refs_1_, bf16[4,8,4,8,128]{4,3,2,1,0:T(8,128)(2,1)S(1)} %collective-permute-done.5.refs_2_, ...), custom_call_target="tpu_custom_call" | custom-call | tf_op jit(solution)/shard_map/pallas_call | solution.py:297
  (27 shorter events, 4.4 us)
Async XLA Ops:
  0.7 18.2 %collective-permute-start = (bf16[32,128]{1,0:T(8,128)(2,1)S(1)}, bf16[32,128]{1,0:T(8,128)(2,1)S(1)}, u32[]{:S(2)}, u32[]{:S(2)}) collective-permute-start(bf16[32,128]{1,0:T(8,128)(2,1)S(1)} %slice.3), channel_id=1, source_target_pairs={{0,1},{1,2},{2,3},{3,4},{4,5},{5,6},{6,7},{8,9},{9,10},{10,11},{11... | collective-permute-start | bytes 24584 | tf_op jit(solution)/shard_map/ppermute | solution.py:322
  11.7 0.9 copy-start.1
  12.6 0.9 copy-start.2
  13.5 0.8 copy-start.3
  14.3 0.7 copy-start.4
  18.9 1.0 %copy-start = (bf16[512,512]{1,0:T(8,128)(2,1)S(1)}, bf16[512,512]{1,0:T(8,128)(2,1)}, u32[]{:S(2)}) copy-start(bf16[512,512]{1,0:T(8,128)(2,1)} %constant.61.clone.interleave_in) | copy-start | bytes 1572868
  19.9 0.7 copy-start.5
  21.7 13.5 %copy-start.6 = (s32[32]{0:T(128)}, s32[32]{0:T(128)S(1)}, u32[]{:S(2)}) copy-start(s32[32]{0:T(128)S(1)} %get-tuple-element.19.blocks) | copy-start | bytes 388
  53.0 14.0 %all-to-all-start.2 = ((bf16[32,8,128]{2,1,0:T(8,128)(2,1)}), bf16[32,8,128]{2,1,0:T(8,128)(2,1)S(1)}, u32[]{:S(2)}, u32[]{:S(2)}) async-start(bf16[32,8,128]{2,1,0:T(8,128)(2,1)} %shard_map.93), calls=%async_computation.2 | async-start | bytes 131072 | tf_op jit(solution)/shard_map/all_to_all | solution.py:376
  58.0 8.7 %collective-permute-start.3 = (bf16[8,4,8,128]{3,2,1,0:T(8,128)(2,1)S(1)}, bf16[8,4,8,128]{3,2,1,0:T(8,128)(2,1)S(1)}, u32[]{:S(2)}, u32[]{:S(2)}) collective-permute-start(bf16[8,4,8,128]{3,2,1,0:T(8,128)(2,1)S(1)} %all_to_all.21), channel_id=1, source_target_pairs={{0,192},{8,200},{16,208},{24,216},{32,224},{40,232},{48,240},{56,2... | collective-permute-start | bytes 196616 | tf_op jit(solution)/shard_map/ppermute | solution.py:375
  59.6 7.1 %collective-permute-start.2 = (bf16[8,4,8,128]{3,2,1,0:T(8,128)(2,1)S(1)}, bf16[8,4,8,128]{3,2,1,0:T(8,128)(2,1)S(1)}, u32[]{:S(2)}, u32[]{:S(2)}) collective-permute-start(bf16[8,4,8,128]{3,2,1,0:T(8,128)(2,1)S(1)} %all_to_all.21), channel_id=1, source_target_pairs={{0,128},{8,136},{16,144},{24,152},{32,160},{40,168},{48,176},{56,1... | collective-permute-start | bytes 196616 | tf_op jit(solution)/shard_map/ppermute | solution.py:375
  60.8 6.2 %collective-permute-start.1 = (bf16[8,4,8,128]{3,2,1,0:T(8,128)(2,1)S(1)}, bf16[8,4,8,128]{3,2,1,0:T(8,128)(2,1)S(1)}, u32[]{:S(2)}, u32[]{:S(2)}) collective-permute-start(bf16[8,4,8,128]{3,2,1,0:T(8,128)(2,1)S(1)} %all_to_all.21), channel_id=1, source_target_pairs={{0,64},{8,72},{16,80},{24,88},{32,96},{40,104},{48,112},{56,120},{... | collective-permute-start | bytes 196616 | tf_op jit(solution)/shard_map/ppermute | solution.py:375
  67.9 22.8 %all-to-all-start.3 = ((bf16[8,32,8,128]{3,2,1,0:T(8,128)(2,1)}), bf16[8,32,8,128]{3,2,1,0:T(8,128)(2,1)S(1)}, u32[]{:S(2)}, u32[]{:S(2)}) async-start(bf16[8,32,8,128]{3,2,1,0:T(8,128)(2,1)} %broadcast_in_dim.2), calls=%async_computation.3 | async-start | bytes 1048576 | tf_op jit(solution)/shard_map/all_to_all | solution.py:381
  71.4 14.4 %collective-permute-start.6 = (bf16[4,8,4,8,128]{4,3,2,1,0:T(8,128)(2,1)S(1)}, bf16[4,8,4,8,128]{4,3,2,1,0:T(8,128)(2,1)S(1)}, u32[]{:S(2)}, u32[]{:S(2)}) collective-permute-start(bf16[4,8,4,8,128]{4,3,2,1,0:T(8,128)(2,1)S(1)} %pad_maximum_fusion.refs_0_), channel_id=1, source_target_pairs={{0,48},{8,56},{16,32},{24,40},{32,16},{40,24},{48,0},{56,8},{64,11... | collective-permute-start | bytes 786440 | tf_op jit(solution)/shard_map/ppermute | solution.py:379
  74.2 11.6 %collective-permute-start.5 = (bf16[4,8,4,8,128]{4,3,2,1,0:T(8,128)(2,1)S(1)}, bf16[4,8,4,8,128]{4,3,2,1,0:T(8,128)(2,1)S(1)}, u32[]{:S(2)}, u32[]{:S(2)}) collective-permute-start(bf16[4,8,4,8,128]{4,3,2,1,0:T(8,128)(2,1)S(1)} %pad_maximum_fusion.refs_0_), channel_id=1, source_target_pairs={{0,32},{8,40},{16,48},{24,56},{32,0},{40,8},{48,16},{56,24},{64,96... | collective-permute-start | bytes 786440 | tf_op jit(solution)/shard_map/ppermute | solution.py:379
  75.1 11.4 %collective-permute-start.4 = (bf16[4,8,4,8,128]{4,3,2,1,0:T(8,128)(2,1)S(1)}, bf16[4,8,4,8,128]{4,3,2,1,0:T(8,128)(2,1)S(1)}, u32[]{:S(2)}, u32[]{:S(2)}) collective-permute-start(bf16[4,8,4,8,128]{4,3,2,1,0:T(8,128)(2,1)S(1)} %pad_maximum_fusion.refs_0_), channel_id=1, source_target_pairs={{0,16},{8,24},{16,0},{24,8},{32,48},{40,56},{48,32},{56,40},{64,80... | collective-permute-start | bytes 786440 | tf_op jit(solution)/shard_map/ppermute | solution.py:379
  75.6 11.0 %collective-permute-start.7 = (bf16[4,8,4,8,128]{4,3,2,1,0:T(8,128)(2,1)S(1)}, bf16[4,8,4,8,128]{4,3,2,1,0:T(8,128)(2,1)S(1)}, u32[]{:S(2)}, u32[]{:S(2)}) collective-permute-start(bf16[4,8,4,8,128]{4,3,2,1,0:T(8,128)(2,1)S(1)} %pad_maximum_fusion.refs_0_), channel_id=1, source_target_pairs={{0,8},{8,0},{16,24},{24,16},{32,40},{40,32},{48,56},{56,48},{64,72... | collective-permute-start | bytes 786440 | tf_op jit(solution)/shard_map/ppermute | solution.py:380
  85.9 1.5 %collective-permute-start.10 = (bf16[4,8,4,8,128]{4,3,2,1,0:T(8,128)(2,1)S(1)}, bf16[4,8,4,8,128]{4,3,2,1,0:T(8,128)(2,1)S(1)}, u32[]{:S(2)}, u32[]{:S(2)}) collective-permute-start(bf16[4,8,4,8,128]{4,3,2,1,0:T(8,128)(2,1)S(1)} %collective-permute-done.6.refs_3_), channel_id=1, source_target_pairs={{0,8},{8,0},{16,24},{24,16},{32,40},{40,32},{48,56},{56,48},{64,72... | collective-permute-start | bytes 786440 | tf_op jit(solution)/shard_map/ppermute | solution.py:380
  85.9 1.9 %collective-permute-start.9 = (bf16[4,8,4,8,128]{4,3,2,1,0:T(8,128)(2,1)S(1)}, bf16[4,8,4,8,128]{4,3,2,1,0:T(8,128)(2,1)S(1)}, u32[]{:S(2)}, u32[]{:S(2)}) collective-permute-start(bf16[4,8,4,8,128]{4,3,2,1,0:T(8,128)(2,1)S(1)} %collective-permute-done.5.refs_2_), channel_id=1, source_target_pairs={{0,8},{8,0},{16,24},{24,16},{32,40},{40,32},{48,56},{56,48},{64,72... | collective-permute-start | bytes 786440 | tf_op jit(solution)/shard_map/ppermute | solution.py:380
  86.5 1.7 %collective-permute-start.8 = (bf16[4,8,4,8,128]{4,3,2,1,0:T(8,128)(2,1)S(1)}, bf16[4,8,4,8,128]{4,3,2,1,0:T(8,128)(2,1)S(1)}, u32[]{:S(2)}, u32[]{:S(2)}) collective-permute-start(bf16[4,8,4,8,128]{4,3,2,1,0:T(8,128)(2,1)S(1)} %collective-permute-done.4.refs_1_), channel_id=1, source_target_pairs={{0,8},{8,0},{16,24},{24,16},{32,40},{40,32},{48,56},{56,48},{64,72... | collective-permute-start | bytes 786440 | tf_op jit(solution)/shard_map/ppermute | solution.py:380

commit v3 on v2

v3 whole, which is shorter than its diff:
```python
import functools
import math

import jax
import jax.numpy as jnp
import numpy as np
from jax import lax
from jax.experimental import pallas as pl
from jax.experimental.pallas import tpu as pltpu
from jax.sharding import PartitionSpec as P

LEN = 16384
FACTOR = 128
BAND = 512
KMAX = 128
COUNT = 32
QUARTERS = BAND // FACTOR
WINDOWS = 8
BATCH = 8
GROUPS = 8
WIDTH = FACTOR // GROUPS
SLOTS = 4
LIMIT = 48 * 1024 * 1024

VMEM = pl.BlockSpec(memory_space=pltpu.VMEM)
SMEM = pl.BlockSpec(memory_space=pltpu.SMEM)
BF16 = jnp.bfloat16
F32 = jnp.float32


def tables():
    index = np.arange(FACTOR)
    angles = np.mod(index[:, None] * index[None, :], FACTOR) * (2.0 * math.pi / FACTOR)
    theta = index[:, None] * index[None, :] * (2.0 * math.pi / LEN)
    parts = [np.cos(angles), -np.sin(angles), np.cos(theta), -np.sin(theta)]
    return np.concatenate(parts).astype(np.float32)


def dot(a, b):
    return jnp.dot(a, b, preferred_element_type=F32)


def dot_t(a, b):
    return lax.dot_general(a, b, (((1,), (1,)), ((), ())), preferred_element_type=F32)


def front_kernel(taps_used, start, window, taps, x, tail, table, out, product, before):
    lane = lax.broadcasted_iota(jnp.int32, (1, FACTOR), 1)
    kept = jnp.where(lane < taps_used[0], taps[...], 0.0)
    kept = jnp.concatenate([kept, jnp.zeros_like(kept)], axis=1)
    spread = jnp.broadcast_to(kept, (2 * FACTOR, 2 * FACTOR))
    matrix = pltpu.roll(spread, FACTOR, 1, stride=1, stride_axis=0)[:, :FACTOR].astype(BF16)
    both = jnp.concatenate([matrix[FACTOR:], matrix[:FACTOR]], axis=1)
    before[...] = dot(tail[...], matrix[:FACTOR])
    first = table[: 2 * FACTOR].astype(BF16)
    low = lax.shift_right_logical(start[0], 7)
    row = lax.broadcasted_iota(jnp.int32, (8, FACTOR), 0)
    pick = (lax.broadcasted_iota(jnp.int32, (8, FACTOR), 1) == low + row).astype(F32).astype(BF16)
    cosine = dot(pick, first[:FACTOR])
    sine = dot(pick, first[FACTOR:])
    second = jnp.concatenate(
        [jnp.concatenate([cosine, -sine], axis=1), jnp.concatenate([sine, cosine], axis=1)], axis=0
    )
    second = (second * (1.0 / FACTOR)).astype(BF16)
    top = lax.broadcasted_iota(jnp.int32, (FACTOR, FACTOR), 0) == 0

    def some(i, carry):
        y = dot(x[pl.ds(BATCH * i, BATCH)].reshape(BATCH * FACTOR, FACTOR), both)
        parts = []
        for j in range(BATCH):
            now = y[j * FACTOR : (j + 1) * FACTOR]
            late = jnp.where(top, before[pl.ds(BATCH * i + j, 1), :], pltpu.roll(now[:, FACTOR:], 1, 0))
            parts.append((now[:, :FACTOR] + late).astype(BF16))
        section = dot(first, jnp.concatenate(parts, axis=1))
        halves = []
        for j in range(BATCH):
            re = section[:FACTOR, j * FACTOR : (j + 1) * FACTOR]
            im = section[FACTOR:, j * FACTOR : (j + 1) * FACTOR]
            twist_re = table[2 * FACTOR : 3 * FACTOR]
            twist_im = table[3 * FACTOR :]
            halves.append(
                jnp.concatenate([re * twist_re - im * twist_im, re * twist_im + im * twist_re], axis=1).astype(BF16)
            )
        got = dot_t(second, jnp.concatenate(halves, axis=0))
        for j in range(BATCH):
            product[:, pl.ds(BATCH * i + j, 1), :] = got[:, None, j * FACTOR : (j + 1) * FACTOR]
        return carry

    lax.fori_loop(0, COUNT // BATCH, some, 0)

    early = lax.broadcasted_iota(jnp.int32, (COUNT, FACTOR), 1) >= (start[0] & (FACTOR - 1))
    residue = lax.broadcasted_iota(jnp.int32, (FACTOR, BAND), 0)
    lane = lax.broadcasted_iota(jnp.int32, (FACTOR, BAND), 1)
    place = (lane & -FACTOR) + ((lane - WIDTH * window[0]) & (FACTOR - 1))
    placed = None
    for q in range(QUARTERS):
        re = jnp.where(early, product[q], product[q + 1])
        im = jnp.where(early, product[8 + q], product[9 + q])
        scale = lax.rsqrt(re * re + im * im + 1.0)
        white = jnp.concatenate([re * scale, im * scale], axis=0).astype(BF16)
        moved = dot(white, (place == QUARTERS * residue + q).astype(F32).astype(BF16))
        placed = moved if placed is None else placed + moved
    for z in range(4):
        for quarter in range(4):
            for o in range(2):
                at = o * COUNT + z * 8
                piece = placed[at : at + 8, quarter * FACTOR : (quarter + 1) * FACTOR]
                out[z * 8 + quarter * 2 + o] = piece.astype(BF16)


def order_kernel(blocks, every, out):
    for i in range(COUNT):
        out[i] = every[blocks[i]]


M_STEP = 8


def spiral(parts, bits):
    for s in range(3):
        parts = [jnp.where(bits[s], parts[(a + (1 << s)) % GROUPS], parts[a]) for a in range(GROUPS)]
    return parts


def cross_kernel(parts, place, *refs):
    count = len(parts)
    mine, theirs, rows = refs[:count], refs[count : 2 * count], refs[2 * count]
    out, left, coef, mixed, stage, done = refs[-6:]
    x, z, core = place[0], place[1], place[2]
    spot = lax.broadcasted_iota(jnp.int32, (8, FACTOR), 1) // WIDTH
    bits = [(spot & (1 << s)) != 0 for s in range(3)]
    inner = lax.broadcasted_iota(jnp.int32, (WIDTH, FACTOR), 0)
    lane = lax.broadcasted_iota(jnp.int32, (WIDTH, FACTOR), 1)
    diagonal = inner == (lane & (WIDTH - 1))

    def cols(part, b, carry):
        for pair in range(2):
            tiles = []
            for half in range(2):
                d = z ^ (2 * pair + half)
                whole = [[], []]
                for w in range(WINDOWS):
                    a = mine[part][d, w, b].astype(F32)
                    t = theirs[part][d, w, b].astype(F32)
                    whole[0].append(jnp.where(core == 0, a, t))
                    whole[1].append(jnp.where(core == 0, t, a))
                tiles.append([spiral(whole[i], bits) for i in range(2)])
            at = pl.multiple_of(b * 32 + pair * 16, 16)
            for g in range(GROUPS):
                for i in range(2):
                    packed = jnp.concatenate([tiles[h][i][-g % GROUPS] for h in range(2)], axis=0)
                    left[part, g, pl.ds(at, 16), i * FACTOR : (i + 1) * FACTOR] = packed.astype(BF16)
        return carry

    for part in range(count):
        lax.fori_loop(0, 4, functools.partial(cols, part), 0)

    def chunk_of(part):
        turn = jnp.int32(parts[0])
        for i in range(1, count):
            turn = jnp.where(part == i, parts[i], turn)
        return x ^ turn

    def multiply(step, slot):
        part = lax.shift_right_logical(step, 2)
        at = (step & 3) * 8 + chunk_of(part) * 2
        for w in range(WINDOWS):
            for i in range(2):
                u = rows[w, at + i].astype(F32)
                if w:
                    u = pltpu.roll(u, FACTOR - WIDTH * w, 1)
                u = pltpu.roll(u, 0, 1, stride=WIDTH, stride_axis=0)
                for s in range(3):
                    u = jnp.where(bits[s], pltpu.roll(u, 8 - (1 << s), 0), u)
                coef[slot, w, i] = u
                if i == 0:
                    coef[slot, w, 2] = -u
        for g in range(GROUPS):
            blocks = [
                [
                    jnp.where(diagonal, coef[slot, w, i, pl.ds(-g % GROUPS, 1), :], 0.0).astype(BF16)
                    for i in range(3)
                ]
                for w in range(WINDOWS)
            ]
            order = [blocks[(c - g) % GROUPS] for c in range(GROUPS)]
            top = jnp.concatenate([jnp.concatenate([k[0], k[1]], axis=1) for k in order], axis=0)
            low = jnp.concatenate([jnp.concatenate([k[1], k[2]], axis=1) for k in order], axis=0)
            mixed[slot, g] = dot(left[part, g], jnp.concatenate([top, low], axis=0))

    def copies(step):
        slot = step % SLOTS
        chunk = chunk_of(lax.shift_right_logical(step, 2))
        for o in range(2):
            lanes = pl.ds(pl.multiple_of((chunk + 4 * o) * FACTOR, FACTOR), FACTOR)
            yield pltpu.make_async_copy(
                stage.at[slot, o], out.at[pl.ds((step & 3) * M_STEP, M_STEP), :, lanes], done.at[slot, o]
            )

    def spread(slot, step):
        target = step % SLOTS
        for t in range(8):
            for o in range(2):
                halves = []
                for h in range(2):
                    lanes = slice(o * FACTOR, (o + 1) * FACTOR)
                    parts = [mixed[slot, g, 16 * t + 8 * h : 16 * t + 8 * h + 8, lanes] for g in range(GROUPS)]
                    halves.append(spiral(parts, bits))
                for m in range(M_STEP):
                    pair = [pltpu.roll(x[-m % GROUPS], FACTOR - WIDTH * m, 1) if m else x[0] for x in halves]
                    stage[target, o, m, 16 * t : 16 * t + 16, :] = jnp.concatenate(pair, axis=0).astype(BF16)

    steps = count * (COUNT // M_STEP)
    multiply(jnp.int32(0), 0)

    def both(i, carry):
        for slot in range(2):
            step = 2 * i + slot

            @pl.when(step >= SLOTS)
            def _():
                for copy in copies(step - SLOTS):
                    copy.wait()

            multiply(jnp.minimum(step + 1, steps - 1), 1 - slot)
            spread(slot, step)
            for copy in copies(step):
                copy.start()
        return carry

    lax.fori_loop(0, steps // 2, both, 0)
    for step in range(steps - SLOTS, steps):
        for copy in copies(jnp.int32(step)):
            copy.wait()


def cross(parts, place, mine, theirs, rows, before):
    args = [place, *mine, *theirs, rows]
    specs = [SMEM] + [VMEM] * (len(args) - 1)
    aliases = {}
    if before is not None:
        aliases = {len(args): 0}
        args.append(before)
        specs.append(pl.BlockSpec(memory_space=pl.ANY))
    return pl.pallas_call(
        functools.partial(cross_kernel, parts),
        in_specs=specs,
        out_specs=pl.BlockSpec(memory_space=pl.ANY),
        scratch_shapes=[
            pltpu.VMEM((len(parts), GROUPS, FACTOR, 2 * FACTOR), BF16),
            pltpu.VMEM((2, WINDOWS, 3, 8, FACTOR), F32),
            pltpu.VMEM((2, GROUPS, FACTOR, 2 * FACTOR), F32),
            pltpu.VMEM((SLOTS, 2, M_STEP, FACTOR, FACTOR), BF16),
            pltpu.SemaphoreType.DMA((SLOTS, 2)),
        ],
        out_shape=jax.ShapeDtypeStruct((COUNT, 128, 2 * BAND), BF16),
        input_output_aliases=aliases,
        compiler_params=pltpu.CompilerParams(vmem_limit_bytes=LIMIT),
    )(*args)


def chan_swap(dz, dx, dc):
    spots = [(z, x, c) for z in range(4) for x in range(4) for c in range(2)]
    at = lambda z, x, c: z * 8 + x * 2 + c
    return [(at(z, x, c), at(z ^ dz, x ^ dx, c ^ dc)) for z, x, c in spots]


def shards(samples, fir_taps, tap_counts, band_start, grid_blocks):
    tail = lax.ppermute(samples[:, -FACTOR:], "win", [(i, i + 1) for i in range(WINDOWS - 1)])
    pieces = pl.pallas_call(
        front_kernel,
        in_specs=[SMEM, SMEM, SMEM, VMEM, VMEM, VMEM, VMEM],
        out_specs=VMEM,
        out_shape=jax.ShapeDtypeStruct((COUNT, 8, FACTOR), BF16),
        scratch_shapes=[pltpu.VMEM((16, COUNT, FACTOR), F32), pltpu.VMEM((COUNT, FACTOR), F32)],
        compiler_params=pltpu.CompilerParams(vmem_limit_bytes=LIMIT),
    )(
        tap_counts,
        band_start,
        lax.axis_index("win").reshape(1),
        fir_taps.reshape(1, FACTOR),
        samples.reshape(COUNT, FACTOR, FACTOR),
        tail,
        tables(),
    )
    every = lax.all_to_all(pieces, "chan", 0, 0, tiled=True)
    ordered = pl.pallas_call(
        order_kernel,
        in_specs=[SMEM, VMEM],
        out_specs=VMEM,
        out_shape=jax.ShapeDtypeStruct((COUNT, 8, FACTOR), BF16),
    )(grid_blocks, every)
    cols = lax.all_to_all(ordered.reshape(WINDOWS, 4, 8, FACTOR), "win", 0, 0, tiled=True)
    ordered, cols = lax.optimization_barrier((ordered, cols))
    near = [lax.ppermute(cols, "chan", chan_swap(d, 0, 0)) for d in (1, 2, 3)]
    rows = lax.all_to_all(ordered, "chan", 0, 0, tiled=True)
    rows, near = lax.optimization_barrier((rows, near))
    mine = [jnp.stack([cols] + near)]
    mine += [lax.ppermute(mine[0], "chan", chan_swap(0, d, 0)) for d in (1, 2, 3)]
    theirs = [lax.ppermute(this, "chan", chan_swap(0, 0, 1)) for this in mine]
    rows = lax.all_to_all(
        jnp.broadcast_to(rows[None], (WINDOWS, COUNT, 8, FACTOR)), "win", 0, 0, tiled=True
    )
    here = lax.axis_index("chan")
    place = jnp.stack([(here // 2) % 4, here // 8, here % 2]).astype(jnp.int32)
    return cross((0, 1, 2, 3), place, mine, theirs, rows, None)


def solution(mesh):
    placed = (P("chan", "win"), P(), P("win"), P(), P())
    return jax.shard_map(
        shards, mesh=mesh, in_specs=placed, out_specs=P("chan", "win", None), check_vma=False
    )
```

time: 105 us -> 101 us (0.962)
  Pallas kernels: 19.4 us -> 15.9 us
  local copies, waits for them, and re-layouts: 8 us -> 4.63 us
  blocking collectives: 29.8 us -> 32.3 us
    unnamed x15 -> x5, local copies, waits for them, and re-layouts: 6.44 us -> 3.07 us
    all_to_all x1, blocking collectives: 16.3 us -> 18.9 us  [shards(): lax.all_to_all(ordered.reshape(WINDOWS, 4, 8, FACTOR), 'win', 0, 0, tiled...]
    pallas_call x1, Pallas kernels: 12.9 us -> 10.8 us  [cross(): pl.pallas_call(functools.partial(cross_kernel, parts), in_specs=specs, ou...]
    pallas_call x2 -> x1, Pallas kernels: 5.07 us -> 3.6 us  [shards(): pl.pallas_call(front_kernel, in_specs=[SMEM, SMEM, SMEM, VMEM, VMEM, VMEM...]
  transfers between devices with their start and end apart: 13 -> 13, of which waited for: 8 -> 8; matrix products, arithmetic and copies ran while one was open for 2% -> 2% of each run, Pallas kernels for 4% -> 0%
where the time goes in v3:
time: 101 us; the launch traced here: 99.1 us
  blocking collectives  32.3 us (32%)
  starting transfers between devices  25.4 us (25%)
  waiting for transfers between devices  19.5 us (19%)
  Pallas kernels  15.9 us (16%)
  local copies, waits for them, and re-layouts  4.63 us (5%)
  between operations  1.38 us (1%)
    all_to_all x1, blocking collectives, shards(): lax.all_to_all(ordered.reshape(WINDOWS, 4, 8, FACTOR), 'win', 0, 0, tiled...  18.9 us
    all_to_all x1, blocking collectives, shards(): every = lax.all_to_all(pieces, 'chan', 0, 0, tiled=True)  13.4 us
    pallas_call x1, Pallas kernels, cross(): pl.pallas_call(functools.partial(cross_kernel, parts), in_specs=specs, ou...  10.8 us
    ppermute x3, waiting for transfers between devices, shards(): lax.ppermute(mine[0], 'chan', chan_swap(0, d, 0))  10.4 us
    ppermute x1, starting transfers between devices, shards(): lax.ppermute(samples[:, -FACTOR:], 'win', [(i, i + 1) for i in range(WIND...  8.18 us
    all_to_all x1, starting transfers between devices, shards(): rows = lax.all_to_all(ordered, 'chan', 0, 0, tiled=True)  4.97 us
    ppermute x3, waiting for transfers between devices, shards(): near = [lax.ppermute(cols, 'chan', chan_swap(d, 0, 0)) for d in (1, 2, 3)]  4.97 us
    ppermute x3, starting transfers between devices, shards(): lax.ppermute(mine[0], 'chan', chan_swap(0, d, 0))  4.18 us
  transfers between devices with their start and end apart: 13, of which 8 were waited for; matrix products, arithmetic and copies ran while one was open for 2% of the time, Pallas kernels for 0%

profile of v3, /device:TPU:32, one launch (start us, length us, event | category | flops | bytes accessed | tf_op | source)
XLA Modules:
  0.0 99.1 jit_solution(5790614204527671479)
XLA Ops:
  0.0 0.7 slice.3
  0.7 8.2 %collective-permute-start = (bf16[32,128]{1,0:T(8,128)(2,1)S(1)}, bf16[32,128]{1,0:T(8,128)(2,1)S(1)}, u32[]{:S(2)}, u32[]{:S(2)}) collective-permute-start(bf16[32,128]{1,0:T(8,128)(2,1)S(1)} %slice.3), channel_id=1, source_target_pairs={{0,1},{1,2},{2,3},{3,4},{4,5},{5,6},{6,7},{8,9},{9,10},{10,11},{11... | collective-permute-start | bytes 24584 | tf_op jit(solution)/shard_map/ppermute | solution.py:269
  10.2 1.5 %copy.7 = bf16[4,8,128,128]{3,2,1,0:T(8,128)(2,1)S(1)} copy(bf16[4,8,128,128]{3,1,2,0:T(8,128)(2,1)} %bitcast.14) | data formatting | bytes 2097152
  11.7 0.9 copy-done
  12.6 0.7 copy-done.1
  13.3 3.6 %shard_map.64 = bf16[32,8,128]{2,1,0:T(8,128)(2,1)S(1)} custom-call(s32[1]{0:T(128)S(6)} %copy.8.taps_used, s32[1]{0:T(128)S(6)} %copy.9.start, s32[1]{0:T(128)} %bitcast.3.window, f32[1,128]{1,0:T(1,128)S(1)} %bitcast.13, bf16[32,128,128]{2,1,0:T(8,128)(2,1)S(1)} %bitcast.12, bf16[32,128]{1,0:T(8,128)(2,1)S(1)} %collective-permute-done.tail, ...), custom_call_target="tpu_custom_call" | custom-call | tf_op jit(solution)/shard_map/pallas_call | solution.py:270
  16.9 13.4 %all_to_all.20.every = bf16[32,8,128]{2,1,0:T(8,128)(2,1)} all-to-all(bf16[32,8,128]{2,1,0:T(8,128)(2,1)S(1)} %shard_map.64), channel_id=1, replica_groups=mesh['chan'=32,'win'=8] {'chan'}, dimensions={0} | all-to-all | bytes 131072 | tf_op jit(solution)/shard_map/all_to_all | solution.py:286
  30.3 1.5 %shard_map.65 = bf16[32,8,128]{2,1,0:T(8,128)(2,1)} custom-call(s32[32]{0:T(128)} %blocks.1, bf16[32,8,128]{2,1,0:T(8,128)(2,1)} %all_to_all.20.every), custom_call_target="tpu_custom_call" | custom-call | tf_op jit(solution)/shard_map/pallas_call | solution.py:287
  31.8 18.9 %all_to_all.21 = bf16[8,4,8,128]{3,2,1,0:T(8,128)(2,1)S(1)} all-to-all(bf16[8,4,8,128]{3,2,1,0:T(8,128)(2,1)} %bitcast.15), channel_id=1, replica_groups=mesh['chan'=32,'win'=8] {'win'}, dimensions={0} | all-to-all | bytes 131072 | tf_op jit(solution)/shard_map/all_to_all | solution.py:293
  50.7 5.0 %all-to-all-start.2 = ((bf16[32,8,128]{2,1,0:T(8,128)(2,1)}), bf16[32,8,128]{2,1,0:T(8,128)(2,1)S(1)}, u32[]{:S(2)}, u32[]{:S(2)}) async-start(bf16[32,8,128]{2,1,0:T(8,128)(2,1)} %shard_map.65), calls=%async_computation.2 | async-start | bytes 131072 | tf_op jit(solution)/shard_map/all_to_all | solution.py:296
  55.7 1.6 %collective-permute-start.3 = (bf16[8,4,8,128]{3,2,1,0:T(8,128)(2,1)S(1)}, bf16[8,4,8,128]{3,2,1,0:T(8,128)(2,1)S(1)}, u32[]{:S(2)}, u32[]{:S(2)}) collective-permute-start(bf16[8,4,8,128]{3,2,1,0:T(8,128)(2,1)S(1)} %all_to_all.21), channel_id=1, source_target_pairs={{0,192},{8,200},{16,208},{24,216},{32,224},{40,232},{48,240},{56,2... | collective-permute-start | bytes 196616 | tf_op jit(solution)/shard_map/ppermute | solution.py:295
  57.3 1.1 %collective-permute-start.2 = (bf16[8,4,8,128]{3,2,1,0:T(8,128)(2,1)S(1)}, bf16[8,4,8,128]{3,2,1,0:T(8,128)(2,1)S(1)}, u32[]{:S(2)}, u32[]{:S(2)}) collective-permute-start(bf16[8,4,8,128]{3,2,1,0:T(8,128)(2,1)S(1)} %all_to_all.21), channel_id=1, source_target_pairs={{0,128},{8,136},{16,144},{24,152},{32,160},{40,168},{48,176},{56,1... | collective-permute-start | bytes 196616 | tf_op jit(solution)/shard_map/ppermute | solution.py:295
  58.5 1.3 %collective-permute-start.1 = (bf16[8,4,8,128]{3,2,1,0:T(8,128)(2,1)S(1)}, bf16[8,4,8,128]{3,2,1,0:T(8,128)(2,1)S(1)}, u32[]{:S(2)}, u32[]{:S(2)}) collective-permute-start(bf16[8,4,8,128]{3,2,1,0:T(8,128)(2,1)S(1)} %all_to_all.21), channel_id=1, source_target_pairs={{0,64},{8,72},{16,80},{24,88},{32,96},{40,104},{48,112},{56,120},{... | collective-permute-start | bytes 196616 | tf_op jit(solution)/shard_map/ppermute | solution.py:295
  59.7 4.7 %collective-permute-done.3 = bf16[8,4,8,128]{3,2,1,0:T(8,128)(2,1)S(1)} collective-permute-done((bf16[8,4,8,128]{3,2,1,0:T(8,128)(2,1)S(1)}, bf16[8,4,8,128]{3,2,1,0:T(8,128)(2,1)S(1)}, u32[]{:S(2)}, u32[]{:S(2)}) %collective-permute-start.3) | collective-permute-done | bytes 65568 | tf_op jit(solution)/shard_map/ppermute | solution.py:295
  64.7 0.9 broadcast_in_dim.2
  65.6 3.5 %all-to-all-start.3 = ((bf16[8,32,8,128]{3,2,1,0:T(8,128)(2,1)}), bf16[8,32,8,128]{3,2,1,0:T(8,128)(2,1)S(1)}, u32[]{:S(2)}, u32[]{:S(2)}) async-start(bf16[8,32,8,128]{3,2,1,0:T(8,128)(2,1)} %broadcast_in_dim.2), calls=%async_computation.3 | async-start | bytes 1048576 | tf_op jit(solution)/shard_map/all_to_all | solution.py:301
  69.1 2.8 %collective-permute-start.6 = (bf16[4,8,4,8,128]{4,3,2,1,0:T(8,128)(2,1)S(1)}, bf16[4,8,4,8,128]{4,3,2,1,0:T(8,128)(2,1)S(1)}, u32[]{:S(2)}, u32[]{:S(2)}) collective-permute-start(bf16[4,8,4,8,128]{4,3,2,1,0:T(8,128)(2,1)S(1)} %pad_maximum_fusion.refs_0_), channel_id=1, source_target_pairs={{0,48},{8,56},{16,32},{24,40},{32,16},{40,24},{48,0},{56,8},{64,11... | collective-permute-start | bytes 786440 | tf_op jit(solution)/shard_map/ppermute | solution.py:299
  71.9 0.8 collective-permute-start.5
  72.8 0.5 collective-permute-start.4
  73.3 10.3 %collective-permute-done.6.refs_3_ = bf16[4,8,4,8,128]{4,3,2,1,0:T(8,128)(2,1)S(1)} collective-permute-done((bf16[4,8,4,8,128]{4,3,2,1,0:T(8,128)(2,1)S(1)}, bf16[4,8,4,8,128]{4,3,2,1,0:T(8,128)(2,1)S(1)}, u32[]{:S(2)}, u32[]{:S(2)}) %collective-permute-start.6) | collective-permute-done | bytes 262176 | tf_op jit(solution)/shard_map/ppermute | solution.py:299
  83.6 0.5 collective-permute-start.9
  84.3 0.8 collective-permute-done.10.refs_7_
  85.9 2.5 %all-to-all-done.3.refs_8_ = bf16[8,32,8,128]{3,2,1,0:T(8,128)(2,1)S(1)} async-done(((bf16[8,32,8,128]{3,2,1,0:T(8,128)(2,1)}), bf16[8,32,8,128]{3,2,1,0:T(8,128)(2,1)S(1)}, u32[]{:S(2)}, u32[]{:S(2)}) %all-to-all-start.3) | async-done | bytes 524320 | tf_op jit(solution)/shard_map/all_to_all | solution.py:301
  88.4 10.8 %shard_map.66 = bf16[32,128,1024]{2,1,0:T(8,128)(2,1)} custom-call(s32[3]{0:T(128)S(1)} %pad_add_fusion.place, bf16[4,8,4,8,128]{4,3,2,1,0:T(8,128)(2,1)S(1)} %pad_maximum_fusion.refs_0_, bf16[4,8,4,8,128]{4,3,2,1,0:T(8,128)(2,1)S(1)} %collective-permute-done.4.refs_1_, bf16[4,8,4,8,128]{4,3,2,1,0:T(8,128)(2,1)S(1)} %collective-permute-done.5.refs_2_, ...), custom_call_target="tpu_custom_call" | custom-call | tf_op jit(solution)/shard_map/pallas_call | solution.py:245
  (16 shorter events, 1.3 us)
Async XLA Ops:
  0.7 11.0 %collective-permute-start = (bf16[32,128]{1,0:T(8,128)(2,1)S(1)}, bf16[32,128]{1,0:T(8,128)(2,1)S(1)}, u32[]{:S(2)}, u32[]{:S(2)}) collective-permute-start(bf16[32,128]{1,0:T(8,128)(2,1)S(1)} %slice.3), channel_id=1, source_target_pairs={{0,1},{1,2},{2,3},{3,4},{4,5},{5,6},{6,7},{8,9},{9,10},{10,11},{11... | collective-permute-start | bytes 24584 | tf_op jit(solution)/shard_map/ppermute | solution.py:269
  11.7 1.0 copy-start
  12.6 0.7 copy-start.1
  50.7 14.0 %all-to-all-start.2 = ((bf16[32,8,128]{2,1,0:T(8,128)(2,1)}), bf16[32,8,128]{2,1,0:T(8,128)(2,1)S(1)}, u32[]{:S(2)}, u32[]{:S(2)}) async-start(bf16[32,8,128]{2,1,0:T(8,128)(2,1)} %shard_map.65), calls=%async_computation.2 | async-start | bytes 131072 | tf_op jit(solution)/shard_map/all_to_all | solution.py:296
  55.7 8.7 %collective-permute-start.3 = (bf16[8,4,8,128]{3,2,1,0:T(8,128)(2,1)S(1)}, bf16[8,4,8,128]{3,2,1,0:T(8,128)(2,1)S(1)}, u32[]{:S(2)}, u32[]{:S(2)}) collective-permute-start(bf16[8,4,8,128]{3,2,1,0:T(8,128)(2,1)S(1)} %all_to_all.21), channel_id=1, source_target_pairs={{0,192},{8,200},{16,208},{24,216},{32,224},{40,232},{48,240},{56,2... | collective-permute-start | bytes 196616 | tf_op jit(solution)/shard_map/ppermute | solution.py:295
  57.3 7.1 %collective-permute-start.2 = (bf16[8,4,8,128]{3,2,1,0:T(8,128)(2,1)S(1)}, bf16[8,4,8,128]{3,2,1,0:T(8,128)(2,1)S(1)}, u32[]{:S(2)}, u32[]{:S(2)}) collective-permute-start(bf16[8,4,8,128]{3,2,1,0:T(8,128)(2,1)S(1)} %all_to_all.21), channel_id=1, source_target_pairs={{0,128},{8,136},{16,144},{24,152},{32,160},{40,168},{48,176},{56,1... | collective-permute-start | bytes 196616 | tf_op jit(solution)/shard_map/ppermute | solution.py:295
  58.5 6.2 %collective-permute-start.1 = (bf16[8,4,8,128]{3,2,1,0:T(8,128)(2,1)S(1)}, bf16[8,4,8,128]{3,2,1,0:T(8,128)(2,1)S(1)}, u32[]{:S(2)}, u32[]{:S(2)}) collective-permute-start(bf16[8,4,8,128]{3,2,1,0:T(8,128)(2,1)S(1)} %all_to_all.21), channel_id=1, source_target_pairs={{0,64},{8,72},{16,80},{24,88},{32,96},{40,104},{48,112},{56,120},{... | collective-permute-start | bytes 196616 | tf_op jit(solution)/shard_map/ppermute | solution.py:295
  65.6 22.8 %all-to-all-start.3 = ((bf16[8,32,8,128]{3,2,1,0:T(8,128)(2,1)}), bf16[8,32,8,128]{3,2,1,0:T(8,128)(2,1)S(1)}, u32[]{:S(2)}, u32[]{:S(2)}) async-start(bf16[8,32,8,128]{3,2,1,0:T(8,128)(2,1)} %broadcast_in_dim.2), calls=%async_computation.3 | async-start | bytes 1048576 | tf_op jit(solution)/shard_map/all_to_all | solution.py:301
  69.1 14.4 %collective-permute-start.6 = (bf16[4,8,4,8,128]{4,3,2,1,0:T(8,128)(2,1)S(1)}, bf16[4,8,4,8,128]{4,3,2,1,0:T(8,128)(2,1)S(1)}, u32[]{:S(2)}, u32[]{:S(2)}) collective-permute-start(bf16[4,8,4,8,128]{4,3,2,1,0:T(8,128)(2,1)S(1)} %pad_maximum_fusion.refs_0_), channel_id=1, source_target_pairs={{0,48},{8,56},{16,32},{24,40},{32,16},{40,24},{48,0},{56,8},{64,11... | collective-permute-start | bytes 786440 | tf_op jit(solution)/shard_map/ppermute | solution.py:299
  71.9 11.6 %collective-permute-start.5 = (bf16[4,8,4,8,128]{4,3,2,1,0:T(8,128)(2,1)S(1)}, bf16[4,8,4,8,128]{4,3,2,1,0:T(8,128)(2,1)S(1)}, u32[]{:S(2)}, u32[]{:S(2)}) collective-permute-start(bf16[4,8,4,8,128]{4,3,2,1,0:T(8,128)(2,1)S(1)} %pad_maximum_fusion.refs_0_), channel_id=1, source_target_pairs={{0,32},{8,40},{16,48},{24,56},{32,0},{40,8},{48,16},{56,24},{64,96... | collective-permute-start | bytes 786440 | tf_op jit(solution)/shard_map/ppermute | solution.py:299
  72.8 11.4 %collective-permute-start.4 = (bf16[4,8,4,8,128]{4,3,2,1,0:T(8,128)(2,1)S(1)}, bf16[4,8,4,8,128]{4,3,2,1,0:T(8,128)(2,1)S(1)}, u32[]{:S(2)}, u32[]{:S(2)}) collective-permute-start(bf16[4,8,4,8,128]{4,3,2,1,0:T(8,128)(2,1)S(1)} %pad_maximum_fusion.refs_0_), channel_id=1, source_target_pairs={{0,16},{8,24},{16,0},{24,8},{32,48},{40,56},{48,32},{56,40},{64,80... | collective-permute-start | bytes 786440 | tf_op jit(solution)/shard_map/ppermute | solution.py:299
  73.3 11.0 %collective-permute-start.7 = (bf16[4,8,4,8,128]{4,3,2,1,0:T(8,128)(2,1)S(1)}, bf16[4,8,4,8,128]{4,3,2,1,0:T(8,128)(2,1)S(1)}, u32[]{:S(2)}, u32[]{:S(2)}) collective-permute-start(bf16[4,8,4,8,128]{4,3,2,1,0:T(8,128)(2,1)S(1)} %pad_maximum_fusion.refs_0_), channel_id=1, source_target_pairs={{0,8},{8,0},{16,24},{24,16},{32,40},{40,32},{48,56},{56,48},{64,72... | collective-permute-start | bytes 786440 | tf_op jit(solution)/shard_map/ppermute | solution.py:300
  83.6 1.5 %collective-permute-start.10 = (bf16[4,8,4,8,128]{4,3,2,1,0:T(8,128)(2,1)S(1)}, bf16[4,8,4,8,128]{4,3,2,1,0:T(8,128)(2,1)S(1)}, u32[]{:S(2)}, u32[]{:S(2)}) collective-permute-start(bf16[4,8,4,8,128]{4,3,2,1,0:T(8,128)(2,1)S(1)} %collective-permute-done.6.refs_3_), channel_id=1, source_target_pairs={{0,8},{8,0},{16,24},{24,16},{32,40},{40,32},{48,56},{56,48},{64,72... | collective-permute-start | bytes 786440 | tf_op jit(solution)/shard_map/ppermute | solution.py:300
  83.6 1.9 %collective-permute-start.9 = (bf16[4,8,4,8,128]{4,3,2,1,0:T(8,128)(2,1)S(1)}, bf16[4,8,4,8,128]{4,3,2,1,0:T(8,128)(2,1)S(1)}, u32[]{:S(2)}, u32[]{:S(2)}) collective-permute-start(bf16[4,8,4,8,128]{4,3,2,1,0:T(8,128)(2,1)S(1)} %collective-permute-done.5.refs_2_), channel_id=1, source_target_pairs={{0,8},{8,0},{16,24},{24,16},{32,40},{40,32},{48,56},{56,48},{64,72... | collective-permute-start | bytes 786440 | tf_op jit(solution)/shard_map/ppermute | solution.py:300
  84.2 1.7 %collective-permute-start.8 = (bf16[4,8,4,8,128]{4,3,2,1,0:T(8,128)(2,1)S(1)}, bf16[4,8,4,8,128]{4,3,2,1,0:T(8,128)(2,1)S(1)}, u32[]{:S(2)}, u32[]{:S(2)}) collective-permute-start(bf16[4,8,4,8,128]{4,3,2,1,0:T(8,128)(2,1)S(1)} %collective-permute-done.4.refs_1_), channel_id=1, source_target_pairs={{0,8},{8,0},{16,24},{24,16},{32,40},{40,32},{48,56},{56,48},{64,72... | collective-permute-start | bytes 786440 | tf_op jit(solution)/shard_map/ppermute | solution.py:300

commit v4 on v3

--- a/solution.py
+++ b/solution.py
@@ -108,9 +108,19 @@
                 out[z * 8 + quarter * 2 + o] = piece.astype(BF16)
 
 
-def order_kernel(blocks, every, out):
+def pack_kernel(blocks, every, out):
     for i in range(COUNT):
-        out[i] = every[blocks[i]]
+        block = every[blocks[i]]
+        for z in range(4):
+            out[z * WINDOWS + i // 4, i % 4] = block
+        for j in range(WINDOWS):
+            out[i // 8 * WINDOWS + j, 4 + i % 8] = block
+
+
+def turn_kernel(got, out):
+    for i in range(COUNT):
+        for r in range(8):
+            out[r, i] = got[i, 4 + r]
 
 
 M_STEP = 8
@@ -126,7 +136,7 @@
     count = len(parts)
     mine, theirs, rows = refs[:count], refs[count : 2 * count], refs[2 * count]
     out, left, coef, mixed, stage, done = refs[-6:]
-    x, z, core = place[0], place[1], place[2]
+    x, core = place[0], place[1]
     spot = lax.broadcasted_iota(jnp.int32, (8, FACTOR), 1) // WIDTH
     bits = [(spot & (1 << s)) != 0 for s in range(3)]
     inner = lax.broadcasted_iota(jnp.int32, (WIDTH, FACTOR), 0)
@@ -137,11 +147,11 @@
         for pair in range(2):
             tiles = []
             for half in range(2):
-                d = z ^ (2 * pair + half)
+                d = 2 * pair + half
                 whole = [[], []]
                 for w in range(WINDOWS):
-                    a = mine[part][d, w, b].astype(F32)
-                    t = theirs[part][d, w, b].astype(F32)
+                    a = mine[part][d * WINDOWS + w, b].astype(F32)
+                    t = theirs[part][d * WINDOWS + w, b].astype(F32)
                     whole[0].append(jnp.where(core == 0, a, t))
                     whole[1].append(jnp.where(core == 0, t, a))
                 tiles.append([spiral(whole[i], bits) for i in range(2)])
@@ -161,12 +171,13 @@
             turn = jnp.where(part == i, parts[i], turn)
         return x ^ turn
 
-    def multiply(step, slot):
+    def prepare(step, slot):
         part = lax.shift_right_logical(step, 2)
-        at = (step & 3) * 8 + chunk_of(part) * 2
+        at = chunk_of(part) * 2
+        z = step & 3
         for w in range(WINDOWS):
             for i in range(2):
-                u = rows[w, at + i].astype(F32)
+                u = rows[at + i, z * WINDOWS + w].astype(F32)
                 if w:
                     u = pltpu.roll(u, FACTOR - WIDTH * w, 1)
                 u = pltpu.roll(u, 0, 1, stride=WIDTH, stride_axis=0)
@@ -175,6 +186,9 @@
                 coef[slot, w, i] = u
                 if i == 0:
                     coef[slot, w, 2] = -u
+
+    def multiply(step, slot):
+        part = lax.shift_right_logical(step, 2)
         for g in range(GROUPS):
             blocks = [
                 [
@@ -211,6 +225,8 @@
                     stage[target, o, m, 16 * t : 16 * t + 16, :] = jnp.concatenate(pair, axis=0).astype(BF16)
 
     steps = count * (COUNT // M_STEP)
+    prepare(jnp.int32(0), 0)
+    prepare(jnp.int32(1), 1)
     multiply(jnp.int32(0), 0)
 
     def both(i, carry):
@@ -222,6 +238,7 @@
                 for copy in copies(step - SLOTS):
                     copy.wait()
 
+            prepare(jnp.minimum(step + 2, steps - 1), slot)
             multiply(jnp.minimum(step + 1, steps - 1), 1 - slot)
             spread(slot, step)
             for copy in copies(step):
@@ -259,14 +276,12 @@
     )(*args)
 
 
-def chan_swap(dz, dx, dc):
-    spots = [(z, x, c) for z in range(4) for x in range(4) for c in range(2)]
-    at = lambda z, x, c: z * 8 + x * 2 + c
-    return [(at(z, x, c), at(z ^ dz, x ^ dx, c ^ dc)) for z, x, c in spots]
+CHAN = ("z", "x", "c")
+WIN = ("y", "h")
 
 
 def shards(samples, fir_taps, tap_counts, band_start, grid_blocks):
-    tail = lax.ppermute(samples[:, -FACTOR:], "win", [(i, i + 1) for i in range(WINDOWS - 1)])
+    tail = lax.ppermute(samples[:, -FACTOR:], WIN, [(i, i + 1) for i in range(WINDOWS - 1)])
     pieces = pl.pallas_call(
         front_kernel,
         in_specs=[SMEM, SMEM, SMEM, VMEM, VMEM, VMEM, VMEM],
@@ -277,37 +292,37 @@
     )(
         tap_counts,
         band_start,
-        lax.axis_index("win").reshape(1),
+        lax.axis_index(WIN).reshape(1),
         fir_taps.reshape(1, FACTOR),
         samples.reshape(COUNT, FACTOR, FACTOR),
         tail,
         tables(),
     )
-    every = lax.all_to_all(pieces, "chan", 0, 0, tiled=True)
-    ordered = pl.pallas_call(
-        order_kernel,
+    every = lax.all_to_all(pieces, CHAN, 0, 0, tiled=True)
+    sent = pl.pallas_call(
+        pack_kernel,
         in_specs=[SMEM, VMEM],
         out_specs=VMEM,
-        out_shape=jax.ShapeDtypeStruct((COUNT, 8, FACTOR), BF16),
+        out_shape=jax.ShapeDtypeStruct((COUNT, 12, 8, FACTOR), BF16),
     )(grid_blocks, every)
-    cols = lax.all_to_all(ordered.reshape(WINDOWS, 4, 8, FACTOR), "win", 0, 0, tiled=True)
-    ordered, cols = lax.optimization_barrier((ordered, cols))
-    near = [lax.ppermute(cols, "chan", chan_swap(d, 0, 0)) for d in (1, 2, 3)]
-    rows = lax.all_to_all(ordered, "chan", 0, 0, tiled=True)
-    rows, near = lax.optimization_barrier((rows, near))
-    mine = [jnp.stack([cols] + near)]
-    mine += [lax.ppermute(mine[0], "chan", chan_swap(0, d, 0)) for d in (1, 2, 3)]
-    theirs = [lax.ppermute(this, "chan", chan_swap(0, 0, 1)) for this in mine]
-    rows = lax.all_to_all(
-        jnp.broadcast_to(rows[None], (WINDOWS, COUNT, 8, FACTOR)), "win", 0, 0, tiled=True
+    got = lax.all_to_all(sent, ("z", *WIN), 0, 0, tiled=True)
+    mine = [got[:, :4]]
+    mine += [lax.ppermute(mine[0], "x", [(i, i ^ d) for i in range(4)]) for d in (1, 2, 3)]
+    theirs = [lax.ppermute(this, "c", [(0, 1), (1, 0)]) for this in mine]
+    rows = pl.pallas_call(
+        turn_kernel,
+        in_specs=[VMEM],
+        out_specs=VMEM,
+        out_shape=jax.ShapeDtypeStruct((8, COUNT, 8, FACTOR), BF16),
+    )(got)
+    rows = lax.all_to_all(rows, ("x", "c"), 0, 0, tiled=True)
+    place = jnp.stack([lax.axis_index("x"), lax.axis_index("c")]).astype(jnp.int32)
+    return cross((0, 1, 2, 3), place, mine, theirs, rows, None)
+
+
+def solution(mesh):
+    fine = jax.sharding.Mesh(mesh.devices.reshape(4, 4, 2, 4, 2), (*CHAN, *WIN))
+    placed = (P(CHAN, WIN), P(), P(WIN), P(), P())
+    return jax.shard_map(
+        shards, mesh=fine, in_specs=placed, out_specs=P(CHAN, WIN, None), check_vma=False
     )
-    here = lax.axis_index("chan")
-    place = jnp.stack([(here // 2) % 4, here // 8, here % 2]).astype(jnp.int32)
-    return cross((0, 1, 2, 3), place, mine, theirs, rows, None)
-
-
-def solution(mesh):
-    placed = (P("chan", "win"), P(), P("win"), P(), P())
-    return jax.shard_map(
-        shards, mesh=mesh, in_specs=placed, out_specs=P("chan", "win", None), check_vma=False
-    )

time: 101 us -> 96.3 us (0.953); the launches traced: 99.1 us -> 95.8 us
  blocking collectives: 32.3 us -> 47.6 us
  waiting for transfers between devices: 19.5 us -> 10.6 us
  starting transfers between devices: 25.4 us -> 16.8 us
    all_to_all x2, blocking collectives: 32.3 us -> 47.6 us  [the longest x1 34.2 us: shards(): got = lax.all_to_all(sent, ('z', *WIN), 0, 0, tiled=True)]
    ppermute x11 -> x8, waiting for transfers between devices: 16.9 us -> 6.39 us  [the longest x3 6.38 us: shards(): lax.ppermute(mine[0], 'x', [(i, i ^ d) for i in range(4)])]
    all_to_all x2 -> x1, starting transfers between devices: 8.47 us -> 3.49 us  [shards(): rows = lax.all_to_all(rows, ('x', 'c'), 0, 0, tiled=True)]
    ppermute x11 -> x8, starting transfers between devices: 16.9 us -> 13.3 us  [the longest x1 8.18 us: shards(): lax.ppermute(samples[:, -FACTOR:], WIN, [(i, i + 1) for i in range(WINDOW...]
    pallas_call x1, Pallas kernels: 10.8 us -> 8.06 us  [cross(): pl.pallas_call(functools.partial(cross_kernel, parts), in_specs=specs, ou...]
    pallas_call x1 -> x2, Pallas kernels: 1.5 us -> 3.87 us  [the longest x1 2.03 us: shards(): pl.pallas_call(turn_kernel, in_specs=[VMEM], out_specs=VMEM, out_shape=ja...]
    all_to_all x2 -> x1, waiting for transfers between devices: 2.53 us -> 4.24 us  [shards(): rows = lax.all_to_all(rows, ('x', 'c'), 0, 0, tiled=True)]
    unnamed x5 -> x7, local copies, waits for them, and re-layouts: 3.07 us -> 3.07 us
  transfers between devices with their start and end apart: 13 -> 9, of which waited for: 8 -> 3; matrix products, arithmetic and copies ran while one was open for 2% -> 2% of each run, Pallas kernels for 0% -> 2%
where the time goes in v4:
time: 96.3 us; the launch traced here: 95.8 us
  blocking collectives  47.6 us (49%)
  starting transfers between devices  16.8 us (17%)
  Pallas kernels  15.5 us (16%)
  waiting for transfers between devices  10.6 us (11%)
  local copies, waits for them, and re-layouts  3.79 us (4%)
  between operations  1.38 us (1%)
    all_to_all x1, blocking collectives, shards(): got = lax.all_to_all(sent, ('z', *WIN), 0, 0, tiled=True)  34.2 us
    all_to_all x1, blocking collectives, shards(): every = lax.all_to_all(pieces, CHAN, 0, 0, tiled=True)  13.4 us
    ppermute x1, starting transfers between devices, shards(): lax.ppermute(samples[:, -FACTOR:], WIN, [(i, i + 1) for i in range(WINDOW...  8.18 us
    pallas_call x1, Pallas kernels, cross(): pl.pallas_call(functools.partial(cross_kernel, parts), in_specs=specs, ou...  8.06 us
    ppermute x3, waiting for transfers between devices, shards(): lax.ppermute(mine[0], 'x', [(i, i ^ d) for i in range(4)])  6.38 us
    all_to_all x1, waiting for transfers between devices, shards(): rows = lax.all_to_all(rows, ('x', 'c'), 0, 0, tiled=True)  4.24 us
    ppermute x3, starting transfers between devices, shards(): lax.ppermute(mine[0], 'x', [(i, i ^ d) for i in range(4)])  4.18 us
    pallas_call x1, Pallas kernels, shards(): pl.pallas_call(front_kernel, in_specs=[SMEM, SMEM, SMEM, VMEM, VMEM, VMEM...  3.59 us
  transfers between devices with their start and end apart: 9, of which 3 were waited for; matrix products, arithmetic and copies ran while one was open for 2% of the time, Pallas kernels for 2%

profile of v4, /device:TPU:32, one launch (start us, length us, event | category | flops | bytes accessed | tf_op | source)
XLA Modules:
  0.0 95.8 jit_solution(1128605075552165678)
XLA Ops:
  0.0 0.7 slice.6
  0.7 8.2 %collective-permute-start = (bf16[32,128]{1,0:T(8,128)(2,1)S(1)}, bf16[32,128]{1,0:T(8,128)(2,1)S(1)}, u32[]{:S(2)}, u32[]{:S(2)}) collective-permute-start(bf16[32,128]{1,0:T(8,128)(2,1)S(1)} %slice.6), channel_id=1, source_target_pairs={{0,1},{1,2},{2,3},{3,4},{4,5},{5,6},{6,7},{8,9},{9,10},{10,11},{11... | collective-permute-start | bytes 24584 | tf_op jit(solution)/shard_map/ppermute | solution.py:284
  10.2 1.5 %copy.7 = bf16[4,8,128,128]{3,2,1,0:T(8,128)(2,1)S(1)} copy(bf16[4,8,128,128]{3,1,2,0:T(8,128)(2,1)} %bitcast.8) | data formatting | bytes 2097152
  11.7 0.0 collective-permute-done.tail
  11.7 0.0 copy-start
  11.7 0.9 copy-done
  12.6 0.7 copy-done.1
  13.3 3.6 %shard_map.64 = bf16[32,8,128]{2,1,0:T(8,128)(2,1)S(1)} custom-call(s32[1]{0:T(128)S(6)} %copy.8.taps_used, s32[1]{0:T(128)S(6)} %copy.9.start, s32[1]{0:T(128)} %bitcast.2.window, f32[1,128]{1,0:T(1,128)S(1)} %bitcast.7, bf16[32,128,128]{2,1,0:T(8,128)(2,1)S(1)} %bitcast.6, bf16[32,128]{1,0:T(8,128)(2,1)S(1)} %collective-permute-done.tail, ...), custom_call_target="tpu_custom_call" | custom-call | tf_op jit(solution)/shard_map/pallas_call | solution.py:285
  16.9 13.4 %all_to_all.15.every = bf16[32,8,128]{2,1,0:T(8,128)(2,1)} all-to-all(bf16[32,8,128]{2,1,0:T(8,128)(2,1)S(1)} %shard_map.64), channel_id=1, replica_groups=mesh['z'=4,'x'=4,'c'=2,'y'=4,'h'=2] {'z','x','c'}, dimensions={0} | all-to-all | bytes 131072 | tf_op jit(solution)/shard_map/all_to_all | solution.py:301
  30.3 1.8 %shard_map.65 = bf16[32,12,8,128]{3,2,1,0:T(8,128)(2,1)} custom-call(s32[32]{0:T(128)} %blocks.1, bf16[32,8,128]{2,1,0:T(8,128)(2,1)} %all_to_all.15.every), custom_call_target="tpu_custom_call" | custom-call | tf_op jit(solution)/shard_map/pallas_call | solution.py:302
  32.2 34.2 %all_to_all.16.got = bf16[32,12,8,128]{3,2,1,0:T(8,128)(2,1)S(1)} all-to-all(bf16[32,12,8,128]{3,2,1,0:T(8,128)(2,1)} %shard_map.65), channel_id=1, replica_groups=mesh['z'=4,'x'=4,'c'=2,'y'=4,'h'=2] {'z','y','h'}, dimensions={0} | all-to-all | bytes 1572864 | tf_op jit(solution)/shard_map/all_to_all | solution.py:308
  66.4 1.3 %collective-permute-start.3 = (bf16[32,4,8,128]{3,2,1,0:T(8,128)(2,1)S(1)}, bf16[32,4,8,128]{3,2,1,0:T(8,128)(2,1)S(1)}, u32[]{:S(2)}, u32[]{:S(2)}) collective-permute-start(bf16[32,4,8,128]{3,2,1,0:T(8,128)(2,1)S(1)} %slice.8.refs_0_), channel_id=1, source_target_pairs={{0,48},{16,32},{32,16},{48,0},{1,49},{17,33},{33,17},{49,1},{2,50}... | collective-permute-start | bytes 786440 | tf_op jit(solution)/shard_map/ppermute | solution.py:310
  67.7 1.4 %collective-permute-start.2 = (bf16[32,4,8,128]{3,2,1,0:T(8,128)(2,1)S(1)}, bf16[32,4,8,128]{3,2,1,0:T(8,128)(2,1)S(1)}, u32[]{:S(2)}, u32[]{:S(2)}) collective-permute-start(bf16[32,4,8,128]{3,2,1,0:T(8,128)(2,1)S(1)} %slice.8.refs_0_), channel_id=1, source_target_pairs={{0,32},{16,48},{32,0},{48,16},{1,33},{17,49},{33,1},{49,17},{2,34}... | collective-permute-start | bytes 786440 | tf_op jit(solution)/shard_map/ppermute | solution.py:310
  69.1 1.5 %collective-permute-start.1 = (bf16[32,4,8,128]{3,2,1,0:T(8,128)(2,1)S(1)}, bf16[32,4,8,128]{3,2,1,0:T(8,128)(2,1)S(1)}, u32[]{:S(2)}, u32[]{:S(2)}) collective-permute-start(bf16[32,4,8,128]{3,2,1,0:T(8,128)(2,1)S(1)} %slice.8.refs_0_), channel_id=1, source_target_pairs={{0,16},{16,0},{32,48},{48,32},{1,17},{17,1},{33,49},{49,33},{2,18}... | collective-permute-start | bytes 786440 | tf_op jit(solution)/shard_map/ppermute | solution.py:310
  70.6 2.0 %shard_map.66 = bf16[8,32,8,128]{3,2,1,0:T(8,128)(2,1)} custom-call(bf16[32,12,8,128]{3,2,1,0:T(8,128)(2,1)} %copy-done.2), custom_call_target="tpu_custom_call" | custom-call | tf_op jit(solution)/shard_map/pallas_call | solution.py:312
  72.6 3.5 %all-to-all-start.2 = ((bf16[8,32,8,128]{3,2,1,0:T(8,128)(2,1)}), bf16[8,32,8,128]{3,2,1,0:T(8,128)(2,1)S(1)}, u32[]{:S(2)}, u32[]{:S(2)}) async-start(bf16[8,32,8,128]{3,2,1,0:T(8,128)(2,1)} %shard_map.66), calls=%async_computation.2 | async-start | bytes 1048576 | tf_op jit(solution)/shard_map/all_to_all | solution.py:318
  76.1 0.4 collective-permute-start.4
  76.5 5.0 %collective-permute-done.3.refs_3_ = bf16[32,4,8,128]{3,2,1,0:T(8,128)(2,1)S(1)} collective-permute-done((bf16[32,4,8,128]{3,2,1,0:T(8,128)(2,1)S(1)}, bf16[32,4,8,128]{3,2,1,0:T(8,128)(2,1)S(1)}, u32[]{:S(2)}, u32[]{:S(2)}) %collective-permute-start.3) | collective-permute-done | bytes 262176 | tf_op jit(solution)/shard_map/ppermute | solution.py:310
  81.5 0.0 collective-permute-start.7
  81.5 0.5 collective-permute-start.6
  82.0 1.4 %collective-permute-done.1.refs_1_ = bf16[32,4,8,128]{3,2,1,0:T(8,128)(2,1)S(1)} collective-permute-done((bf16[32,4,8,128]{3,2,1,0:T(8,128)(2,1)S(1)}, bf16[32,4,8,128]{3,2,1,0:T(8,128)(2,1)S(1)}, u32[]{:S(2)}, u32[]{:S(2)}) %collective-permute-start.1) | collective-permute-done | bytes 262176 | tf_op jit(solution)/shard_map/ppermute | solution.py:310
  83.4 0.1 pad_add_fusion.place
  83.5 4.2 %all-to-all-done.2.refs_8_ = bf16[8,32,8,128]{3,2,1,0:T(8,128)(2,1)S(1)} async-done(((bf16[8,32,8,128]{3,2,1,0:T(8,128)(2,1)}), bf16[8,32,8,128]{3,2,1,0:T(8,128)(2,1)S(1)}, u32[]{:S(2)}, u32[]{:S(2)}) %all-to-all-start.2) | async-done | bytes 524320 | tf_op jit(solution)/shard_map/all_to_all | solution.py:318
  87.7 8.1 %shard_map.67 = bf16[32,128,1024]{2,1,0:T(8,128)(2,1)} custom-call(s32[2]{0:T(128)S(1)} %pad_add_fusion.place, bf16[32,4,8,128]{3,2,1,0:T(8,128)(2,1)S(1)} %slice.8.refs_0_, bf16[32,4,8,128]{3,2,1,0:T(8,128)(2,1)S(1)} %collective-permute-done.1.refs_1_, bf16[32,4,8,128]{3,2,1,0:T(8,128)(2,1)S(1)} %collective-permute-done.2.refs_2_, ...), custom_call_target="tpu_custom_call" | custom-call | tf_op jit(solution)/shard_map/pallas_call | solution.py:262
  (10 shorter events, 0.0 us)
Async XLA Ops:
  0.7 11.0 %collective-permute-start = (bf16[32,128]{1,0:T(8,128)(2,1)S(1)}, bf16[32,128]{1,0:T(8,128)(2,1)S(1)}, u32[]{:S(2)}, u32[]{:S(2)}) collective-permute-start(bf16[32,128]{1,0:T(8,128)(2,1)S(1)} %slice.6), channel_id=1, source_target_pairs={{0,1},{1,2},{2,3},{3,4},{4,5},{5,6},{6,7},{8,9},{9,10},{10,11},{11... | collective-permute-start | bytes 24584 | tf_op jit(solution)/shard_map/ppermute | solution.py:284
  11.7 1.0 copy-start
  12.6 0.7 copy-start.1
  66.4 4.2 %copy-start.2 = (bf16[32,12,8,128]{3,2,1,0:T(8,128)(2,1)}, bf16[32,12,8,128]{3,2,1,0:T(8,128)(2,1)S(1)}, u32[]{:S(2)}) copy-start(bf16[32,12,8,128]{3,2,1,0:T(8,128)(2,1)S(1)} %all_to_all.16.got) | copy-start | bytes 2359300
  66.4 15.1 %collective-permute-start.3 = (bf16[32,4,8,128]{3,2,1,0:T(8,128)(2,1)S(1)}, bf16[32,4,8,128]{3,2,1,0:T(8,128)(2,1)S(1)}, u32[]{:S(2)}, u32[]{:S(2)}) collective-permute-start(bf16[32,4,8,128]{3,2,1,0:T(8,128)(2,1)S(1)} %slice.8.refs_0_), channel_id=1, source_target_pairs={{0,48},{16,32},{32,16},{48,0},{1,49},{17,33},{33,17},{49,1},{2,50}... | collective-permute-start | bytes 786440 | tf_op jit(solution)/shard_map/ppermute | solution.py:310
  67.7 13.8 %collective-permute-start.2 = (bf16[32,4,8,128]{3,2,1,0:T(8,128)(2,1)S(1)}, bf16[32,4,8,128]{3,2,1,0:T(8,128)(2,1)S(1)}, u32[]{:S(2)}, u32[]{:S(2)}) collective-permute-start(bf16[32,4,8,128]{3,2,1,0:T(8,128)(2,1)S(1)} %slice.8.refs_0_), channel_id=1, source_target_pairs={{0,32},{16,48},{32,0},{48,16},{1,33},{17,49},{33,1},{49,17},{2,34}... | collective-permute-start | bytes 786440 | tf_op jit(solution)/shard_map/ppermute | solution.py:310
  69.1 14.3 %collective-permute-start.1 = (bf16[32,4,8,128]{3,2,1,0:T(8,128)(2,1)S(1)}, bf16[32,4,8,128]{3,2,1,0:T(8,128)(2,1)S(1)}, u32[]{:S(2)}, u32[]{:S(2)}) collective-permute-start(bf16[32,4,8,128]{3,2,1,0:T(8,128)(2,1)S(1)} %slice.8.refs_0_), channel_id=1, source_target_pairs={{0,16},{16,0},{32,48},{48,32},{1,17},{17,1},{33,49},{49,33},{2,18}... | collective-permute-start | bytes 786440 | tf_op jit(solution)/shard_map/ppermute | solution.py:310
  72.6 15.1 %all-to-all-start.2 = ((bf16[8,32,8,128]{3,2,1,0:T(8,128)(2,1)}), bf16[8,32,8,128]{3,2,1,0:T(8,128)(2,1)S(1)}, u32[]{:S(2)}, u32[]{:S(2)}) async-start(bf16[8,32,8,128]{3,2,1,0:T(8,128)(2,1)} %shard_map.66), calls=%async_computation.2 | async-start | bytes 1048576 | tf_op jit(solution)/shard_map/all_to_all | solution.py:318
  76.1 7.4 %collective-permute-start.4 = (bf16[32,4,8,128]{3,2,1,0:T(8,128)(2,1)S(1)}, bf16[32,4,8,128]{3,2,1,0:T(8,128)(2,1)S(1)}, u32[]{:S(2)}, u32[]{:S(2)}) collective-permute-start(bf16[32,4,8,128]{3,2,1,0:T(8,128)(2,1)S(1)} %slice.8.refs_0_), channel_id=1, source_target_pairs={{0,8},{8,0},{1,9},{9,1},{2,10},{10,2},{3,11},{11,3},{4,12},{12,4},... | collective-permute-start | bytes 786440 | tf_op jit(solution)/shard_map/ppermute | solution.py:311
  81.5 6.3 %collective-permute-start.7 = (bf16[32,4,8,128]{3,2,1,0:T(8,128)(2,1)S(1)}, bf16[32,4,8,128]{3,2,1,0:T(8,128)(2,1)S(1)}, u32[]{:S(2)}, u32[]{:S(2)}) collective-permute-start(bf16[32,4,8,128]{3,2,1,0:T(8,128)(2,1)S(1)} %collective-permute-done.3.refs_3_), channel_id=1, source_target_pairs={{0,8},{8,0},{1,9},{9,1},{2,10},{10,2},{3,11},{11,3},{4,12},{12,4},... | collective-permute-start | bytes 786440 | tf_op jit(solution)/shard_map/ppermute | solution.py:311
  81.5 6.3 %collective-permute-start.6 = (bf16[32,4,8,128]{3,2,1,0:T(8,128)(2,1)S(1)}, bf16[32,4,8,128]{3,2,1,0:T(8,128)(2,1)S(1)}, u32[]{:S(2)}, u32[]{:S(2)}) collective-permute-start(bf16[32,4,8,128]{3,2,1,0:T(8,128)(2,1)S(1)} %collective-permute-done.2.refs_2_), channel_id=1, source_target_pairs={{0,8},{8,0},{1,9},{9,1},{2,10},{10,2},{3,11},{11,3},{4,12},{12,4},... | collective-permute-start | bytes 786440 | tf_op jit(solution)/shard_map/ppermute | solution.py:311
  83.4 4.3 %collective-permute-start.5 = (bf16[32,4,8,128]{3,2,1,0:T(8,128)(2,1)S(1)}, bf16[32,4,8,128]{3,2,1,0:T(8,128)(2,1)S(1)}, u32[]{:S(2)}, u32[]{:S(2)}) collective-permute-start(bf16[32,4,8,128]{3,2,1,0:T(8,128)(2,1)S(1)} %collective-permute-done.1.refs_1_), channel_id=1, source_target_pairs={{0,8},{8,0},{1,9},{9,1},{2,10},{10,2},{3,11},{11,3},{4,12},{12,4},... | collective-permute-start | bytes 786440 | tf_op jit(solution)/shard_map/ppermute | solution.py:311

commit v5 on v4

--- a/solution.py
+++ b/solution.py
@@ -21,6 +21,7 @@
 WIDTH = FACTOR // GROUPS
 SLOTS = 4
 LIMIT = 48 * 1024 * 1024
+SMALL = pltpu.CompilerParams(vmem_limit_bytes=8 * 1024 * 1024)
 
 VMEM = pl.BlockSpec(memory_space=pltpu.VMEM)
 SMEM = pl.BlockSpec(memory_space=pltpu.SMEM)
@@ -132,11 +133,11 @@
     return parts
 
 
-def cross_kernel(parts, place, *refs):
+def cross_kernel(parts, chunk_at, core_at, *refs):
     count = len(parts)
     mine, theirs, rows = refs[:count], refs[count : 2 * count], refs[2 * count]
     out, left, coef, mixed, stage, done = refs[-6:]
-    x, core = place[0], place[1]
+    x, core = chunk_at[0], core_at[0]
     spot = lax.broadcasted_iota(jnp.int32, (8, FACTOR), 1) // WIDTH
     bits = [(spot & (1 << s)) != 0 for s in range(3)]
     inner = lax.broadcasted_iota(jnp.int32, (WIDTH, FACTOR), 0)
@@ -251,9 +252,9 @@
             copy.wait()
 
 
-def cross(parts, place, mine, theirs, rows, before):
-    args = [place, *mine, *theirs, rows]
-    specs = [SMEM] + [VMEM] * (len(args) - 1)
+def cross(parts, chunk_at, core_at, mine, theirs, rows, before):
+    args = [chunk_at, core_at, *mine, *theirs, rows]
+    specs = [SMEM] * 2 + [VMEM] * (len(args) - 2)
     aliases = {}
     if before is not None:
         aliases = {len(args): 0}
@@ -304,6 +305,7 @@
         in_specs=[SMEM, VMEM],
         out_specs=VMEM,
         out_shape=jax.ShapeDtypeStruct((COUNT, 12, 8, FACTOR), BF16),
+        compiler_params=SMALL,
     )(grid_blocks, every)
     got = lax.all_to_all(sent, ("z", *WIN), 0, 0, tiled=True)
     mine = [got[:, :4]]
@@ -314,10 +316,11 @@
         in_specs=[VMEM],
         out_specs=VMEM,
         out_shape=jax.ShapeDtypeStruct((8, COUNT, 8, FACTOR), BF16),
+        compiler_params=SMALL,
     )(got)
     rows = lax.all_to_all(rows, ("x", "c"), 0, 0, tiled=True)
-    place = jnp.stack([lax.axis_index("x"), lax.axis_index("c")]).astype(jnp.int32)
-    return cross((0, 1, 2, 3), place, mine, theirs, rows, None)
+    chunk_at, core_at = lax.axis_index("x").reshape(1), lax.axis_index("c").reshape(1)
+    return cross((0, 1, 2, 3), chunk_at, core_at, mine, theirs, rows, None)
 
 
 def solution(mesh):

time: 96.3 us -> 94.8 us (0.984)
  Pallas kernels: 15.5 us -> 12.6 us
  waiting for transfers between devices: 10.6 us -> 11.8 us
    pallas_call x1, Pallas kernels: 1.83 us -> 0.65 us  [shards(): pl.pallas_call(pack_kernel, in_specs=[SMEM, VMEM], out_specs=VMEM, out_sh...]
    ppermute x3, waiting for transfers between devices: 6.38 us -> 7.57 us  [shards(): lax.ppermute(mine[0], 'x', [(i, i ^ d) for i in range(4)])]
    pallas_call x1, Pallas kernels: 2.03 us -> 0.89 us  [shards(): pl.pallas_call(turn_kernel, in_specs=[VMEM], out_specs=VMEM, out_shape=ja...]
  transfers between devices with their start and end apart: 9 -> 9, of which waited for: 3 -> 2; matrix products, arithmetic and copies ran while one was open for 2% -> 2% of each run, Pallas kernels for 2% -> 1%
where the time goes in v5:
time: 94.8 us; the launch traced here: 94.4 us
  blocking collectives  47.3 us (50%)
  starting transfers between devices  16.9 us (18%)
  Pallas kernels  12.6 us (13%)
  waiting for transfers between devices  11.8 us (12%)
  local copies, waits for them, and re-layouts  4.44 us (5%)
  between operations  1.38 us (1%)
    all_to_all x1, blocking collectives, shards(): got = lax.all_to_all(sent, ('z', *WIN), 0, 0, tiled=True)  34 us
    all_to_all x1, blocking collectives, shards(): every = lax.all_to_all(pieces, CHAN, 0, 0, tiled=True)  13.3 us
    ppermute x1, starting transfers between devices, shards(): lax.ppermute(samples[:, -FACTOR:], WIN, [(i, i + 1) for i in range(WINDOW...  8.18 us
    ppermute x3, waiting for transfers between devices, shards(): lax.ppermute(mine[0], 'x', [(i, i ^ d) for i in range(4)])  7.57 us
    pallas_call x1, Pallas kernels, cross(): pl.pallas_call(functools.partial(cross_kernel, parts), in_specs=specs, ou...  7.52 us
    all_to_all x1, waiting for transfers between devices, shards(): rows = lax.all_to_all(rows, ('x', 'c'), 0, 0, tiled=True)  4.19 us
    ppermute x3, starting transfers between devices, shards(): lax.ppermute(mine[0], 'x', [(i, i ^ d) for i in range(4)])  4.18 us
    unnamed x7, local copies, waits for them, and re-layouts  3.72 us
  transfers between devices with their start and end apart: 9, of which 2 were waited for; matrix products, arithmetic and copies ran while one was open for 2% of the time, Pallas kernels for 1%

profile of v5, /device:TPU:32, one launch (start us, length us, event | category | flops | bytes accessed | tf_op | source)
XLA Modules:
  0.0 94.4 jit_solution(8615859348154520545)
XLA Ops:
  0.0 0.7 slice.6
  0.7 8.2 %collective-permute-start = (bf16[32,128]{1,0:T(8,128)(2,1)S(1)}, bf16[32,128]{1,0:T(8,128)(2,1)S(1)}, u32[]{:S(2)}, u32[]{:S(2)}) collective-permute-start(bf16[32,128]{1,0:T(8,128)(2,1)S(1)} %slice.6), channel_id=1, source_target_pairs={{0,1},{1,2},{2,3},{3,4},{4,5},{5,6},{6,7},{8,9},{9,10},{10,11},{11... | collective-permute-start | bytes 24584 | tf_op jit(solution)/shard_map/ppermute | solution.py:285
  10.2 1.5 %copy.7 = bf16[4,8,128,128]{3,2,1,0:T(8,128)(2,1)S(1)} copy(bf16[4,8,128,128]{3,1,2,0:T(8,128)(2,1)} %bitcast.8) | data formatting | bytes 2097152
  11.7 0.0 collective-permute-done.tail
  11.7 0.0 copy-start
  11.7 0.9 copy-done
  12.6 0.7 copy-done.1
  13.3 3.6 %shard_map.64 = bf16[32,8,128]{2,1,0:T(8,128)(2,1)S(1)} custom-call(s32[1]{0:T(128)S(6)} %copy.8.taps_used, s32[1]{0:T(128)S(6)} %copy.9.start, s32[1]{0:T(128)} %bitcast.2.window, f32[1,128]{1,0:T(1,128)S(1)} %bitcast.7, bf16[32,128,128]{2,1,0:T(8,128)(2,1)S(1)} %bitcast.6, bf16[32,128]{1,0:T(8,128)(2,1)S(1)} %collective-permute-done.tail, ...), custom_call_target="tpu_custom_call" | custom-call | tf_op jit(solution)/shard_map/pallas_call | solution.py:286
  16.9 13.3 %all_to_all.15.every = bf16[32,8,128]{2,1,0:T(8,128)(2,1)S(1)} all-to-all(bf16[32,8,128]{2,1,0:T(8,128)(2,1)S(1)} %shard_map.64), channel_id=1, replica_groups=mesh['z'=4,'x'=4,'c'=2,'y'=4,'h'=2] {'z','x','c'}, dimensions={0} | all-to-all | bytes 131072 | tf_op jit(solution)/shard_map/all_to_all | solution.py:302
  30.2 0.7 copy-done.2
  30.9 0.6 shard_map.65
  31.5 34.0 %all_to_all.16.got = bf16[32,12,8,128]{3,2,1,0:T(8,128)(2,1)S(1)} all-to-all(bf16[32,12,8,128]{3,2,1,0:T(8,128)(2,1)S(1)} %shard_map.65), channel_id=1, replica_groups=mesh['z'=4,'x'=4,'c'=2,'y'=4,'h'=2] {'z','y','h'}, dimensions={0} | all-to-all | bytes 1572864 | tf_op jit(solution)/shard_map/all_to_all | solution.py:310
  65.5 1.3 %collective-permute-start.3 = (bf16[32,4,8,128]{3,2,1,0:T(8,128)(2,1)S(1)}, bf16[32,4,8,128]{3,2,1,0:T(8,128)(2,1)S(1)}, u32[]{:S(2)}, u32[]{:S(2)}) collective-permute-start(bf16[32,4,8,128]{3,2,1,0:T(8,128)(2,1)S(1)} %slice.8.refs_0_), channel_id=1, source_target_pairs={{0,48},{16,32},{32,16},{48,0},{1,49},{17,33},{33,17},{49,1},{2,50}... | collective-permute-start | bytes 786440 | tf_op jit(solution)/shard_map/ppermute | solution.py:312
  66.8 1.4 %collective-permute-start.2 = (bf16[32,4,8,128]{3,2,1,0:T(8,128)(2,1)S(1)}, bf16[32,4,8,128]{3,2,1,0:T(8,128)(2,1)S(1)}, u32[]{:S(2)}, u32[]{:S(2)}) collective-permute-start(bf16[32,4,8,128]{3,2,1,0:T(8,128)(2,1)S(1)} %slice.8.refs_0_), channel_id=1, source_target_pairs={{0,32},{16,48},{32,0},{48,16},{1,33},{17,49},{33,1},{49,17},{2,34}... | collective-permute-start | bytes 786440 | tf_op jit(solution)/shard_map/ppermute | solution.py:312
  68.3 1.5 %collective-permute-start.1 = (bf16[32,4,8,128]{3,2,1,0:T(8,128)(2,1)S(1)}, bf16[32,4,8,128]{3,2,1,0:T(8,128)(2,1)S(1)}, u32[]{:S(2)}, u32[]{:S(2)}) collective-permute-start(bf16[32,4,8,128]{3,2,1,0:T(8,128)(2,1)S(1)} %slice.8.refs_0_), channel_id=1, source_target_pairs={{0,16},{16,0},{32,48},{48,32},{1,17},{17,1},{33,49},{49,33},{2,18}... | collective-permute-start | bytes 786440 | tf_op jit(solution)/shard_map/ppermute | solution.py:312
  69.7 0.9 shard_map.66
  70.6 3.5 %all-to-all-start.2 = ((bf16[8,32,8,128]{3,2,1,0:T(8,128)(2,1)}), bf16[8,32,8,128]{3,2,1,0:T(8,128)(2,1)S(1)}, u32[]{:S(2)}, u32[]{:S(2)}) async-start(bf16[8,32,8,128]{3,2,1,0:T(8,128)(2,1)} %shard_map.66), calls=%async_computation.2 | async-start | bytes 1048576 | tf_op jit(solution)/shard_map/all_to_all | solution.py:321
  74.1 0.4 collective-permute-start.4
  74.5 7.6 %collective-permute-done.3.refs_3_ = bf16[32,4,8,128]{3,2,1,0:T(8,128)(2,1)S(1)} collective-permute-done((bf16[32,4,8,128]{3,2,1,0:T(8,128)(2,1)S(1)}, bf16[32,4,8,128]{3,2,1,0:T(8,128)(2,1)S(1)}, u32[]{:S(2)}, u32[]{:S(2)}) %collective-permute-start.3) | collective-permute-done | bytes 262176 | tf_op jit(solution)/shard_map/ppermute | solution.py:312
  82.1 0.0 collective-permute-start.7
  82.1 0.5 collective-permute-start.6
  82.6 0.1 collective-permute-start.5
  82.7 4.2 %all-to-all-done.2.refs_8_ = bf16[8,32,8,128]{3,2,1,0:T(8,128)(2,1)S(1)} async-done(((bf16[8,32,8,128]{3,2,1,0:T(8,128)(2,1)}), bf16[8,32,8,128]{3,2,1,0:T(8,128)(2,1)S(1)}, u32[]{:S(2)}, u32[]{:S(2)}) %all-to-all-start.2) | async-done | bytes 524320 | tf_op jit(solution)/shard_map/all_to_all | solution.py:321
  86.9 7.5 %shard_map.67 = bf16[32,128,1024]{2,1,0:T(8,128)(2,1)} custom-call(s32[1]{0:T(128)} %bitcast.chunk_at, s32[1]{0:T(128)} %bitcast.1.core_at, bf16[32,4,8,128]{3,2,1,0:T(8,128)(2,1)S(1)} %slice.8.refs_0_, bf16[32,4,8,128]{3,2,1,0:T(8,128)(2,1)S(1)} %collective-permute-done.1.refs_1_, bf16[32,4,8,128]{3,2,1,0:T(8,128)(2,1)S(1)} %collective-permute-done.2.refs_2_, ...), custom_call_target="tpu_custom_call" | custom-call | tf_op jit(solution)/shard_map/pallas_call | solution.py:263
  (9 shorter events, 0.0 us)
Async XLA Ops:
  0.7 11.0 %collective-permute-start = (bf16[32,128]{1,0:T(8,128)(2,1)S(1)}, bf16[32,128]{1,0:T(8,128)(2,1)S(1)}, u32[]{:S(2)}, u32[]{:S(2)}) collective-permute-start(bf16[32,128]{1,0:T(8,128)(2,1)S(1)} %slice.6), channel_id=1, source_target_pairs={{0,1},{1,2},{2,3},{3,4},{4,5},{5,6},{6,7},{8,9},{9,10},{10,11},{11... | collective-permute-start | bytes 24584 | tf_op jit(solution)/shard_map/ppermute | solution.py:285
  11.7 1.0 %copy-start = (f32[512,128]{1,0:T(8,128)S(1)}, f32[512,128]{1,0:T(8,128)}, u32[]{:S(2)}) copy-start(f32[512,128]{1,0:T(8,128)} %constant.19.clone.table) | copy-start | bytes 786436
  12.6 0.7 copy-start.1
  30.2 0.7 copy-start.2
  65.5 16.5 %collective-permute-start.3 = (bf16[32,4,8,128]{3,2,1,0:T(8,128)(2,1)S(1)}, bf16[32,4,8,128]{3,2,1,0:T(8,128)(2,1)S(1)}, u32[]{:S(2)}, u32[]{:S(2)}) collective-permute-start(bf16[32,4,8,128]{3,2,1,0:T(8,128)(2,1)S(1)} %slice.8.refs_0_), channel_id=1, source_target_pairs={{0,48},{16,32},{32,16},{48,0},{1,49},{17,33},{33,17},{49,1},{2,50}... | collective-permute-start | bytes 786440 | tf_op jit(solution)/shard_map/ppermute | solution.py:312
  66.8 15.3 %collective-permute-start.2 = (bf16[32,4,8,128]{3,2,1,0:T(8,128)(2,1)S(1)}, bf16[32,4,8,128]{3,2,1,0:T(8,128)(2,1)S(1)}, u32[]{:S(2)}, u32[]{:S(2)}) collective-permute-start(bf16[32,4,8,128]{3,2,1,0:T(8,128)(2,1)S(1)} %slice.8.refs_0_), channel_id=1, source_target_pairs={{0,32},{16,48},{32,0},{48,16},{1,33},{17,49},{33,1},{49,17},{2,34}... | collective-permute-start | bytes 786440 | tf_op jit(solution)/shard_map/ppermute | solution.py:312
  68.3 14.3 %collective-permute-start.1 = (bf16[32,4,8,128]{3,2,1,0:T(8,128)(2,1)S(1)}, bf16[32,4,8,128]{3,2,1,0:T(8,128)(2,1)S(1)}, u32[]{:S(2)}, u32[]{:S(2)}) collective-permute-start(bf16[32,4,8,128]{3,2,1,0:T(8,128)(2,1)S(1)} %slice.8.refs_0_), channel_id=1, source_target_pairs={{0,16},{16,0},{32,48},{48,32},{1,17},{17,1},{33,49},{49,33},{2,18}... | collective-permute-start | bytes 786440 | tf_op jit(solution)/shard_map/ppermute | solution.py:312
  70.6 16.3 %all-to-all-start.2 = ((bf16[8,32,8,128]{3,2,1,0:T(8,128)(2,1)}), bf16[8,32,8,128]{3,2,1,0:T(8,128)(2,1)S(1)}, u32[]{:S(2)}, u32[]{:S(2)}) async-start(bf16[8,32,8,128]{3,2,1,0:T(8,128)(2,1)} %shard_map.66), calls=%async_computation.2 | async-start | bytes 1048576 | tf_op jit(solution)/shard_map/all_to_all | solution.py:321
  74.1 8.6 %collective-permute-start.4 = (bf16[32,4,8,128]{3,2,1,0:T(8,128)(2,1)S(1)}, bf16[32,4,8,128]{3,2,1,0:T(8,128)(2,1)S(1)}, u32[]{:S(2)}, u32[]{:S(2)}) collective-permute-start(bf16[32,4,8,128]{3,2,1,0:T(8,128)(2,1)S(1)} %slice.8.refs_0_), channel_id=1, source_target_pairs={{0,8},{8,0},{1,9},{9,1},{2,10},{10,2},{3,11},{11,3},{4,12},{12,4},... | collective-permute-start | bytes 786440 | tf_op jit(solution)/shard_map/ppermute | solution.py:313
  82.1 4.8 %collective-permute-start.7 = (bf16[32,4,8,128]{3,2,1,0:T(8,128)(2,1)S(1)}, bf16[32,4,8,128]{3,2,1,0:T(8,128)(2,1)S(1)}, u32[]{:S(2)}, u32[]{:S(2)}) collective-permute-start(bf16[32,4,8,128]{3,2,1,0:T(8,128)(2,1)S(1)} %collective-permute-done.3.refs_3_), channel_id=1, source_target_pairs={{0,8},{8,0},{1,9},{9,1},{2,10},{10,2},{3,11},{11,3},{4,12},{12,4},... | collective-permute-start | bytes 786440 | tf_op jit(solution)/shard_map/ppermute | solution.py:313
  82.1 4.8 %collective-permute-start.6 = (bf16[32,4,8,128]{3,2,1,0:T(8,128)(2,1)S(1)}, bf16[32,4,8,128]{3,2,1,0:T(8,128)(2,1)S(1)}, u32[]{:S(2)}, u32[]{:S(2)}) collective-permute-start(bf16[32,4,8,128]{3,2,1,0:T(8,128)(2,1)S(1)} %collective-permute-done.2.refs_2_), channel_id=1, source_target_pairs={{0,8},{8,0},{1,9},{9,1},{2,10},{10,2},{3,11},{11,3},{4,12},{12,4},... | collective-permute-start | bytes 786440 | tf_op jit(solution)/shard_map/ppermute | solution.py:313
  82.6 4.3 %collective-permute-start.5 = (bf16[32,4,8,128]{3,2,1,0:T(8,128)(2,1)S(1)}, bf16[32,4,8,128]{3,2,1,0:T(8,128)(2,1)S(1)}, u32[]{:S(2)}, u32[]{:S(2)}) collective-permute-start(bf16[32,4,8,128]{3,2,1,0:T(8,128)(2,1)S(1)} %collective-permute-done.1.refs_1_), channel_id=1, source_target_pairs={{0,8},{8,0},{1,9},{9,1},{2,10},{10,2},{3,11},{11,3},{4,12},{12,4},... | collective-permute-start | bytes 786440 | tf_op jit(solution)/shard_map/ppermute | solution.py:313

commit v6 on v5

--- a/solution.py
+++ b/solution.py
@@ -45,16 +45,19 @@
     return lax.dot_general(a, b, (((1,), (1,)), ((), ())), preferred_element_type=F32)
 
 
-def front_kernel(taps_used, start, window, taps, x, tail, table, out, product, before):
+def front_kernel(settings, x, tail, table, out, product, before):
+    window = lax.axis_index("y") * 2 + lax.axis_index("h")
     lane = lax.broadcasted_iota(jnp.int32, (1, FACTOR), 1)
-    kept = jnp.where(lane < taps_used[0], taps[...], 0.0)
+    used = jnp.broadcast_to(settings[:, FACTOR : FACTOR + 1], (1, FACTOR)).astype(jnp.int32)
+    start = jnp.broadcast_to(settings[:, FACTOR + 1 : FACTOR + 2], (1, FACTOR)).astype(jnp.int32)
+    kept = jnp.where(lane < used, settings[:, :FACTOR], 0.0)
     kept = jnp.concatenate([kept, jnp.zeros_like(kept)], axis=1)
     spread = jnp.broadcast_to(kept, (2 * FACTOR, 2 * FACTOR))
     matrix = pltpu.roll(spread, FACTOR, 1, stride=1, stride_axis=0)[:, :FACTOR].astype(BF16)
     both = jnp.concatenate([matrix[FACTOR:], matrix[:FACTOR]], axis=1)
     before[...] = dot(tail[...], matrix[:FACTOR])
     first = table[: 2 * FACTOR].astype(BF16)
-    low = lax.shift_right_logical(start[0], 7)
+    low = lax.shift_right_logical(start, 7)
     row = lax.broadcasted_iota(jnp.int32, (8, FACTOR), 0)
     pick = (lax.broadcasted_iota(jnp.int32, (8, FACTOR), 1) == low + row).astype(F32).astype(BF16)
     cosine = dot(pick, first[:FACTOR])
@@ -89,10 +92,10 @@
 
     lax.fori_loop(0, COUNT // BATCH, some, 0)
 
-    early = lax.broadcasted_iota(jnp.int32, (COUNT, FACTOR), 1) >= (start[0] & (FACTOR - 1))
+    early = lax.broadcasted_iota(jnp.int32, (COUNT, FACTOR), 1) >= (start & (FACTOR - 1))
     residue = lax.broadcasted_iota(jnp.int32, (FACTOR, BAND), 0)
     lane = lax.broadcasted_iota(jnp.int32, (FACTOR, BAND), 1)
-    place = (lane & -FACTOR) + ((lane - WIDTH * window[0]) & (FACTOR - 1))
+    place = (lane & -FACTOR) + ((lane - WIDTH * window) & (FACTOR - 1))
     placed = None
     for q in range(QUARTERS):
         re = jnp.where(early, product[q], product[q + 1])
@@ -133,11 +136,11 @@
     return parts
 
 
-def cross_kernel(parts, chunk_at, core_at, *refs):
+def cross_kernel(parts, *refs):
     count = len(parts)
     mine, theirs, rows = refs[:count], refs[count : 2 * count], refs[2 * count]
     out, left, coef, mixed, stage, done = refs[-6:]
-    x, core = chunk_at[0], core_at[0]
+    x, core = lax.axis_index("x"), lax.axis_index("c")
     spot = lax.broadcasted_iota(jnp.int32, (8, FACTOR), 1) // WIDTH
     bits = [(spot & (1 << s)) != 0 for s in range(3)]
     inner = lax.broadcasted_iota(jnp.int32, (WIDTH, FACTOR), 0)
@@ -252,9 +255,9 @@
             copy.wait()
 
 
-def cross(parts, chunk_at, core_at, mine, theirs, rows, before):
-    args = [chunk_at, core_at, *mine, *theirs, rows]
-    specs = [SMEM] * 2 + [VMEM] * (len(args) - 2)
+def cross(parts, mine, theirs, rows, before):
+    args = [*mine, *theirs, rows]
+    specs = [VMEM] * len(args)
     aliases = {}
     if before is not None:
         aliases = {len(args): 0}
@@ -283,18 +286,18 @@
 
 def shards(samples, fir_taps, tap_counts, band_start, grid_blocks):
     tail = lax.ppermute(samples[:, -FACTOR:], WIN, [(i, i + 1) for i in range(WINDOWS - 1)])
+    settings = jnp.concatenate(
+        [fir_taps, tap_counts.astype(F32), band_start.astype(F32), jnp.zeros((FACTOR - 2,), F32)]
+    )
     pieces = pl.pallas_call(
         front_kernel,
-        in_specs=[SMEM, SMEM, SMEM, VMEM, VMEM, VMEM, VMEM],
+        in_specs=[VMEM, VMEM, VMEM, VMEM],
         out_specs=VMEM,
         out_shape=jax.ShapeDtypeStruct((COUNT, 8, FACTOR), BF16),
         scratch_shapes=[pltpu.VMEM((16, COUNT, FACTOR), F32), pltpu.VMEM((COUNT, FACTOR), F32)],
         compiler_params=pltpu.CompilerParams(vmem_limit_bytes=LIMIT),
     )(
-        tap_counts,
-        band_start,
-        lax.axis_index(WIN).reshape(1),
-        fir_taps.reshape(1, FACTOR),
+        settings.reshape(1, 2 * FACTOR),
         samples.reshape(COUNT, FACTOR, FACTOR),
         tail,
         tables(),
@@ -319,8 +322,7 @@
         compiler_params=SMALL,
     )(got)
     rows = lax.all_to_all(rows, ("x", "c"), 0, 0, tiled=True)
-    chunk_at, core_at = lax.axis_index("x").reshape(1), lax.axis_index("c").reshape(1)
-    return cross((0, 1, 2, 3), chunk_at, core_at, mine, theirs, rows, None)
+    return cross((0, 1, 2, 3), mine, theirs, rows, None)
 
 
 def solution(mesh):

time: 94.8 us -> 94.2 us (level)
    unnamed x7 -> x5, local copies, waits for them, and re-layouts: 3.72 us -> 3.07 us
where the time goes in v6:
time: 94.2 us; the launch traced here: 93.8 us
  blocking collectives  46.6 us (49%)
  starting transfers between devices  16.9 us (18%)
  Pallas kernels  12.7 us (13%)
  waiting for transfers between devices  11.8 us (13%)
  local copies, waits for them, and re-layouts  3.78 us (4%)
  between operations  1.38 us (1%)
    all_to_all x1, blocking collectives, shards(): got = lax.all_to_all(sent, ('z', *WIN), 0, 0, tiled=True)  33.3 us
    all_to_all x1, blocking collectives, shards(): every = lax.all_to_all(pieces, CHAN, 0, 0, tiled=True)  13.3 us
    ppermute x1, starting transfers between devices, shards(): lax.ppermute(samples[:, -FACTOR:], WIN, [(i, i + 1) for i in range(WINDOW...  8.18 us
    ppermute x3, waiting for transfers between devices, shards(): lax.ppermute(mine[0], 'x', [(i, i ^ d) for i in range(4)])  7.57 us
    pallas_call x1, Pallas kernels, cross(): pl.pallas_call(functools.partial(cross_kernel, parts), in_specs=specs, ou...  7.53 us
    all_to_all x1, waiting for transfers between devices, shards(): rows = lax.all_to_all(rows, ('x', 'c'), 0, 0, tiled=True)  4.19 us
    ppermute x3, starting transfers between devices, shards(): lax.ppermute(mine[0], 'x', [(i, i ^ d) for i in range(4)])  4.18 us
    pallas_call x1, Pallas kernels, shards(): pl.pallas_call(front_kernel, in_specs=[VMEM, VMEM, VMEM, VMEM], out_specs...  3.66 us
  transfers between devices with their start and end apart: 9, of which 2 were waited for; matrix products, arithmetic and copies ran while one was open for 2% of the time, Pallas kernels for 1%

profile of v6, /device:TPU:32, one launch (start us, length us, event | category | flops | bytes accessed | tf_op | source)
XLA Modules:
  0.0 93.8 jit_solution(17696855839482432253)
XLA Ops:
  0.0 0.7 slice.6
  0.7 8.2 %collective-permute-start = (bf16[32,128]{1,0:T(8,128)(2,1)S(1)}, bf16[32,128]{1,0:T(8,128)(2,1)S(1)}, u32[]{:S(2)}, u32[]{:S(2)}) collective-permute-start(bf16[32,128]{1,0:T(8,128)(2,1)S(1)} %slice.6), channel_id=1, source_target_pairs={{0,1},{1,2},{2,3},{3,4},{4,5},{5,6},{6,7},{8,9},{9,10},{10,11},{11... | collective-permute-start | bytes 24584 | tf_op jit(solution)/shard_map/ppermute | solution.py:288
  10.2 0.7 pad_maximum_fusion
  10.9 1.5 %copy.7 = bf16[4,8,128,128]{3,2,1,0:T(8,128)(2,1)S(1)} copy(bf16[4,8,128,128]{3,1,2,0:T(8,128)(2,1)} %bitcast.5) | data formatting | bytes 2097152
  12.4 0.0 copy-start
  12.4 0.9 %copy-done = f32[512,128]{1,0:T(8,128)S(1)} copy-done((f32[512,128]{1,0:T(8,128)S(1)}, f32[512,128]{1,0:T(8,128)}, u32[]{:S(2)}) %copy-start) | copy-done | bytes 262168
  13.4 3.7 %shard_map.64 = bf16[32,8,128]{2,1,0:T(8,128)(2,1)S(1)} custom-call(f32[1,256]{1,0:T(1,128)S(1)} %bitcast.4, bf16[32,128,128]{2,1,0:T(8,128)(2,1)S(1)} %bitcast.3, bf16[32,128]{1,0:T(8,128)(2,1)S(1)} %collective-permute-done.tail, f32[512,128]{1,0:T(8,128)S(1)} %copy-done), custom_call_target="tpu_custom_call" | custom-call | tf_op jit(solution)/shard_map/pallas_call | solution.py:292
  17.0 13.3 %all_to_all.15.every = bf16[32,8,128]{2,1,0:T(8,128)(2,1)S(1)} all-to-all(bf16[32,8,128]{2,1,0:T(8,128)(2,1)S(1)} %shard_map.64), channel_id=1, replica_groups=mesh['z'=4,'x'=4,'c'=2,'y'=4,'h'=2] {'z','x','c'}, dimensions={0} | all-to-all | bytes 131072 | tf_op jit(solution)/shard_map/all_to_all | solution.py:305
  30.4 0.7 copy-done.1
  31.0 0.6 shard_map.65
  31.7 33.3 %all_to_all.16.got = bf16[32,12,8,128]{3,2,1,0:T(8,128)(2,1)S(1)} all-to-all(bf16[32,12,8,128]{3,2,1,0:T(8,128)(2,1)S(1)} %shard_map.65), channel_id=1, replica_groups=mesh['z'=4,'x'=4,'c'=2,'y'=4,'h'=2] {'z','y','h'}, dimensions={0} | all-to-all | bytes 1572864 | tf_op jit(solution)/shard_map/all_to_all | solution.py:313
  65.0 1.3 %collective-permute-start.3 = (bf16[32,4,8,128]{3,2,1,0:T(8,128)(2,1)S(1)}, bf16[32,4,8,128]{3,2,1,0:T(8,128)(2,1)S(1)}, u32[]{:S(2)}, u32[]{:S(2)}) collective-permute-start(bf16[32,4,8,128]{3,2,1,0:T(8,128)(2,1)S(1)} %slice.8.refs_0_), channel_id=1, source_target_pairs={{0,48},{16,32},{32,16},{48,0},{1,49},{17,33},{33,17},{49,1},{2,50}... | collective-permute-start | bytes 786440 | tf_op jit(solution)/shard_map/ppermute | solution.py:315
  66.2 1.4 %collective-permute-start.2 = (bf16[32,4,8,128]{3,2,1,0:T(8,128)(2,1)S(1)}, bf16[32,4,8,128]{3,2,1,0:T(8,128)(2,1)S(1)}, u32[]{:S(2)}, u32[]{:S(2)}) collective-permute-start(bf16[32,4,8,128]{3,2,1,0:T(8,128)(2,1)S(1)} %slice.8.refs_0_), channel_id=1, source_target_pairs={{0,32},{16,48},{32,0},{48,16},{1,33},{17,49},{33,1},{49,17},{2,34}... | collective-permute-start | bytes 786440 | tf_op jit(solution)/shard_map/ppermute | solution.py:315
  67.7 1.5 %collective-permute-start.1 = (bf16[32,4,8,128]{3,2,1,0:T(8,128)(2,1)S(1)}, bf16[32,4,8,128]{3,2,1,0:T(8,128)(2,1)S(1)}, u32[]{:S(2)}, u32[]{:S(2)}) collective-permute-start(bf16[32,4,8,128]{3,2,1,0:T(8,128)(2,1)S(1)} %slice.8.refs_0_), channel_id=1, source_target_pairs={{0,16},{16,0},{32,48},{48,32},{1,17},{17,1},{33,49},{49,33},{2,18}... | collective-permute-start | bytes 786440 | tf_op jit(solution)/shard_map/ppermute | solution.py:315
  69.1 0.9 shard_map.66
  70.0 3.5 %all-to-all-start.2 = ((bf16[8,32,8,128]{3,2,1,0:T(8,128)(2,1)}), bf16[8,32,8,128]{3,2,1,0:T(8,128)(2,1)S(1)}, u32[]{:S(2)}, u32[]{:S(2)}) async-start(bf16[8,32,8,128]{3,2,1,0:T(8,128)(2,1)} %shard_map.66), calls=%async_computation.2 | async-start | bytes 1048576 | tf_op jit(solution)/shard_map/all_to_all | solution.py:324
  73.5 0.4 collective-permute-start.4
  73.9 7.6 %collective-permute-done.3.refs_3_ = bf16[32,4,8,128]{3,2,1,0:T(8,128)(2,1)S(1)} collective-permute-done((bf16[32,4,8,128]{3,2,1,0:T(8,128)(2,1)S(1)}, bf16[32,4,8,128]{3,2,1,0:T(8,128)(2,1)S(1)}, u32[]{:S(2)}, u32[]{:S(2)}) %collective-permute-start.3) | collective-permute-done | bytes 262176 | tf_op jit(solution)/shard_map/ppermute | solution.py:315
  81.5 0.5 collective-permute-start.6
  82.0 0.1 collective-permute-start.5
  82.1 4.2 %all-to-all-done.2.refs_8_ = bf16[8,32,8,128]{3,2,1,0:T(8,128)(2,1)S(1)} async-done(((bf16[8,32,8,128]{3,2,1,0:T(8,128)(2,1)}), bf16[8,32,8,128]{3,2,1,0:T(8,128)(2,1)S(1)}, u32[]{:S(2)}, u32[]{:S(2)}) %all-to-all-start.2) | async-done | bytes 524320 | tf_op jit(solution)/shard_map/all_to_all | solution.py:324
  86.3 0.0 collective-permute-done.7.refs_7_
  86.3 0.0 collective-permute-done.6.refs_6_
  86.3 7.5 %shard_map.67 = bf16[32,128,1024]{2,1,0:T(8,128)(2,1)} custom-call(bf16[32,4,8,128]{3,2,1,0:T(8,128)(2,1)S(1)} %slice.8.refs_0_, bf16[32,4,8,128]{3,2,1,0:T(8,128)(2,1)S(1)} %collective-permute-done.1.refs_1_, bf16[32,4,8,128]{3,2,1,0:T(8,128)(2,1)S(1)} %collective-permute-done.2.refs_2_, bf16[32,4,8,128]{3,2,1,0:T(8,128)(2,1)S(1)} %collective-permute-done.3.refs_3_, ...), custom_call_target="tpu_custom_call" | custom-call | tf_op jit(solution)/shard_map/pallas_call | solution.py:266
  (9 shorter events, 0.0 us)
Async XLA Ops:
  0.7 11.7 %collective-permute-start = (bf16[32,128]{1,0:T(8,128)(2,1)S(1)}, bf16[32,128]{1,0:T(8,128)(2,1)S(1)}, u32[]{:S(2)}, u32[]{:S(2)}) collective-permute-start(bf16[32,128]{1,0:T(8,128)(2,1)S(1)} %slice.6), channel_id=1, source_target_pairs={{0,1},{1,2},{2,3},{3,4},{4,5},{5,6},{6,7},{8,9},{9,10},{10,11},{11... | collective-permute-start | bytes 24584 | tf_op jit(solution)/shard_map/ppermute | solution.py:288
  12.4 1.0 %copy-start = (f32[512,128]{1,0:T(8,128)S(1)}, f32[512,128]{1,0:T(8,128)}, u32[]{:S(2)}) copy-start(f32[512,128]{1,0:T(8,128)} %constant.4.clone.table) | copy-start | bytes 786436
  30.4 0.7 copy-start.1
  65.0 16.5 %collective-permute-start.3 = (bf16[32,4,8,128]{3,2,1,0:T(8,128)(2,1)S(1)}, bf16[32,4,8,128]{3,2,1,0:T(8,128)(2,1)S(1)}, u32[]{:S(2)}, u32[]{:S(2)}) collective-permute-start(bf16[32,4,8,128]{3,2,1,0:T(8,128)(2,1)S(1)} %slice.8.refs_0_), channel_id=1, source_target_pairs={{0,48},{16,32},{32,16},{48,0},{1,49},{17,33},{33,17},{49,1},{2,50}... | collective-permute-start | bytes 786440 | tf_op jit(solution)/shard_map/ppermute | solution.py:315
  66.2 15.3 %collective-permute-start.2 = (bf16[32,4,8,128]{3,2,1,0:T(8,128)(2,1)S(1)}, bf16[32,4,8,128]{3,2,1,0:T(8,128)(2,1)S(1)}, u32[]{:S(2)}, u32[]{:S(2)}) collective-permute-start(bf16[32,4,8,128]{3,2,1,0:T(8,128)(2,1)S(1)} %slice.8.refs_0_), channel_id=1, source_target_pairs={{0,32},{16,48},{32,0},{48,16},{1,33},{17,49},{33,1},{49,17},{2,34}... | collective-permute-start | bytes 786440 | tf_op jit(solution)/shard_map/ppermute | solution.py:315
  67.7 14.3 %collective-permute-start.1 = (bf16[32,4,8,128]{3,2,1,0:T(8,128)(2,1)S(1)}, bf16[32,4,8,128]{3,2,1,0:T(8,128)(2,1)S(1)}, u32[]{:S(2)}, u32[]{:S(2)}) collective-permute-start(bf16[32,4,8,128]{3,2,1,0:T(8,128)(2,1)S(1)} %slice.8.refs_0_), channel_id=1, source_target_pairs={{0,16},{16,0},{32,48},{48,32},{1,17},{17,1},{33,49},{49,33},{2,18}... | collective-permute-start | bytes 786440 | tf_op jit(solution)/shard_map/ppermute | solution.py:315
  70.0 16.3 %all-to-all-start.2 = ((bf16[8,32,8,128]{3,2,1,0:T(8,128)(2,1)}), bf16[8,32,8,128]{3,2,1,0:T(8,128)(2,1)S(1)}, u32[]{:S(2)}, u32[]{:S(2)}) async-start(bf16[8,32,8,128]{3,2,1,0:T(8,128)(2,1)} %shard_map.66), calls=%async_computation.2 | async-start | bytes 1048576 | tf_op jit(solution)/shard_map/all_to_all | solution.py:324
  73.5 8.6 %collective-permute-start.4 = (bf16[32,4,8,128]{3,2,1,0:T(8,128)(2,1)S(1)}, bf16[32,4,8,128]{3,2,1,0:T(8,128)(2,1)S(1)}, u32[]{:S(2)}, u32[]{:S(2)}) collective-permute-start(bf16[32,4,8,128]{3,2,1,0:T(8,128)(2,1)S(1)} %slice.8.refs_0_), channel_id=1, source_target_pairs={{0,8},{8,0},{1,9},{9,1},{2,10},{10,2},{3,11},{11,3},{4,12},{12,4},... | collective-permute-start | bytes 786440 | tf_op jit(solution)/shard_map/ppermute | solution.py:316
  81.5 4.8 %collective-permute-start.7 = (bf16[32,4,8,128]{3,2,1,0:T(8,128)(2,1)S(1)}, bf16[32,4,8,128]{3,2,1,0:T(8,128)(2,1)S(1)}, u32[]{:S(2)}, u32[]{:S(2)}) collective-permute-start(bf16[32,4,8,128]{3,2,1,0:T(8,128)(2,1)S(1)} %collective-permute-done.3.refs_3_), channel_id=1, source_target_pairs={{0,8},{8,0},{1,9},{9,1},{2,10},{10,2},{3,11},{11,3},{4,12},{12,4},... | collective-permute-start | bytes 786440 | tf_op jit(solution)/shard_map/ppermute | solution.py:316
  81.5 4.8 %collective-permute-start.6 = (bf16[32,4,8,128]{3,2,1,0:T(8,128)(2,1)S(1)}, bf16[32,4,8,128]{3,2,1,0:T(8,128)(2,1)S(1)}, u32[]{:S(2)}, u32[]{:S(2)}) collective-permute-start(bf16[32,4,8,128]{3,2,1,0:T(8,128)(2,1)S(1)} %collective-permute-done.2.refs_2_), channel_id=1, source_target_pairs={{0,8},{8,0},{1,9},{9,1},{2,10},{10,2},{3,11},{11,3},{4,12},{12,4},... | collective-permute-start | bytes 786440 | tf_op jit(solution)/shard_map/ppermute | solution.py:316
  82.0 4.3 %collective-permute-start.5 = (bf16[32,4,8,128]{3,2,1,0:T(8,128)(2,1)S(1)}, bf16[32,4,8,128]{3,2,1,0:T(8,128)(2,1)S(1)}, u32[]{:S(2)}, u32[]{:S(2)}) collective-permute-start(bf16[32,4,8,128]{3,2,1,0:T(8,128)(2,1)S(1)} %collective-permute-done.1.refs_1_), channel_id=1, source_target_pairs={{0,8},{8,0},{1,9},{9,1},{2,10},{10,2},{3,11},{11,3},{4,12},{12,4},... | collective-permute-start | bytes 786440 | tf_op jit(solution)/shard_map/ppermute | solution.py:316

commit v7 on v6

--- a/solution.py
+++ b/solution.py
@@ -311,9 +311,7 @@
         compiler_params=SMALL,
     )(grid_blocks, every)
     got = lax.all_to_all(sent, ("z", *WIN), 0, 0, tiled=True)
-    mine = [got[:, :4]]
-    mine += [lax.ppermute(mine[0], "x", [(i, i ^ d) for i in range(4)]) for d in (1, 2, 3)]
-    theirs = [lax.ppermute(this, "c", [(0, 1), (1, 0)]) for this in mine]
+    cols = got[:, :4]
     rows = pl.pallas_call(
         turn_kernel,
         in_specs=[VMEM],
@@ -321,6 +319,11 @@
         out_shape=jax.ShapeDtypeStruct((8, COUNT, 8, FACTOR), BF16),
         compiler_params=SMALL,
     )(got)
+    last, rows = lax.optimization_barrier((cols, rows))
+    mine = [cols] + [
+        lax.ppermute(last if d == 2 else cols, "x", [(i, i ^ d) for i in range(4)]) for d in (1, 2, 3)
+    ]
+    theirs = [lax.ppermute(this, "c", [(0, 1), (1, 0)]) for this in mine]
     rows = lax.all_to_all(rows, ("x", "c"), 0, 0, tiled=True)
     return cross((0, 1, 2, 3), mine, theirs, rows, None)
 

time: 94.2 us -> 94.1 us (level)
  transfers between devices with their start and end apart: 9 -> 9, of which waited for: 2 -> 3; matrix products, arithmetic and copies ran while one was open for 2% -> 2% of each run, Pallas kernels for 1% -> 0%
where the time goes in v7:
time: 94.1 us; the launch traced here: 93.7 us
  blocking collectives  46.6 us (50%)
  starting transfers between devices  16.2 us (17%)
  Pallas kernels  12.7 us (13%)
  waiting for transfers between devices  12.3 us (13%)
  local copies, waits for them, and re-layouts  3.78 us (4%)
  between operations  1.37 us (1%)
    all_to_all x1, blocking collectives, shards(): got = lax.all_to_all(sent, ('z', *WIN), 0, 0, tiled=True)  33.3 us
    all_to_all x1, blocking collectives, shards(): every = lax.all_to_all(pieces, CHAN, 0, 0, tiled=True)  13.3 us
    ppermute x1, starting transfers between devices, shards(): lax.ppermute(samples[:, -FACTOR:], WIN, [(i, i + 1) for i in range(WINDOW...  8.18 us
    ppermute x3, waiting for transfers between devices, shards(): lax.ppermute(last if d == 2 else cols, 'x', [(i, i ^ d) for i in range(4)])  7.93 us
    pallas_call x1, Pallas kernels, cross(): pl.pallas_call(functools.partial(cross_kernel, parts), in_specs=specs, ou...  7.53 us
    all_to_all x1, waiting for transfers between devices, shards(): rows = lax.all_to_all(rows, ('x', 'c'), 0, 0, tiled=True)  4.35 us
    pallas_call x1, Pallas kernels, shards(): pl.pallas_call(front_kernel, in_specs=[VMEM, VMEM, VMEM, VMEM], out_specs...  3.66 us
    all_to_all x1, starting transfers between devices, shards(): rows = lax.all_to_all(rows, ('x', 'c'), 0, 0, tiled=True)  3.54 us
  transfers between devices with their start and end apart: 9, of which 3 were waited for; matrix products, arithmetic and copies ran while one was open for 2% of the time, Pallas kernels for 0%

profile of v7, /device:TPU:32, one launch (start us, length us, event | category | flops | bytes accessed | tf_op | source)
XLA Modules:
  0.0 93.7 jit_solution(16304254997846641365)
XLA Ops:
  0.0 0.7 slice.6
  0.7 8.2 %collective-permute-start = (bf16[32,128]{1,0:T(8,128)(2,1)S(1)}, bf16[32,128]{1,0:T(8,128)(2,1)S(1)}, u32[]{:S(2)}, u32[]{:S(2)}) collective-permute-start(bf16[32,128]{1,0:T(8,128)(2,1)S(1)} %slice.6), channel_id=1, source_target_pairs={{0,1},{1,2},{2,3},{3,4},{4,5},{5,6},{6,7},{8,9},{9,10},{10,11},{11... | collective-permute-start | bytes 24584 | tf_op jit(solution)/shard_map/ppermute | solution.py:288
  10.2 0.7 pad_maximum_fusion
  10.9 1.5 %copy.7 = bf16[4,8,128,128]{3,2,1,0:T(8,128)(2,1)S(1)} copy(bf16[4,8,128,128]{3,1,2,0:T(8,128)(2,1)} %bitcast.5) | data formatting | bytes 2097152
  12.4 0.0 collective-permute-done.tail
  12.4 0.0 copy-start
  12.4 0.9 %copy-done = f32[512,128]{1,0:T(8,128)S(1)} copy-done((f32[512,128]{1,0:T(8,128)S(1)}, f32[512,128]{1,0:T(8,128)}, u32[]{:S(2)}) %copy-start) | copy-done | bytes 262168
  13.4 3.7 %shard_map.64 = bf16[32,8,128]{2,1,0:T(8,128)(2,1)S(1)} custom-call(f32[1,256]{1,0:T(1,128)S(1)} %bitcast.4, bf16[32,128,128]{2,1,0:T(8,128)(2,1)S(1)} %bitcast.3, bf16[32,128]{1,0:T(8,128)(2,1)S(1)} %collective-permute-done.tail, f32[512,128]{1,0:T(8,128)S(1)} %copy-done), custom_call_target="tpu_custom_call" | custom-call | tf_op jit(solution)/shard_map/pallas_call | solution.py:292
  17.0 13.3 %all_to_all.15.every = bf16[32,8,128]{2,1,0:T(8,128)(2,1)S(1)} all-to-all(bf16[32,8,128]{2,1,0:T(8,128)(2,1)S(1)} %shard_map.64), channel_id=1, replica_groups=mesh['z'=4,'x'=4,'c'=2,'y'=4,'h'=2] {'z','x','c'}, dimensions={0} | all-to-all | bytes 131072 | tf_op jit(solution)/shard_map/all_to_all | solution.py:305
  30.4 0.7 copy-done.1
  31.0 0.6 shard_map.65
  31.7 33.3 %all_to_all.16.got = bf16[32,12,8,128]{3,2,1,0:T(8,128)(2,1)S(1)} all-to-all(bf16[32,12,8,128]{3,2,1,0:T(8,128)(2,1)S(1)} %shard_map.65), channel_id=1, replica_groups=mesh['z'=4,'x'=4,'c'=2,'y'=4,'h'=2] {'z','y','h'}, dimensions={0} | all-to-all | bytes 1572864 | tf_op jit(solution)/shard_map/all_to_all | solution.py:313
  65.0 0.9 shard_map.66
  65.9 1.1 %collective-permute-start.2 = (bf16[32,4,8,128]{3,2,1,0:T(8,128)(2,1)S(1)}, bf16[32,4,8,128]{3,2,1,0:T(8,128)(2,1)S(1)}, u32[]{:S(2)}, u32[]{:S(2)}) collective-permute-start(bf16[32,4,8,128]{3,2,1,0:T(8,128)(2,1)S(1)} %slice.8.refs_0_), channel_id=1, source_target_pairs={{0,32},{16,48},{32,0},{48,16},{1,33},{17,49},{33,1},{49,17},{2,34}... | collective-permute-start | bytes 786440 | tf_op jit(solution)/shard_map/ppermute | solution.py:324
  66.9 2.2 %collective-permute-start.3 = (bf16[32,4,8,128]{3,2,1,0:T(8,128)(2,1)S(1)}, bf16[32,4,8,128]{3,2,1,0:T(8,128)(2,1)S(1)}, u32[]{:S(2)}, u32[]{:S(2)}) collective-permute-start(bf16[32,4,8,128]{3,2,1,0:T(8,128)(2,1)S(1)} %slice.8.refs_0_), channel_id=1, source_target_pairs={{0,48},{16,32},{32,16},{48,0},{1,49},{17,33},{33,17},{49,1},{2,50}... | collective-permute-start | bytes 786440 | tf_op jit(solution)/shard_map/ppermute | solution.py:324
  69.1 0.3 collective-permute-start.1
  69.3 3.5 %all-to-all-start.2 = ((bf16[8,32,8,128]{3,2,1,0:T(8,128)(2,1)}), bf16[8,32,8,128]{3,2,1,0:T(8,128)(2,1)S(1)}, u32[]{:S(2)}, u32[]{:S(2)}) async-start(bf16[8,32,8,128]{3,2,1,0:T(8,128)(2,1)} %shard_map.66), calls=%async_computation.2 | async-start | bytes 1048576 | tf_op jit(solution)/shard_map/all_to_all | solution.py:327
  72.9 0.5 collective-permute-start.4
  73.4 3.3 %collective-permute-done.2.refs_2_ = bf16[32,4,8,128]{3,2,1,0:T(8,128)(2,1)S(1)} collective-permute-done((bf16[32,4,8,128]{3,2,1,0:T(8,128)(2,1)S(1)}, bf16[32,4,8,128]{3,2,1,0:T(8,128)(2,1)S(1)}, u32[]{:S(2)}, u32[]{:S(2)}) %collective-permute-start.2) | collective-permute-done | bytes 262176 | tf_op jit(solution)/shard_map/ppermute | solution.py:324
  76.6 4.7 %collective-permute-done.3.refs_3_ = bf16[32,4,8,128]{3,2,1,0:T(8,128)(2,1)S(1)} collective-permute-done((bf16[32,4,8,128]{3,2,1,0:T(8,128)(2,1)S(1)}, bf16[32,4,8,128]{3,2,1,0:T(8,128)(2,1)S(1)}, u32[]{:S(2)}, u32[]{:S(2)}) %collective-permute-start.3) | collective-permute-done | bytes 262176 | tf_op jit(solution)/shard_map/ppermute | solution.py:324
  81.3 0.0 collective-permute-start.7
  81.3 0.5 collective-permute-start.5
  81.8 4.3 %all-to-all-done.2.refs_8_ = bf16[8,32,8,128]{3,2,1,0:T(8,128)(2,1)S(1)} async-done(((bf16[8,32,8,128]{3,2,1,0:T(8,128)(2,1)}), bf16[8,32,8,128]{3,2,1,0:T(8,128)(2,1)S(1)}, u32[]{:S(2)}, u32[]{:S(2)}) %all-to-all-start.2) | async-done | bytes 524320 | tf_op jit(solution)/shard_map/all_to_all | solution.py:327
  86.2 7.5 %shard_map.67 = bf16[32,128,1024]{2,1,0:T(8,128)(2,1)} custom-call(bf16[32,4,8,128]{3,2,1,0:T(8,128)(2,1)S(1)} %slice.8.refs_0_, bf16[32,4,8,128]{3,2,1,0:T(8,128)(2,1)S(1)} %collective-permute-done.1.refs_1_, bf16[32,4,8,128]{3,2,1,0:T(8,128)(2,1)S(1)} %collective-permute-done.2.refs_2_, bf16[32,4,8,128]{3,2,1,0:T(8,128)(2,1)S(1)} %collective-permute-done.3.refs_3_, ...), custom_call_target="tpu_custom_call" | custom-call | tf_op jit(solution)/shard_map/pallas_call | solution.py:266
  (9 shorter events, 0.0 us)
Async XLA Ops:
  0.7 11.7 %collective-permute-start = (bf16[32,128]{1,0:T(8,128)(2,1)S(1)}, bf16[32,128]{1,0:T(8,128)(2,1)S(1)}, u32[]{:S(2)}, u32[]{:S(2)}) collective-permute-start(bf16[32,128]{1,0:T(8,128)(2,1)S(1)} %slice.6), channel_id=1, source_target_pairs={{0,1},{1,2},{2,3},{3,4},{4,5},{5,6},{6,7},{8,9},{9,10},{10,11},{11... | collective-permute-start | bytes 24584 | tf_op jit(solution)/shard_map/ppermute | solution.py:288
  12.4 1.0 %copy-start = (f32[512,128]{1,0:T(8,128)S(1)}, f32[512,128]{1,0:T(8,128)}, u32[]{:S(2)}) copy-start(f32[512,128]{1,0:T(8,128)} %constant.4.clone.table) | copy-start | bytes 786436
  30.4 0.7 copy-start.1
  65.9 10.8 %collective-permute-start.2 = (bf16[32,4,8,128]{3,2,1,0:T(8,128)(2,1)S(1)}, bf16[32,4,8,128]{3,2,1,0:T(8,128)(2,1)S(1)}, u32[]{:S(2)}, u32[]{:S(2)}) collective-permute-start(bf16[32,4,8,128]{3,2,1,0:T(8,128)(2,1)S(1)} %slice.8.refs_0_), channel_id=1, source_target_pairs={{0,32},{16,48},{32,0},{48,16},{1,33},{17,49},{33,1},{49,17},{2,34}... | collective-permute-start | bytes 786440 | tf_op jit(solution)/shard_map/ppermute | solution.py:324
  66.9 14.4 %collective-permute-start.3 = (bf16[32,4,8,128]{3,2,1,0:T(8,128)(2,1)S(1)}, bf16[32,4,8,128]{3,2,1,0:T(8,128)(2,1)S(1)}, u32[]{:S(2)}, u32[]{:S(2)}) collective-permute-start(bf16[32,4,8,128]{3,2,1,0:T(8,128)(2,1)S(1)} %slice.8.refs_0_), channel_id=1, source_target_pairs={{0,48},{16,32},{32,16},{48,0},{1,49},{17,33},{33,17},{49,1},{2,50}... | collective-permute-start | bytes 786440 | tf_op jit(solution)/shard_map/ppermute | solution.py:324
  69.1 12.2 %collective-permute-start.1 = (bf16[32,4,8,128]{3,2,1,0:T(8,128)(2,1)S(1)}, bf16[32,4,8,128]{3,2,1,0:T(8,128)(2,1)S(1)}, u32[]{:S(2)}, u32[]{:S(2)}) collective-permute-start(bf16[32,4,8,128]{3,2,1,0:T(8,128)(2,1)S(1)} %slice.8.refs_0_), channel_id=1, source_target_pairs={{0,16},{16,0},{32,48},{48,32},{1,17},{17,1},{33,49},{49,33},{2,18}... | collective-permute-start | bytes 786440 | tf_op jit(solution)/shard_map/ppermute | solution.py:324
  69.3 16.8 %all-to-all-start.2 = ((bf16[8,32,8,128]{3,2,1,0:T(8,128)(2,1)}), bf16[8,32,8,128]{3,2,1,0:T(8,128)(2,1)S(1)}, u32[]{:S(2)}, u32[]{:S(2)}) async-start(bf16[8,32,8,128]{3,2,1,0:T(8,128)(2,1)} %shard_map.66), calls=%async_computation.2 | async-start | bytes 1048576 | tf_op jit(solution)/shard_map/all_to_all | solution.py:327
  72.9 8.9 %collective-permute-start.4 = (bf16[32,4,8,128]{3,2,1,0:T(8,128)(2,1)S(1)}, bf16[32,4,8,128]{3,2,1,0:T(8,128)(2,1)S(1)}, u32[]{:S(2)}, u32[]{:S(2)}) collective-permute-start(bf16[32,4,8,128]{3,2,1,0:T(8,128)(2,1)S(1)} %slice.8.refs_0_), channel_id=1, source_target_pairs={{0,8},{8,0},{1,9},{9,1},{2,10},{10,2},{3,11},{11,3},{4,12},{12,4},... | collective-permute-start | bytes 786440 | tf_op jit(solution)/shard_map/ppermute | solution.py:326
  76.6 9.5 %collective-permute-start.6 = (bf16[32,4,8,128]{3,2,1,0:T(8,128)(2,1)S(1)}, bf16[32,4,8,128]{3,2,1,0:T(8,128)(2,1)S(1)}, u32[]{:S(2)}, u32[]{:S(2)}) collective-permute-start(bf16[32,4,8,128]{3,2,1,0:T(8,128)(2,1)S(1)} %collective-permute-done.2.refs_2_), channel_id=1, source_target_pairs={{0,8},{8,0},{1,9},{9,1},{2,10},{10,2},{3,11},{11,3},{4,12},{12,4},... | collective-permute-start | bytes 786440 | tf_op jit(solution)/shard_map/ppermute | solution.py:326
  81.3 4.9 %collective-permute-start.7 = (bf16[32,4,8,128]{3,2,1,0:T(8,128)(2,1)S(1)}, bf16[32,4,8,128]{3,2,1,0:T(8,128)(2,1)S(1)}, u32[]{:S(2)}, u32[]{:S(2)}) collective-permute-start(bf16[32,4,8,128]{3,2,1,0:T(8,128)(2,1)S(1)} %collective-permute-done.3.refs_3_), channel_id=1, source_target_pairs={{0,8},{8,0},{1,9},{9,1},{2,10},{10,2},{3,11},{11,3},{4,12},{12,4},... | collective-permute-start | bytes 786440 | tf_op jit(solution)/shard_map/ppermute | solution.py:326
  81.3 4.9 %collective-permute-start.5 = (bf16[32,4,8,128]{3,2,1,0:T(8,128)(2,1)S(1)}, bf16[32,4,8,128]{3,2,1,0:T(8,128)(2,1)S(1)}, u32[]{:S(2)}, u32[]{:S(2)}) collective-permute-start(bf16[32,4,8,128]{3,2,1,0:T(8,128)(2,1)S(1)} %collective-permute-done.1.refs_1_), channel_id=1, source_target_pairs={{0,8},{8,0},{1,9},{9,1},{2,10},{10,2},{3,11},{11,3},{4,12},{12,4},... | collective-permute-start | bytes 786440 | tf_op jit(solution)/shard_map/ppermute | solution.py:326

commit v8 on v7

--- a/solution.py
+++ b/solution.py
@@ -16,7 +16,7 @@
 COUNT = 32
 QUARTERS = BAND // FACTOR
 WINDOWS = 8
-BATCH = 8
+BATCH = 16
 GROUPS = 8
 WIDTH = FACTOR // GROUPS
 SLOTS = 4

time: 94.1 us -> 93.3 us (level)
  no operation moved by 1% of the time
where the time goes in v8:
time: 93.3 us; the launch traced here: 92.9 us
  blocking collectives  46.6 us (50%)
  starting transfers between devices  16.2 us (17%)
  waiting for transfers between devices  12.3 us (13%)
  Pallas kernels  11.9 us (13%)
  local copies, waits for them, and re-layouts  3.78 us (4%)
  between operations  1.37 us (1%)
    all_to_all x1, blocking collectives, shards(): got = lax.all_to_all(sent, ('z', *WIN), 0, 0, tiled=True)  33.3 us
    all_to_all x1, blocking collectives, shards(): every = lax.all_to_all(pieces, CHAN, 0, 0, tiled=True)  13.3 us
    ppermute x1, starting transfers between devices, shards(): lax.ppermute(samples[:, -FACTOR:], WIN, [(i, i + 1) for i in range(WINDOW...  8.18 us
    ppermute x3, waiting for transfers between devices, shards(): lax.ppermute(last if d == 2 else cols, 'x', [(i, i ^ d) for i in range(4)])  7.93 us
    pallas_call x1, Pallas kernels, cross(): pl.pallas_call(functools.partial(cross_kernel, parts), in_specs=specs, ou...  7.53 us
    all_to_all x1, waiting for transfers between devices, shards(): rows = lax.all_to_all(rows, ('x', 'c'), 0, 0, tiled=True)  4.35 us
    all_to_all x1, starting transfers between devices, shards(): rows = lax.all_to_all(rows, ('x', 'c'), 0, 0, tiled=True)  3.54 us
    ppermute x3, starting transfers between devices, shards(): lax.ppermute(last if d == 2 else cols, 'x', [(i, i ^ d) for i in range(4)])  3.49 us
  transfers between devices with their start and end apart: 9, of which 3 were waited for; matrix products, arithmetic and copies ran while one was open for 2% of the time, Pallas kernels for 0%

profile of v8, /device:TPU:32, one launch (start us, length us, event | category | flops | bytes accessed | tf_op | source)
XLA Modules:
  0.0 92.9 jit_solution(6433310323080327745)
XLA Ops:
  0.0 0.7 slice.6
  0.7 8.2 %collective-permute-start = (bf16[32,128]{1,0:T(8,128)(2,1)S(1)}, bf16[32,128]{1,0:T(8,128)(2,1)S(1)}, u32[]{:S(2)}, u32[]{:S(2)}) collective-permute-start(bf16[32,128]{1,0:T(8,128)(2,1)S(1)} %slice.6), channel_id=1, source_target_pairs={{0,1},{1,2},{2,3},{3,4},{4,5},{5,6},{6,7},{8,9},{9,10},{10,11},{11... | collective-permute-start | bytes 24584 | tf_op jit(solution)/shard_map/ppermute | solution.py:288
  10.2 0.7 pad_maximum_fusion
  10.9 1.5 %copy.7 = bf16[4,8,128,128]{3,2,1,0:T(8,128)(2,1)S(1)} copy(bf16[4,8,128,128]{3,1,2,0:T(8,128)(2,1)} %bitcast.5) | data formatting | bytes 2097152
  12.4 0.0 collective-permute-done.tail
  12.4 0.0 copy-start
  12.4 0.9 %copy-done = f32[512,128]{1,0:T(8,128)S(1)} copy-done((f32[512,128]{1,0:T(8,128)S(1)}, f32[512,128]{1,0:T(8,128)}, u32[]{:S(2)}) %copy-start) | copy-done | bytes 262168
  13.4 2.8 %shard_map.64 = bf16[32,8,128]{2,1,0:T(8,128)(2,1)S(1)} custom-call(f32[1,256]{1,0:T(1,128)S(1)} %bitcast.4, bf16[32,128,128]{2,1,0:T(8,128)(2,1)S(1)} %bitcast.3, bf16[32,128]{1,0:T(8,128)(2,1)S(1)} %collective-permute-done.tail, f32[512,128]{1,0:T(8,128)S(1)} %copy-done), custom_call_target="tpu_custom_call" | custom-call | tf_op jit(solution)/shard_map/pallas_call | solution.py:292
  16.2 13.3 %all_to_all.15.every = bf16[32,8,128]{2,1,0:T(8,128)(2,1)S(1)} all-to-all(bf16[32,8,128]{2,1,0:T(8,128)(2,1)S(1)} %shard_map.64), channel_id=1, replica_groups=mesh['z'=4,'x'=4,'c'=2,'y'=4,'h'=2] {'z','x','c'}, dimensions={0} | all-to-all | bytes 131072 | tf_op jit(solution)/shard_map/all_to_all | solution.py:305
  29.5 0.7 copy-done.1
  30.2 0.6 shard_map.65
  30.8 33.3 %all_to_all.16.got = bf16[32,12,8,128]{3,2,1,0:T(8,128)(2,1)S(1)} all-to-all(bf16[32,12,8,128]{3,2,1,0:T(8,128)(2,1)S(1)} %shard_map.65), channel_id=1, replica_groups=mesh['z'=4,'x'=4,'c'=2,'y'=4,'h'=2] {'z','y','h'}, dimensions={0} | all-to-all | bytes 1572864 | tf_op jit(solution)/shard_map/all_to_all | solution.py:313
  64.1 0.9 shard_map.66
  65.0 1.1 %collective-permute-start.2 = (bf16[32,4,8,128]{3,2,1,0:T(8,128)(2,1)S(1)}, bf16[32,4,8,128]{3,2,1,0:T(8,128)(2,1)S(1)}, u32[]{:S(2)}, u32[]{:S(2)}) collective-permute-start(bf16[32,4,8,128]{3,2,1,0:T(8,128)(2,1)S(1)} %slice.8.refs_0_), channel_id=1, source_target_pairs={{0,32},{16,48},{32,0},{48,16},{1,33},{17,49},{33,1},{49,17},{2,34}... | collective-permute-start | bytes 786440 | tf_op jit(solution)/shard_map/ppermute | solution.py:324
  66.0 2.2 %collective-permute-start.3 = (bf16[32,4,8,128]{3,2,1,0:T(8,128)(2,1)S(1)}, bf16[32,4,8,128]{3,2,1,0:T(8,128)(2,1)S(1)}, u32[]{:S(2)}, u32[]{:S(2)}) collective-permute-start(bf16[32,4,8,128]{3,2,1,0:T(8,128)(2,1)S(1)} %slice.8.refs_0_), channel_id=1, source_target_pairs={{0,48},{16,32},{32,16},{48,0},{1,49},{17,33},{33,17},{49,1},{2,50}... | collective-permute-start | bytes 786440 | tf_op jit(solution)/shard_map/ppermute | solution.py:324
  68.2 0.3 collective-permute-start.1
  68.5 3.5 %all-to-all-start.2 = ((bf16[8,32,8,128]{3,2,1,0:T(8,128)(2,1)}), bf16[8,32,8,128]{3,2,1,0:T(8,128)(2,1)S(1)}, u32[]{:S(2)}, u32[]{:S(2)}) async-start(bf16[8,32,8,128]{3,2,1,0:T(8,128)(2,1)} %shard_map.66), calls=%async_computation.2 | async-start | bytes 1048576 | tf_op jit(solution)/shard_map/all_to_all | solution.py:327
  72.0 0.5 collective-permute-start.4
  72.5 3.3 %collective-permute-done.2.refs_2_ = bf16[32,4,8,128]{3,2,1,0:T(8,128)(2,1)S(1)} collective-permute-done((bf16[32,4,8,128]{3,2,1,0:T(8,128)(2,1)S(1)}, bf16[32,4,8,128]{3,2,1,0:T(8,128)(2,1)S(1)}, u32[]{:S(2)}, u32[]{:S(2)}) %collective-permute-start.2) | collective-permute-done | bytes 262176 | tf_op jit(solution)/shard_map/ppermute | solution.py:324
  75.8 0.0 collective-permute-start.6
  75.8 4.7 %collective-permute-done.3.refs_3_ = bf16[32,4,8,128]{3,2,1,0:T(8,128)(2,1)S(1)} collective-permute-done((bf16[32,4,8,128]{3,2,1,0:T(8,128)(2,1)S(1)}, bf16[32,4,8,128]{3,2,1,0:T(8,128)(2,1)S(1)}, u32[]{:S(2)}, u32[]{:S(2)}) %collective-permute-start.3) | collective-permute-done | bytes 262176 | tf_op jit(solution)/shard_map/ppermute | solution.py:324
  80.5 0.5 collective-permute-start.5
  81.0 4.3 %all-to-all-done.2.refs_8_ = bf16[8,32,8,128]{3,2,1,0:T(8,128)(2,1)S(1)} async-done(((bf16[8,32,8,128]{3,2,1,0:T(8,128)(2,1)}), bf16[8,32,8,128]{3,2,1,0:T(8,128)(2,1)S(1)}, u32[]{:S(2)}, u32[]{:S(2)}) %all-to-all-start.2) | async-done | bytes 524320 | tf_op jit(solution)/shard_map/all_to_all | solution.py:327
  85.3 7.5 %shard_map.67 = bf16[32,128,1024]{2,1,0:T(8,128)(2,1)} custom-call(bf16[32,4,8,128]{3,2,1,0:T(8,128)(2,1)S(1)} %slice.8.refs_0_, bf16[32,4,8,128]{3,2,1,0:T(8,128)(2,1)S(1)} %collective-permute-done.1.refs_1_, bf16[32,4,8,128]{3,2,1,0:T(8,128)(2,1)S(1)} %collective-permute-done.2.refs_2_, bf16[32,4,8,128]{3,2,1,0:T(8,128)(2,1)S(1)} %collective-permute-done.3.refs_3_, ...), custom_call_target="tpu_custom_call" | custom-call | tf_op jit(solution)/shard_map/pallas_call | solution.py:266
  (9 shorter events, 0.0 us)
Async XLA Ops:
  0.7 11.7 %collective-permute-start = (bf16[32,128]{1,0:T(8,128)(2,1)S(1)}, bf16[32,128]{1,0:T(8,128)(2,1)S(1)}, u32[]{:S(2)}, u32[]{:S(2)}) collective-permute-start(bf16[32,128]{1,0:T(8,128)(2,1)S(1)} %slice.6), channel_id=1, source_target_pairs={{0,1},{1,2},{2,3},{3,4},{4,5},{5,6},{6,7},{8,9},{9,10},{10,11},{11... | collective-permute-start | bytes 24584 | tf_op jit(solution)/shard_map/ppermute | solution.py:288
  12.4 1.0 %copy-start = (f32[512,128]{1,0:T(8,128)S(1)}, f32[512,128]{1,0:T(8,128)}, u32[]{:S(2)}) copy-start(f32[512,128]{1,0:T(8,128)} %constant.4.clone.table) | copy-start | bytes 786436
  29.5 0.7 copy-start.1
  65.0 10.8 %collective-permute-start.2 = (bf16[32,4,8,128]{3,2,1,0:T(8,128)(2,1)S(1)}, bf16[32,4,8,128]{3,2,1,0:T(8,128)(2,1)S(1)}, u32[]{:S(2)}, u32[]{:S(2)}) collective-permute-start(bf16[32,4,8,128]{3,2,1,0:T(8,128)(2,1)S(1)} %slice.8.refs_0_), channel_id=1, source_target_pairs={{0,32},{16,48},{32,0},{48,16},{1,33},{17,49},{33,1},{49,17},{2,34}... | collective-permute-start | bytes 786440 | tf_op jit(solution)/shard_map/ppermute | solution.py:324
  66.0 14.4 %collective-permute-start.3 = (bf16[32,4,8,128]{3,2,1,0:T(8,128)(2,1)S(1)}, bf16[32,4,8,128]{3,2,1,0:T(8,128)(2,1)S(1)}, u32[]{:S(2)}, u32[]{:S(2)}) collective-permute-start(bf16[32,4,8,128]{3,2,1,0:T(8,128)(2,1)S(1)} %slice.8.refs_0_), channel_id=1, source_target_pairs={{0,48},{16,32},{32,16},{48,0},{1,49},{17,33},{33,17},{49,1},{2,50}... | collective-permute-start | bytes 786440 | tf_op jit(solution)/shard_map/ppermute | solution.py:324
  68.2 12.2 %collective-permute-start.1 = (bf16[32,4,8,128]{3,2,1,0:T(8,128)(2,1)S(1)}, bf16[32,4,8,128]{3,2,1,0:T(8,128)(2,1)S(1)}, u32[]{:S(2)}, u32[]{:S(2)}) collective-permute-start(bf16[32,4,8,128]{3,2,1,0:T(8,128)(2,1)S(1)} %slice.8.refs_0_), channel_id=1, source_target_pairs={{0,16},{16,0},{32,48},{48,32},{1,17},{17,1},{33,49},{49,33},{2,18}... | collective-permute-start | bytes 786440 | tf_op jit(solution)/shard_map/ppermute | solution.py:324
  68.5 16.8 %all-to-all-start.2 = ((bf16[8,32,8,128]{3,2,1,0:T(8,128)(2,1)}), bf16[8,32,8,128]{3,2,1,0:T(8,128)(2,1)S(1)}, u32[]{:S(2)}, u32[]{:S(2)}) async-start(bf16[8,32,8,128]{3,2,1,0:T(8,128)(2,1)} %shard_map.66), calls=%async_computation.2 | async-start | bytes 1048576 | tf_op jit(solution)/shard_map/all_to_all | solution.py:327
  72.0 8.9 %collective-permute-start.4 = (bf16[32,4,8,128]{3,2,1,0:T(8,128)(2,1)S(1)}, bf16[32,4,8,128]{3,2,1,0:T(8,128)(2,1)S(1)}, u32[]{:S(2)}, u32[]{:S(2)}) collective-permute-start(bf16[32,4,8,128]{3,2,1,0:T(8,128)(2,1)S(1)} %slice.8.refs_0_), channel_id=1, source_target_pairs={{0,8},{8,0},{1,9},{9,1},{2,10},{10,2},{3,11},{11,3},{4,12},{12,4},... | collective-permute-start | bytes 786440 | tf_op jit(solution)/shard_map/ppermute | solution.py:326
  75.8 9.5 %collective-permute-start.6 = (bf16[32,4,8,128]{3,2,1,0:T(8,128)(2,1)S(1)}, bf16[32,4,8,128]{3,2,1,0:T(8,128)(2,1)S(1)}, u32[]{:S(2)}, u32[]{:S(2)}) collective-permute-start(bf16[32,4,8,128]{3,2,1,0:T(8,128)(2,1)S(1)} %collective-permute-done.2.refs_2_), channel_id=1, source_target_pairs={{0,8},{8,0},{1,9},{9,1},{2,10},{10,2},{3,11},{11,3},{4,12},{12,4},... | collective-permute-start | bytes 786440 | tf_op jit(solution)/shard_map/ppermute | solution.py:326
  80.5 4.9 %collective-permute-start.7 = (bf16[32,4,8,128]{3,2,1,0:T(8,128)(2,1)S(1)}, bf16[32,4,8,128]{3,2,1,0:T(8,128)(2,1)S(1)}, u32[]{:S(2)}, u32[]{:S(2)}) collective-permute-start(bf16[32,4,8,128]{3,2,1,0:T(8,128)(2,1)S(1)} %collective-permute-done.3.refs_3_), channel_id=1, source_target_pairs={{0,8},{8,0},{1,9},{9,1},{2,10},{10,2},{3,11},{11,3},{4,12},{12,4},... | collective-permute-start | bytes 786440 | tf_op jit(solution)/shard_map/ppermute | solution.py:326
  80.5 4.9 %collective-permute-start.5 = (bf16[32,4,8,128]{3,2,1,0:T(8,128)(2,1)S(1)}, bf16[32,4,8,128]{3,2,1,0:T(8,128)(2,1)S(1)}, u32[]{:S(2)}, u32[]{:S(2)}) collective-permute-start(bf16[32,4,8,128]{3,2,1,0:T(8,128)(2,1)S(1)} %collective-permute-done.1.refs_1_), channel_id=1, source_target_pairs={{0,8},{8,0},{1,9},{9,1},{2,10},{10,2},{3,11},{11,3},{4,12},{12,4},... | collective-permute-start | bytes 786440 | tf_op jit(solution)/shard_map/ppermute | solution.py:326
